TPU v7x, 32 devices: a whole 2x2x4 slice. The times are simulated.
32 devices in a mesh: dp: 4 (over x, core), ha: 4 (over z), wa: 2 (over y).
Axes of the slice: x: 2, y: 2, z: 4, core: 2. Of those that a mesh axis runs over, the one named last changes fastest.
Arguments:
- images: bfloat16 [2, 256, 16, 16, 512], P(None, 'dp', 'ha', 'wa'), may hold values from -6 to 6
- labels: int32 [2, 256], P(None, 'dp'), may hold values from 0 to 999
- class_counts: int32 [1000], replicated, may hold values from 1 to 8
- owner_share: int32 [4], replicated, may hold values from 2 to 6, as said below
- w_entry: float32 [3456, 512], P('dp'), may hold values from -0.25 to 0.25
- first_entry: float32 [3456, 512], P('dp'), may hold values from -0.00030517578 to 0.00030517578
- second_entry: float32 [3456, 512], P('dp'), may hold values from 2e-10 to 8e-10
- w_in: float32 [1, 1152, 1536], P(None, 'dp'), may hold values from -0.15625 to 0.15625
- first_in: float32 [1, 1152, 1536], P(None, 'dp'), may hold values from -0.00012207031 to 0.00012207031
- second_in: float32 [1, 1152, 1536], P(None, 'dp'), may hold values from 1.3e-11 to 5.3e-11
- w_mid: float32 [2, 2, 1152, 1152], P(None, None, 'dp'), may hold values from -0.1875 to 0.1875
- first_mid: float32 [2, 2, 1152, 1152], P(None, None, 'dp'), may hold values from -0.00021362305 to 0.00021362305
- second_mid: float32 [2, 2, 1152, 1152], P(None, None, 'dp'), may hold values from 8.7e-11 to 3.5e-10
- w_out: float32 [2, 2304, 768], P(None, 'dp'), may hold values from -0.21875 to 0.21875
- first_out: float32 [2, 2304, 768], P(None, 'dp'), may hold values from -0.00015258789 to 0.00015258789
- second_out: float32 [2, 2304, 768], P(None, 'dp'), may hold values from 2.1e-11 to 8.5e-11
- se_down: float32 [2, 1152, 1536], P(None, 'dp'), may hold values from -0.15625 to 0.15625
- first_down: float32 [2, 1152, 1536], P(None, 'dp'), may hold values from -1.1444092e-05 to 1.1444092e-05
- second_down: float32 [2, 1152, 1536], P(None, 'dp'), may hold values from 1.7e-13 to 6.8e-13
- se_up: float32 [2, 2304, 768], P(None, 'dp'), may hold values from -0.21875 to 0.21875
- first_up: float32 [2, 2304, 768], P(None, 'dp'), may hold values from -4.7683716e-06 to 4.7683716e-06
- second_up: float32 [2, 2304, 768], P(None, 'dp'), may hold values from 3.5e-14 to 1.4e-13
- w_final: float32 [4608, 1536], P('dp'), may hold values from -0.15625 to 0.15625
- first_final: float32 [4608, 1536], P('dp'), may hold values from -0.00015258789 to 0.00015258789
- second_final: float32 [4608, 1536], P('dp'), may hold values from 6.5e-11 to 2.6e-10
- head: float32 [4608, 1000], P('dp'), may hold values from -0.3125 to 0.3125
- first_head: float32 [4608, 1000], P('dp'), may hold values from -6.1035156e-05 to 6.1035156e-05
- second_head: float32 [4608, 1000], P('dp'), may hold values from 1e-11 to 4e-11
- small_params: float32 [1002], replicated, may hold values from -2 to 5
- first_small: float32 [1002], replicated, may hold values from -0.0066 to 0.0066
- second_small: float32 [1002], replicated, may hold values from 4e-11 to 4e-07
Outputs:
- loss_sum: float32 [], replicated
- new_first_entry: float32 [3456, 512], P('dp')
- new_second_entry: float32 [3456, 512], P('dp')
- new_w_entry: float32 [3456, 512], P('dp')
- new_first_in: float32 [1, 1152, 1536], P(None, 'dp')
- new_second_in: float32 [1, 1152, 1536], P(None, 'dp')
- new_w_in: float32 [1, 1152, 1536], P(None, 'dp')
- new_first_mid: float32 [2, 2, 1152, 1152], P(None, None, 'dp')
- new_second_mid: float32 [2, 2, 1152, 1152], P(None, None, 'dp')
- new_w_mid: float32 [2, 2, 1152, 1152], P(None, None, 'dp')
- new_first_out: float32 [2, 2304, 768], P(None, 'dp')
- new_second_out: float32 [2, 2304, 768], P(None, 'dp')
- new_w_out: float32 [2, 2304, 768], P(None, 'dp')
- new_first_down: float32 [2, 1152, 1536], P(None, 'dp')
- new_second_down: float32 [2, 1152, 1536], P(None, 'dp')
- new_se_down: float32 [2, 1152, 1536], P(None, 'dp')
- new_first_up: float32 [2, 2304, 768], P(None, 'dp')
- new_second_up: float32 [2, 2304, 768], P(None, 'dp')
- new_se_up: float32 [2, 2304, 768], P(None, 'dp')
- new_first_final: float32 [4608, 1536], P('dp')
- new_second_final: float32 [4608, 1536], P('dp')
- new_w_final: float32 [4608, 1536], P('dp')
- new_first_head: float32 [4608, 1000], P('dp')
- new_second_head: float32 [4608, 1000], P('dp')
- new_head: float32 [4608, 1000], P('dp')
- new_first_small: float32 [1002], replicated
- new_second_small: float32 [1002], replicated
- new_small_params: float32 [1002], replicated
Inputs may be any that keep to these rules, and one draw needn't show every extreme that they name: `owner_share`: entries sum to 16.
All inputs are finite; a program needn't handle non-finite values.
Results may differ from a plain program's by a relative error of at most 0.04.
Values may be sent and summed in bfloat16 or wider, within the bound.
A program may use at most 640 MiB of HBM per device.

v0:
```python
import jax
import jax.numpy as jnp
from jax import lax
from jax.sharding import PartitionSpec as P

NECK = 768
GROUP = 128
HEIGHT = 8
BREADTH = 8
LAYERS = 2
STEP_COUNT = 5


GAMMA = 1.7015043497085571
ALPHA = 0.2
CLIP = 0.01
RATE = 0.05
SMALL_RATE = 0.5
DECAY_ONE = 0.9
DECAY_TWO = 0.999
ADAM_EPS = 1e-08
WEIGHT_DECAY = 5e-05
STD_EPS = 0.0001
ROW_DIMS = (0, 1, 2, 1, 1, 1, 0, 0)


def padded_2(block, sides, width):
    for axis, dim in sides:
        count = lax.axis_size(axis)
        forward = [(i, i + 1) for i in range(count - 1)]
        backward = [(target, source) for source, target in forward]
        low = lax.ppermute(
            lax.slice_in_dim(block, block.shape[dim] - width, None, axis=dim), axis, forward
        )
        high = lax.ppermute(lax.slice_in_dim(block, 0, width, axis=dim), axis, backward)
        block = jnp.concatenate([low, block, high], axis=dim)
    return block


def shifted(block, axis, distance):
    devices = range(lax.axis_size(axis))
    route = [(i - distance, i) for i in devices if i - distance in devices]
    return lax.ppermute(block, axis, route)


def shortened(value):
    return jax.tree.map(lambda a: a.astype(jnp.bfloat16) if a.dtype == jnp.float32 else a, value)


def gelu_act(values):
    return jax.nn.gelu(values, approximate=True)


def gelu_slope(values, upstream):
    return jax.vjp(gelu_act, values)[1](upstream)[0]


def standardize(weight):
    fan_in = weight.shape[-1]
    centre = weight - jnp.mean(weight, axis=-1, keepdims=True)
    spread = jnp.mean(centre * centre, axis=-1, keepdims=True)
    return centre * lax.rsqrt(spread * fan_in + STD_EPS)


def through_standard(weight, gradient):
    return jax.vjp(standardize, weight)[1](gradient)[0]


def owner_tables(shares, local_rows):
    devices = lax.axis_size("dp")
    part = local_rows // 6
    rows = 4 * devices * part
    ends = jnp.cumsum(shares)
    starts = ends - shares
    device_ids = jnp.arange(devices, dtype=jnp.int32)
    part_ids = jnp.arange(4 * devices, dtype=jnp.int32)
    owner = jnp.sum((part_ids[:, None] >= ends[None, :]).astype(jnp.int32), axis=1)
    first_part = jnp.sum(
        jnp.where(owner[:, None] == device_ids[None, :], starts[None, :], 0), axis=1
    )
    slot = owner * 6 + part_ids - first_part
    row_ids = jnp.arange(rows, dtype=jnp.int32)
    row_map = jnp.take(slot, row_ids // part) * part + row_ids % part
    padded_ids = jnp.arange(6 * devices * part, dtype=jnp.int32)
    holder = padded_ids // (6 * part)
    local_part = padded_ids % (6 * part) // part
    holder_hit = holder[:, None] == device_ids[None, :]
    holder_share = jnp.sum(jnp.where(holder_hit, shares[None, :], 0), axis=1)
    holder_start = jnp.sum(jnp.where(holder_hit, starts[None, :], 0), axis=1)
    valid = local_part < holder_share
    source = jnp.minimum((holder_start + local_part) * part + padded_ids % part, rows - 1)
    return (row_map, source, valid)


def place_mask(valid, dim, rank):
    shape = [1] * rank
    shape[dim] = valid.shape[0]
    return valid.astype(jnp.float32).reshape(shape)


def to_slots(gradients, tables):
    return tuple(
        (
            jnp.take(gradients[k], tables[k][1], axis=ROW_DIMS[k])
            * place_mask(tables[k][2], ROW_DIMS[k], gradients[k].ndim)
            for k in range(8)
        )
    )


def project(inputs, weight):
    flat_in = inputs.reshape(-1, inputs.shape[-1])
    result = lax.dot_general(
        flat_in, weight, (((1,), (1,)), ((), ())), preferred_element_type=jnp.float32
    )
    return result.reshape(inputs.shape[:-1] + (weight.shape[0],))


def back_project(upstream, weight):
    return lax.dot_general(
        upstream,
        weight,
        (((upstream.ndim - 1,), (0,)), ((), ())),
        preferred_element_type=jnp.float32,
    )


def outer_sum(inputs, upstream):
    flat_in = inputs.reshape(-1, inputs.shape[-1])
    flat_up = upstream.reshape(-1, upstream.shape[-1])
    return lax.dot_general(
        flat_up, flat_in, (((0,), (0,)), ((), ())), preferred_element_type=jnp.float32
    )


def pad_edges(values):
    padded = padded_2(values, (("ha", 1), ("wa", 2)), 1)
    return padded


def stride_extend(values):
    next_cols = shifted(values[:, :, 0:1], "wa", -1)
    wider = jnp.concatenate([values, next_cols], axis=2)
    next_rows = shifted(wider[:, 0:1], "ha", -1)
    extended = jnp.concatenate([wider, next_rows], axis=1)
    return extended


def stride_fold(grad_ext):
    back_rows = shifted(grad_ext[:, -1:].astype(jnp.bfloat16), "ha", 1).astype(jnp.float32)
    upper = jnp.concatenate([grad_ext[:, 0:1] + back_rows, grad_ext[:, 1:-1]], axis=1)
    back_cols = shifted(shortened(upper[:, :, -1:]), "wa", 1)
    folded = jnp.concatenate([upper[:, :, 0:1] + back_cols, upper[:, :, 1:-1]], axis=2)
    return folded


def spatial_sum(values):
    summed = jnp.sum(values, axis=(1, 2))
    summed = lax.psum(summed.astype(jnp.bfloat16), ("ha", "wa")).astype(jnp.float32)
    return summed


def tap_window(padded, shift_y, shift_x, out_h, out_w, stride):
    window = padded[
        :,
        shift_y : shift_y + stride * (out_h - 1) + 1 : stride,
        shift_x : shift_x + stride * (out_w - 1) + 1 : stride,
    ]
    return window.reshape(padded.shape[0], out_h, out_w, padded.shape[-1] // GROUP, GROUP)


def conv_forward(padded, weight, out_h, out_w, stride):
    groups = padded.shape[-1] // GROUP
    kernel = weight.reshape(groups, GROUP, 9, GROUP)
    total = jnp.zeros((padded.shape[0], out_h, out_w, groups, GROUP), jnp.float32)
    for offset in range(9):
        window = tap_window(padded, offset // 3, offset % 3, out_h, out_w, stride)
        total = total + jnp.einsum(
            "nhwgc,goc->nhwgo", window, kernel[:, :, offset, :], preferred_element_type=jnp.float32
        )
    return total.reshape(padded.shape[0], out_h, out_w, padded.shape[-1])


def conv_backward(upstream, padded, weight):
    amount, tile_h, tile_w, channels = upstream.shape
    groups = channels // GROUP
    kernel = weight.reshape(groups, GROUP, 9, GROUP)
    grouped = upstream.reshape(amount, tile_h, tile_w, groups, GROUP)
    padded_up = pad_edges(upstream)
    grad_in = jnp.zeros((amount, tile_h, tile_w, groups, GROUP), jnp.float32)
    tap_grads = []
    for offset in range(9):
        shift_y = offset // 3
        shift_x = offset % 3
        window_up = tap_window(padded_up, 2 - shift_y, 2 - shift_x, tile_h, tile_w, 1)
        grad_in = grad_in + jnp.einsum(
            "nhwgo,goc->nhwgc",
            window_up,
            kernel[:, :, offset, :],
            preferred_element_type=jnp.float32,
        )
        window_in = tap_window(padded, shift_y, shift_x, tile_h, tile_w, 1)
        tap_grads.append(
            jnp.einsum("nhwgc,nhwgo->goc", window_in, grouped, preferred_element_type=jnp.float32)
        )
    grad_w = jnp.stack(tap_grads, axis=2)
    return (grad_in.reshape(amount, tile_h, tile_w, channels), grad_w.reshape(channels, 9 * GROUP))


def conv_backward_stride(upstream, extended, weight):
    amount, out_h, out_w, channels = upstream.shape
    groups = channels // GROUP
    kernel = weight.reshape(groups, GROUP, 9, GROUP)
    grouped = upstream.reshape(amount, out_h, out_w, groups, GROUP)
    phases = [
        [jnp.zeros((amount, out_h + 1, out_w + 1, channels), jnp.float32) for parity_x in range(2)]
        for parity_y in range(2)
    ]
    tap_grads = []
    for offset in range(9):
        shift_y = offset // 3
        shift_x = offset % 3
        term = jnp.einsum(
            "nhwgo,goc->nhwgc", grouped, kernel[:, :, offset, :], preferred_element_type=jnp.float32
        ).reshape(amount, out_h, out_w, channels)
        placed = jnp.pad(
            term,
            ((0, 0), (shift_y // 2, 1 - shift_y // 2), (shift_x // 2, 1 - shift_x // 2), (0, 0)),
        )
        phases[shift_y % 2][shift_x % 2] = phases[shift_y % 2][shift_x % 2] + placed
        window_in = tap_window(extended, shift_y, shift_x, out_h, out_w, 2)
        tap_grads.append(
            jnp.einsum("nhwgc,nhwgo->goc", window_in, grouped, preferred_element_type=jnp.float32)
        )
    even_rows = jnp.stack([phases[0][0], phases[0][1]], axis=3)
    odd_rows = jnp.stack([phases[1][0], phases[1][1]], axis=3)
    woven = jnp.stack([even_rows, odd_rows], axis=2).reshape(
        amount, 2 * out_h + 2, 2 * out_w + 2, channels
    )
    grad_ext = woven[:, : extended.shape[1], : extended.shape[2]]
    grad_w = jnp.stack(tap_grads, axis=2)
    return (stride_fold(grad_ext), grad_w.reshape(channels, 9 * GROUP))


def pool_pairs(values):
    amount, size_h, size_w, channels = values.shape
    summed = jnp.sum(
        values.reshape(amount, size_h // 2, 2, size_w // 2, 2, channels),
        axis=(2, 4),
        dtype=jnp.float32,
    )
    return (summed * 0.25).astype(jnp.bfloat16)


def layer_forward(hidden, layer_i, in_w, skip_w, mid_w, out_w, down_w, up_w, skip_value):
    pre_scale = (1.0 + layer_i * ALPHA * ALPHA) ** (-0.5)
    act_zero = (gelu_act(hidden) * (GAMMA * pre_scale)).astype(jnp.bfloat16)
    pre_one = project(act_zero, in_w)
    act_one = (gelu_act(pre_one) * GAMMA).astype(jnp.bfloat16)
    if layer_i == 0:
        pad_one = stride_extend(act_one)
        pre_two = conv_forward(pad_one, mid_w[0], hidden.shape[1] // 2, hidden.shape[2] // 2, 2)
    else:
        pad_one = pad_edges(act_one)
        pre_two = conv_forward(pad_one, mid_w[0], hidden.shape[1], hidden.shape[2], 1)
    tile_h = pre_two.shape[1]
    tile_w = pre_two.shape[2]
    pad_two = pad_edges((gelu_act(pre_two) * GAMMA).astype(jnp.bfloat16))
    pre_three = conv_forward(pad_two, mid_w[1], tile_h, tile_w, 1)
    act_three = (gelu_act(pre_three) * GAMMA).astype(jnp.bfloat16)
    pre_four = project(act_three, out_w)
    squeezed = (spatial_sum(pre_four) / (HEIGHT * BREADTH)).astype(jnp.bfloat16)
    pre_down = project(squeezed, down_w)
    act_down = gelu_act(pre_down).astype(jnp.bfloat16)
    pre_up = project(act_down, up_w)
    gate_value = 2.0 * jax.nn.sigmoid(pre_up)
    branch = ALPHA * skip_value * pre_four * gate_value[:, None, None, :]
    if layer_i == 0:
        pooled = pool_pairs(act_zero)
        updated = project(pooled, skip_w) + branch
    else:
        pooled = act_zero
        updated = hidden + branch
    stored = (
        hidden,
        act_zero,
        pre_one,
        pad_one,
        pre_two,
        pad_two,
        pre_three,
        act_three,
        pre_four,
        squeezed,
        pre_down,
        act_down,
        pre_up,
        pooled,
    )
    return (updated, stored)


def layer_backward(grad_hidden, stored, layer_i, in_w, mid_w, out_w, down_w, up_w, skip_value):
    (
        hidden,
        act_zero,
        pre_one,
        pad_one,
        pre_two,
        pad_two,
        pre_three,
        act_three,
        pre_four,
        squeezed,
        pre_down,
        act_down,
        pre_up,
        pooled,
    ) = stored
    pre_scale = (1.0 + layer_i * ALPHA * ALPHA) ** (-0.5)
    gate_sig = jax.nn.sigmoid(pre_up)
    gate_value = 2.0 * gate_sig
    gain_part = ALPHA * jnp.sum(grad_hidden * pre_four * gate_value[:, None, None, :])
    grad_branch = grad_hidden * (ALPHA * skip_value)
    grad_gate = spatial_sum(grad_branch * pre_four)
    grad_up = (grad_gate * 2.0 * gate_sig * (1.0 - gate_sig)).astype(jnp.bfloat16)
    up_grad = outer_sum(act_down, grad_up)
    grad_down = gelu_slope(pre_down, back_project(grad_up, up_w)).astype(jnp.bfloat16)
    down_grad = outer_sum(squeezed, grad_down)
    grad_squeezed = back_project(grad_down, down_w)
    grad_four = (
        grad_branch * gate_value[:, None, None, :]
        + grad_squeezed[:, None, None, :] / (HEIGHT * BREADTH)
    ).astype(jnp.bfloat16)
    out_grad = outer_sum(act_three, grad_four)
    grad_three = (gelu_slope(pre_three, back_project(grad_four, out_w)) * GAMMA).astype(
        jnp.bfloat16
    )
    grad_act_two, mid_grad_b = conv_backward(grad_three, pad_two, mid_w[1])
    grad_two = (gelu_slope(pre_two, grad_act_two) * GAMMA).astype(jnp.bfloat16)
    if layer_i == 0:
        grad_act_one, mid_grad_a = conv_backward_stride(grad_two, pad_one, mid_w[0])
    else:
        grad_act_one, mid_grad_a = conv_backward(grad_two, pad_one, mid_w[0])
    grad_one = (gelu_slope(pre_one, grad_act_one) * GAMMA).astype(jnp.bfloat16)
    in_grad = outer_sum(act_zero, grad_one)
    mids = jnp.stack([mid_grad_a, mid_grad_b])
    if layer_i == 0:
        skip_grad = outer_sum(pooled, grad_hidden.astype(jnp.bfloat16))
        entry_grad = jnp.concatenate([in_grad, skip_grad], axis=0)
        return (None, (entry_grad, mids, out_grad, down_grad, up_grad), gain_part)
    grad_zero = back_project(grad_one, in_w)
    grad_prev = grad_hidden + gelu_slope(hidden, grad_zero) * (GAMMA * pre_scale)
    return (grad_prev, (in_grad, mids, out_grad, down_grad, up_grad), gain_part)


def head_pass(hidden, labels_mb, class_weight, final_w, head_w, head_bias, images_all):
    cell_count = HEIGHT * BREADTH
    hidden_low = hidden.astype(jnp.bfloat16)
    pre_final = project(hidden_low, final_w)
    pooled = (spatial_sum(gelu_act(pre_final) * GAMMA) / cell_count).astype(jnp.bfloat16)
    logits = jnp.dot(pooled, head_w, preferred_element_type=jnp.float32) + head_bias
    largest = jnp.max(logits, axis=1, keepdims=True)
    log_total = largest[:, 0] + jnp.log(jnp.sum(jnp.exp(logits - largest), axis=1))
    one_hot = (labels_mb[:, None] == jnp.arange(logits.shape[1])[None, :]).astype(jnp.float32)
    picked = jnp.sum(one_hot * logits, axis=1)
    image_weight = jnp.sum(one_hot * class_weight[None, :], axis=1)
    micro_loss = jnp.sum(image_weight * (log_total - picked))
    softmax_p = jnp.exp(logits - log_total[:, None])
    grad_logits = image_weight[:, None] * (softmax_p - one_hot) / images_all
    grad_low = grad_logits.astype(jnp.bfloat16)
    head_grad = lax.dot_general(
        pooled, grad_low, (((0,), (0,)), ((), ())), preferred_element_type=jnp.float32
    )
    grad_pooled = (
        lax.dot_general(
            grad_low, head_w, (((1,), (1,)), ((), ())), preferred_element_type=jnp.float32
        )
        / cell_count
    )
    grad_final = (
        gelu_slope(pre_final, jnp.broadcast_to(grad_pooled[:, None, None, :], pre_final.shape))
        * GAMMA
    ).astype(jnp.bfloat16)
    final_grad = outer_sum(hidden_low, grad_final)
    grad_hidden = back_project(grad_final, final_w)
    return (grad_hidden, (final_grad, head_grad, jnp.sum(grad_logits, axis=0)), micro_loss)


def tree_add(previous, current):
    return tuple((older_part + newer_part for older_part, newer_part in zip(previous, current)))


def reduce_end(gradients, tables):
    slots = to_slots(gradients, tables)
    shards = (
        lax.psum_scatter(
            slots[0].astype(jnp.bfloat16), "dp", scatter_dimension=0, tiled=True
        ).astype(jnp.float32),
        lax.psum_scatter(
            slots[1].astype(jnp.bfloat16), "dp", scatter_dimension=1, tiled=True
        ).astype(jnp.float32),
        lax.psum_scatter(
            slots[2].astype(jnp.bfloat16), "dp", scatter_dimension=2, tiled=True
        ).astype(jnp.float32),
        lax.psum_scatter(
            slots[3].astype(jnp.bfloat16), "dp", scatter_dimension=1, tiled=True
        ).astype(jnp.float32),
        lax.psum_scatter(
            slots[4].astype(jnp.bfloat16), "dp", scatter_dimension=1, tiled=True
        ).astype(jnp.float32),
        lax.psum_scatter(
            slots[5].astype(jnp.bfloat16), "dp", scatter_dimension=1, tiled=True
        ).astype(jnp.float32),
        lax.psum_scatter(
            slots[6].astype(jnp.bfloat16), "dp", scatter_dimension=0, tiled=True
        ).astype(jnp.float32),
        lax.psum_scatter(
            slots[7].astype(jnp.bfloat16), "dp", scatter_dimension=0, tiled=True
        ).astype(jnp.float32),
    )
    return (
        lax.psum(shards[0].astype(jnp.bfloat16), ("ha", "wa")).astype(jnp.float32),
        lax.psum(shards[1].astype(jnp.bfloat16), ("ha", "wa")).astype(jnp.float32),
        lax.psum(shards[2].astype(jnp.bfloat16), ("ha", "wa")).astype(jnp.float32),
        lax.psum(shards[3].astype(jnp.bfloat16), ("ha", "wa")).astype(jnp.float32),
        lax.psum(shards[4].astype(jnp.bfloat16), ("ha", "wa")).astype(jnp.float32),
        lax.psum(shards[5].astype(jnp.bfloat16), ("ha", "wa")).astype(jnp.float32),
        lax.psum(shards[6].astype(jnp.bfloat16), ("ha", "wa")).astype(jnp.float32),
        lax.psum(shards[7].astype(jnp.bfloat16), ("ha", "wa")).astype(jnp.float32),
    )


def clip_unit(gradient, weight):
    weight_norm = jnp.sqrt(jnp.sum(weight * weight, axis=-1, keepdims=True))
    grad_norm = jnp.sqrt(jnp.sum(gradient * gradient, axis=-1, keepdims=True))
    ceiling = CLIP * weight_norm
    return gradient * (ceiling / jnp.maximum(grad_norm, ceiling))


def adam_step(weight, gradient, moment_one, moment_two, rate):
    first_new = DECAY_ONE * moment_one + (1.0 - DECAY_ONE) * gradient
    second_new = DECAY_TWO * moment_two + (1.0 - DECAY_TWO) * gradient * gradient
    first_hat = first_new / (1.0 - DECAY_ONE**STEP_COUNT)
    second_hat = second_new / (1.0 - DECAY_TWO**STEP_COUNT)
    weight_new = weight - rate * (
        first_hat / (jnp.sqrt(second_hat) + ADAM_EPS) + WEIGHT_DECAY * weight
    )
    return (first_new, second_new, weight_new)


def body(
    images,
    labels,
    class_counts,
    owner_share,
    w_entry,
    first_entry,
    second_entry,
    w_in,
    first_in,
    second_in,
    w_mid,
    first_mid,
    second_mid,
    w_out,
    first_out,
    second_out,
    se_down,
    first_down,
    second_down,
    se_up,
    first_up,
    second_up,
    w_final,
    first_final,
    second_final,
    head,
    first_head,
    second_head,
    small_params,
    first_small,
    second_small,
):
    masters = (w_entry, w_in, w_mid, w_out, se_down, se_up, w_final, head)
    gathered = (
        lax.all_gather(standardize(w_entry).astype(jnp.bfloat16), "dp", axis=0, tiled=True),
        lax.all_gather(standardize(w_in).astype(jnp.bfloat16), "dp", axis=1, tiled=True),
        lax.all_gather(standardize(w_mid).astype(jnp.bfloat16), "dp", axis=2, tiled=True),
        lax.all_gather(standardize(w_out).astype(jnp.bfloat16), "dp", axis=1, tiled=True),
        lax.all_gather(se_down.astype(jnp.bfloat16), "dp", axis=1, tiled=True),
        lax.all_gather(se_up.astype(jnp.bfloat16), "dp", axis=1, tiled=True),
        lax.all_gather(standardize(w_final).astype(jnp.bfloat16), "dp", axis=0, tiled=True),
        lax.all_gather(head.astype(jnp.bfloat16), "dp", axis=0, tiled=True),
    )
    tables = [owner_tables(owner_share, masters[k].shape[ROW_DIMS[k]]) for k in range(8)]
    full = tuple((jnp.take(gathered[k], tables[k][0], axis=ROW_DIMS[k]) for k in range(8)))
    skip_gain = small_params[:LAYERS]
    head_bias = small_params[LAYERS:]
    images_all = images.shape[0] * labels.shape[1] * lax.axis_size("dp")
    replica_scale = 1.0 / (lax.axis_size("ha") * lax.axis_size("wa"))
    class_weight = 1.0 / class_counts.astype(jnp.float32)
    grads_sum = tuple((jnp.zeros(weight.shape, jnp.float32) for weight in full))
    owned_sum = tuple((jnp.zeros(weight.shape, jnp.float32) for weight in masters))
    loss_acc = jnp.zeros((), jnp.float32)
    gain_acc = jnp.zeros(skip_gain.shape, jnp.float32)
    bias_acc = jnp.zeros(head_bias.shape, jnp.float32)
    for micro_i in range(images.shape[0]):
        hidden = images[micro_i].astype(jnp.float32)
        stored_all = []
        for layer_i in range(LAYERS):
            if layer_i == 0:
                in_now = full[0][:NECK]
                skip_now = full[0][NECK:]
            else:
                in_now = full[1][layer_i - 1]
                skip_now = None
            hidden, stored = layer_forward(
                hidden,
                layer_i,
                in_now,
                skip_now,
                full[2][layer_i],
                full[3][layer_i],
                full[4][layer_i],
                full[5][layer_i],
                skip_gain[layer_i],
            )
            stored_all.append(stored)
        grad_hidden, head_grads, micro_loss = head_pass(
            hidden, labels[micro_i], class_weight, full[6], full[7], head_bias, images_all
        )
        grads_by_layer = [None] * LAYERS
        gain_parts = [None] * LAYERS
        for layer_i in reversed(range(LAYERS)):
            in_now = full[0][:NECK] if layer_i == 0 else full[1][layer_i - 1]
            grad_hidden, layer_grads, gain_part = layer_backward(
                grad_hidden,
                stored_all[layer_i],
                layer_i,
                in_now,
                full[2][layer_i],
                full[3][layer_i],
                full[4][layer_i],
                full[5][layer_i],
                skip_gain[layer_i],
            )
            grads_by_layer[layer_i] = layer_grads
            gain_parts[layer_i] = gain_part
        micro_grads = (
            grads_by_layer[0][0],
            jnp.stack([grads_by_layer[1][0]]),
            jnp.stack([layer_grads[1] for layer_grads in grads_by_layer]),
            jnp.stack([layer_grads[2] for layer_grads in grads_by_layer]),
            jnp.stack([layer_grads[3] for layer_grads in grads_by_layer]) * replica_scale,
            jnp.stack([layer_grads[4] for layer_grads in grads_by_layer]) * replica_scale,
            head_grads[0],
            head_grads[1] * replica_scale,
        )
        loss_acc = loss_acc + micro_loss * replica_scale
        gain_acc = gain_acc + jnp.stack(gain_parts)
        bias_acc = bias_acc + head_grads[2] * replica_scale
        grads_sum = tree_add(grads_sum, micro_grads)
    owned_sum = reduce_end(grads_sum, tables)
    loss_sum, small_grad = lax.psum(
        (loss_acc, jnp.concatenate([gain_acc, bias_acc])), ("dp", "ha", "wa")
    )
    grad_entry = clip_unit(through_standard(w_entry, owned_sum[0]), w_entry)
    grad_in = clip_unit(through_standard(w_in, owned_sum[1]), w_in)
    grad_mid = clip_unit(through_standard(w_mid, owned_sum[2]), w_mid)
    grad_out = clip_unit(through_standard(w_out, owned_sum[3]), w_out)
    grad_down = clip_unit(owned_sum[4], se_down)
    grad_up = clip_unit(owned_sum[5], se_up)
    grad_final = clip_unit(through_standard(w_final, owned_sum[6]), w_final)
    entry_one, entry_two, entry_new = adam_step(
        w_entry, grad_entry, first_entry, second_entry, RATE
    )
    in_one, in_two, in_new = adam_step(w_in, grad_in, first_in, second_in, RATE)
    mid_one, mid_two, mid_new = adam_step(w_mid, grad_mid, first_mid, second_mid, RATE)
    out_one, out_two, out_new = adam_step(w_out, grad_out, first_out, second_out, RATE)
    down_one, down_two, down_new = adam_step(se_down, grad_down, first_down, second_down, RATE)
    up_one, up_two, up_new = adam_step(se_up, grad_up, first_up, second_up, RATE)
    final_one, final_two, final_new = adam_step(
        w_final, grad_final, first_final, second_final, RATE
    )
    head_one, head_two, head_new = adam_step(head, owned_sum[7], first_head, second_head, RATE)
    small_one, small_two, small_new = adam_step(
        small_params, small_grad, first_small, second_small, SMALL_RATE
    )
    return (
        loss_sum,
        entry_one,
        entry_two,
        entry_new,
        in_one,
        in_two,
        in_new,
        mid_one,
        mid_two,
        mid_new,
        out_one,
        out_two,
        out_new,
        down_one,
        down_two,
        down_new,
        up_one,
        up_two,
        up_new,
        final_one,
        final_two,
        final_new,
        head_one,
        head_two,
        head_new,
        small_one,
        small_two,
        small_new,
    )


def solution(mesh):
    return jax.shard_map(
        body,
        mesh=mesh,
        in_specs=(
            P(None, "dp", "ha", "wa", None),
            P(None, "dp"),
            P(),
            P(),
            P("dp", None),
            P("dp", None),
            P("dp", None),
            P(None, "dp", None),
            P(None, "dp", None),
            P(None, "dp", None),
            P(None, None, "dp", None),
            P(None, None, "dp", None),
            P(None, None, "dp", None),
            P(None, "dp", None),
            P(None, "dp", None),
            P(None, "dp", None),
            P(None, "dp", None),
            P(None, "dp", None),
            P(None, "dp", None),
            P(None, "dp", None),
            P(None, "dp", None),
            P(None, "dp", None),
            P("dp", None),
            P("dp", None),
            P("dp", None),
            P("dp", None),
            P("dp", None),
            P("dp", None),
            P(),
            P(),
            P(),
        ),
        out_specs=(
            P(),
            P("dp", None),
            P("dp", None),
            P("dp", None),
            P(None, "dp", None),
            P(None, "dp", None),
            P(None, "dp", None),
            P(None, None, "dp", None),
            P(None, None, "dp", None),
            P(None, None, "dp", None),
            P(None, "dp", None),
            P(None, "dp", None),
            P(None, "dp", None),
            P(None, "dp", None),
            P(None, "dp", None),
            P(None, "dp", None),
            P(None, "dp", None),
            P(None, "dp", None),
            P(None, "dp", None),
            P("dp", None),
            P("dp", None),
            P("dp", None),
            P("dp", None),
            P("dp", None),
            P("dp", None),
            P(),
            P(),
            P(),
        ),
        check_vma=False,
    )
```

profile of v0, /device:TPU:0, one launch (start us, length us, event | category | flops | bytes accessed | tf_op | source)
XLA Modules:
  0.0 3175.0 jit_solution(12179168676451805728)
XLA Ops:
  169.8 17.5 collective-permute-done.1
  187.9 17.5 collective-permute-done.15
  244.0 30.7 gather_fusion.2
  290.4 17.1 gather_fusion.12
  312.7 43.4 %copy.2447 = bf16[2,2,1152,1152]{3,1,2,0:T(2,128)(2,1)} copy(bf16[2,2,1152,1152]{3,2,1,0:T(8,128)(2,1)} %all-gather.11.cloned.1.call-done) | data formatting | bytes 21233664 | tf_op jit(solution)/shard_map/all_gather | solution.py:489
  356.1 33.6 %gather_fusion.1 = bf16[768,2,2,1152]{3,2,1,0:T(2,128)(2,1)} fusion(bf16[2,2,1152,1152]{3,1,2,0:T(2,128)(2,1)} %copy.2447, s32[1024]{0:T(1024)S(1)} %pad_clamp_fusion.6), kind=kCustom, calls=%fused_computation.5 | custom fusion | bytes 14158848 | tf_op jit(solution)/shard_map/jit(_take)/gather | solution.py:497
  399.9 42.0 %slice_reduce_fusion = (bf16[768,1152]{1,0:T(8,128)(2,1)}, bf16[768,1152]{1,0:T(8,128)(2,1)}, bf16[768,1152]{1,0:T(8,128)(2,1)}, bf16[768,1152]{1,0:T(8,128)(2,1)}) fusion(bf16[2,2,768,1152]{3,1,0,2:T(2,128)(2,1)S(1)} %fusion.16), kind=kLoop, calls=%fused_computation.243 | loop fusion | bytes 14155776 | tf_op jit(solution)/shard_map/slice | solution.py:265
  589.0 54.7 %all-reduce.47.cloned.1.call-done = (bf16[64,1536]{1,0:T(8,128)(2,1)}, bf16[64,1536]{1,0:T(8,128)(2,1)}) async-done(((bf16[64,1536]{1,0:T(8,128)(2,1)}, bf16[64,1536]{1,0:T(8,128)(2,1)}), (bf16[64,1536]{1,0:T(8,128)(2,1)}, bf16[64,1536]{1,0:T(8,128)(2,1)})) %all-reduce.47.cloned.1.call-update) | async-done | bytes 393232 | tf_op jit(solution)/shard_map/psum | solution.py:159
  786.3 33.1 %all-reduce.45.cloned.1.call-done = (bf16[64,1536]{1,0:T(8,128)(2,1)}, bf16[64,1536]{1,0:T(8,128)(2,1)}) async-done(((bf16[64,1536]{1,0:T(8,128)(2,1)}, bf16[64,1536]{1,0:T(8,128)(2,1)}), (bf16[64,1536]{1,0:T(8,128)(2,1)}, bf16[64,1536]{1,0:T(8,128)(2,1)})) %all-reduce.45.cloned.1.call-update) | async-done | bytes 393232 | tf_op jit(solution)/shard_map/psum | solution.py:159
  831.7 79.9 %all-gather.21.cloned.1.call-done = bf16[4608,1536]{1,0:T(8,128)(2,1)} async-done(((bf16[1152,1536]{1,0:T(8,128)(2,1)}), bf16[4608,1536]{1,0:T(8,128)(2,1)}) %all-gather.21.cloned.1.call-update) | async-done | bytes 14155792 | tf_op jit(solution)/shard_map/all_gather | solution.py:493
  911.6 26.4 gather_fusion.4
  989.4 20.8 gather_fusion.5
  1010.2 45.9 %all-reduce.43.cloned.1.call-done = (bf16[64,3072]{1,0:T(8,128)(2,1)}, bf16[64,3072]{1,0:T(8,128)(2,1)}) async-done(((bf16[64,3072]{1,0:T(8,128)(2,1)}, bf16[64,3072]{1,0:T(8,128)(2,1)}), (bf16[64,3072]{1,0:T(8,128)(2,1)}, bf16[64,3072]{1,0:T(8,128)(2,1)})) %all-reduce.43.cloned.1.call-update) | async-done | bytes 786448 | tf_op jit(solution)/shard_map/psum | solution.py:159
  1104.3 67.3 %all-reduce.41.cloned.1.call-done = (bf16[64,1536]{1,0:T(8,128)(2,1)}, bf16[64,1536]{1,0:T(8,128)(2,1)}) async-done(((bf16[64,1536]{1,0:T(8,128)(2,1)}, bf16[64,1536]{1,0:T(8,128)(2,1)}), (bf16[64,1536]{1,0:T(8,128)(2,1)}, bf16[64,1536]{1,0:T(8,128)(2,1)})) %all-reduce.41.cloned.1.call-update) | async-done | bytes 393232 | tf_op jit(solution)/shard_map/psum | solution.py:159
  1443.7 58.0 %all-reduce.39.cloned.1.call-done = (bf16[64,1536]{1,0:T(8,128)(2,1)}, bf16[64,1536]{1,0:T(8,128)(2,1)}) async-done(((bf16[64,1536]{1,0:T(8,128)(2,1)}, bf16[64,1536]{1,0:T(8,128)(2,1)}), (bf16[64,1536]{1,0:T(8,128)(2,1)}, bf16[64,1536]{1,0:T(8,128)(2,1)})) %all-reduce.39.cloned.1.call-update) | async-done | bytes 393232 | tf_op jit(solution)/shard_map/psum | solution.py:159
  1568.3 29.2 copy.2838
  1603.2 29.1 copy.2828
  1632.3 29.8 gather_fusion.15
  1662.1 30.3 gather_fusion.14
  1699.8 22.1 copy.2834
  1721.9 42.4 %gather_fusion.9 = f32[1152,2,1536]{2,1,0:T(2,128)} fusion(f32[2,768,1536]{2,0,1:T(2,128)} %copy.2834, s32[2048]{0:T(1024)S(1)} %copy-done.390), kind=kCustom, calls=%fused_computation.13 | custom fusion | bytes 28316160 | tf_op jit(solution)/shard_map/jit(_take)/gather | solution.py:104
  1776.6 21.1 fusion
  1945.8 49.9 %gather_fusion.8 = f32[1152,2,2,1152]{3,2,1,0:T(2,128)} fusion(f32[2,2,768,1152]{3,1,2,0:T(2,128)} %maximum_add_fusion, s32[2048]{0:T(1024)S(1)} %copy-done.390), kind=kCustom, calls=%fused_computation.12 | custom fusion | bytes 42471936 | tf_op jit(solution)/shard_map/jit(_take)/gather | solution.py:104
  1995.7 16.9 multiply_convert_fusion.1
  2237.2 25.4 gather_fusion.11
  2290.7 17.4 bitcast_add_fusion
  2308.2 34.1 %gather_fusion.10 = f32[4608,1536]{1,0:T(8,128)} fusion(f32[3072,1536]{1,0:T(8,128)} %bitcast_add_fusion, s32[5120]{0:T(1024)S(1)} %pad_clamp_fusion), kind=kCustom, calls=%fused_computation.14 | custom fusion | bytes 56641536 | tf_op jit(solution)/shard_map/jit(_take)/gather | solution.py:104
  2342.3 17.0 multiply_convert_fusion
  2381.9 59.9 %reduce-scatter.15.cloned.1.call-done = bf16[1152,1000]{1,0:T(8,128)(2,1)} async-done(((bf16[4608,1000]{1,0:T(8,128)(2,1)}), bf16[1152,1000]{1,0:T(8,128)(2,1)}) %reduce-scatter.15.cloned.1.call-update) | async-done | bytes 2304016 | tf_op jit(solution)/shard_map/reduce_scatter | solution.py:418
  2441.8 112.0 %reduce-scatter.13.cloned.1.call-done = bf16[1152,1536]{1,0:T(8,128)(2,1)} async-done(((bf16[4608,1536]{1,0:T(8,128)(2,1)}), bf16[1152,1536]{1,0:T(8,128)(2,1)}) %reduce-scatter.13.cloned.1.call-update) | async-done | bytes 3538960 | tf_op jit(solution)/shard_map/reduce_scatter | solution.py:415
  2581.0 43.8 %all-reduce.21 = (f32[]{:T(128)}, f32[1002]{0:T(1024)S(1)}) all-reduce(f32[]{:T(128)S(6)} %add.1936, f32[1002]{0:T(1024)S(1)} %pad_maximum_fusion.78), channel_id=1, replica_groups=mesh['dp'=4,'ha'=4,'wa'=2] {'dp','ha','wa'}, use_global_device_ids=true, to_apply=%region_37.42 | all-reduce | flops 1003 | bytes 8024 | tf_op jit(solution)/shard_map/psum | solution.py:565
  2625.4 421.2 %all-reduce.37.cloned.1.call-done = (bf16[864,512]{1,0:T(8,128)(2,1)}, bf16[1,288,1536]{2,1,0:T(8,128)(2,1)}, bf16[2,2,288,1152]{3,2,1,0:T(8,128)(2,1)}, bf16[2,...) async-done(((bf16[864,512]{1,0:T(8,128)(2,1)}, ...) | async-done | bytes 15575056 | tf_op jit(solution)/shard_map/psum | solution.py:423
  (1871 shorter events, 1556.4 us)
Async XLA Ops:
  7.2 112.5 %all-gather.9.cloned.1.call-start = ((), (), s32[]{:S(2)}) async-start(), calls=%async_computation.5 | async-start | bytes 4423680 | tf_op jit(solution)/shard_map/all_gather | solution.py:487
  12.0 136.9 %all-gather.19.cloned.1.call-start = ((), (), s32[]{:S(2)}) async-start(), calls=%async_computation.10 | async-start | bytes 4423680 | tf_op jit(solution)/shard_map/all_gather | solution.py:488
  15.0 195.3 %all-gather.17.cloned.1.call-start = ((), (), s32[]{:S(2)}) async-start(), calls=%async_computation.9 | async-start | bytes 8847360 | tf_op jit(solution)/shard_map/all_gather | solution.py:492
  21.0 223.0 %all-gather.15.cloned.1.call-start = ((), (), s32[]{:S(2)}) async-start(), calls=%async_computation.8 | async-start | bytes 8847360 | tf_op jit(solution)/shard_map/all_gather | solution.py:491
  27.5 262.9 %all-gather.13.cloned.1.call-start = ((), (), s32[]{:S(2)}) async-start(), calls=%async_computation.7 | async-start | bytes 8847360 | tf_op jit(solution)/shard_map/all_gather | solution.py:490
  33.0 279.7 %all-gather.11.cloned.1.call-start = ((), (), s32[]{:S(2)}) async-start(), calls=%async_computation.6 | async-start | bytes 13271040 | tf_op jit(solution)/shard_map/all_gather | solution.py:489
  44.9 598.8 %all-reduce.47.cloned.1.call-start = ((), (), s32[]{:S(2)}) async-start(), calls=%async_computation.23 | async-start | bytes 786432 | tf_op jit(solution)/shard_map/psum | solution.py:159
  571.1 248.3 %all-reduce.45.cloned.1.call-start = ((), (), s32[]{:S(2)}) async-start(), calls=%async_computation.22 | async-start | bytes 786432 | tf_op jit(solution)/shard_map/psum | solution.py:159
  745.7 165.9 %all-gather.21.cloned.1.call-start = ((), (), s32[]{:S(2)}) async-start(), calls=%async_computation.11 | async-start | bytes 17694720 | tf_op jit(solution)/shard_map/all_gather | solution.py:493
  751.3 225.3 %all-gather.23.cloned.1.call-start = ((), (), s32[]{:S(2)}) async-start(), calls=%async_computation.12 | async-start | bytes 11520000 | tf_op jit(solution)/shard_map/all_gather | solution.py:494
  755.4 300.7 %all-reduce.43.cloned.1.call-start = ((), (), s32[]{:S(2)}) async-start(), calls=%async_computation.21 | async-start | bytes 1572864 | tf_op jit(solution)/shard_map/psum | solution.py:159
  960.7 211.0 %all-reduce.41.cloned.1.call-start = ((), (), s32[]{:S(2)}) async-start(), calls=%async_computation.20 | async-start | bytes 786432 | tf_op jit(solution)/shard_map/psum | solution.py:159
  1101.1 400.6 %all-reduce.39.cloned.1.call-start = ((), (), s32[]{:S(2)}) async-start(), calls=%async_computation.19 | async-start | bytes 786432 | tf_op jit(solution)/shard_map/psum | solution.py:159
  1207.8 61.4 %collective-permute-start.29 = (bf16[64,1,4,768]{3,0,2,1:T(8,128)(2,1)}, bf16[64,1,4,768]{3,0,2,1:T(8,128)(2,1)}, u32[]{:S(2)}, u32[]{:S(2)}) collective-permute-start(bf16[64,1,4,768]{3,0,2,1:T(8,128)(2,1)} %get-tuple-element.531), channel_id=1, source_target_pairs={{2,0},{4,2},{6,4},{3,1},{5,3},{7,5},{10,8},{12,10},{14,12},{11,9},... | collective-permute-start | bytes 1179656 | tf_op jit(solution)/shard_map/ppermute | solution.py:35
  1209.3 60.0 %collective-permute-start.28 = (bf16[64,1,4,768]{3,0,2,1:T(8,128)(2,1)}, bf16[64,1,4,768]{3,0,2,1:T(8,128)(2,1)}, u32[]{:S(2)}, u32[]{:S(2)}) collective-permute-start(bf16[64,1,4,768]{3,0,2,1:T(8,128)(2,1)} %get-tuple-element.532), channel_id=1, source_target_pairs={{0,2},{2,4},{4,6},{1,3},{3,5},{5,7},{8,10},{10,12},{12,14},{9,11},... | collective-permute-start | bytes 1179656 | tf_op jit(solution)/shard_map/ppermute | solution.py:32
  1214.6 62.9 %collective-permute-start.43 = (bf16[64,1,4,768]{3,0,2,1:T(8,128)(2,1)}, bf16[64,1,4,768]{3,0,2,1:T(8,128)(2,1)S(1)}, u32[]{:S(2)}, u32[]{:S(2)}) collective-permute-start(bf16[64,1,4,768]{3,0,2,1:T(8,128)(2,1)} %get-tuple-element.523), channel_id=1, source_target_pairs={{2,0},{4,2},{6,4},{3,1},{5,3},{7,5},{10,8},{12,10},{14,12},{11,9},... | collective-permute-start | bytes 1179656 | tf_op jit(solution)/shard_map/ppermute | solution.py:35
  1215.9 61.6 %collective-permute-start.42 = (bf16[64,1,4,768]{3,0,2,1:T(8,128)(2,1)}, bf16[64,1,4,768]{3,0,2,1:T(8,128)(2,1)}, u32[]{:S(2)}, u32[]{:S(2)}) collective-permute-start(bf16[64,1,4,768]{3,0,2,1:T(8,128)(2,1)} %get-tuple-element.524), channel_id=1, source_target_pairs={{0,2},{2,4},{4,6},{1,3},{3,5},{5,7},{8,10},{10,12},{12,14},{9,11},... | collective-permute-start | bytes 1179656 | tf_op jit(solution)/shard_map/ppermute | solution.py:32
  1297.3 80.5 %collective-permute-start.33 = (bf16[64,1,4,768]{3,0,2,1:T(8,128)(2,1)}, bf16[64,1,4,768]{3,0,2,1:T(8,128)(2,1)S(1)}, u32[]{:S(2)}, u32[]{:S(2)}) collective-permute-start(bf16[64,1,4,768]{3,0,2,1:T(8,128)(2,1)} %get-tuple-element.527), channel_id=1, source_target_pairs={{2,0},{4,2},{6,4},{3,1},{5,3},{7,5},{10,8},{12,10},{14,12},{11,9},... | collective-permute-start | bytes 1179656 | tf_op jit(solution)/shard_map/ppermute | solution.py:35
  1298.6 79.2 %collective-permute-start.32 = (bf16[64,1,4,768]{3,0,2,1:T(8,128)(2,1)}, bf16[64,1,4,768]{3,0,2,1:T(8,128)(2,1)S(1)}, u32[]{:S(2)}, u32[]{:S(2)}) collective-permute-start(bf16[64,1,4,768]{3,0,2,1:T(8,128)(2,1)} %get-tuple-element.528), channel_id=1, source_target_pairs={{0,2},{2,4},{4,6},{1,3},{3,5},{5,7},{8,10},{10,12},{12,14},{9,11},... | collective-permute-start | bytes 1179656 | tf_op jit(solution)/shard_map/ppermute | solution.py:32
  1314.7 70.8 %collective-permute-start.47 = (bf16[64,1,4,768]{3,0,2,1:T(8,128)(2,1)}, bf16[64,1,4,768]{3,0,2,1:T(8,128)(2,1)S(1)}, u32[]{:S(2)}, u32[]{:S(2)}) collective-permute-start(bf16[64,1,4,768]{3,0,2,1:T(8,128)(2,1)} %get-tuple-element.519), channel_id=1, source_target_pairs={{2,0},{4,2},{6,4},{3,1},{5,3},{7,5},{10,8},{12,10},{14,12},{11,9},... | collective-permute-start | bytes 1179656 | tf_op jit(solution)/shard_map/ppermute | solution.py:35
  1316.0 69.5 %collective-permute-start.46 = (bf16[64,1,4,768]{3,0,2,1:T(8,128)(2,1)}, bf16[64,1,4,768]{3,0,2,1:T(8,128)(2,1)S(1)}, u32[]{:S(2)}, u32[]{:S(2)}) collective-permute-start(bf16[64,1,4,768]{3,0,2,1:T(8,128)(2,1)} %get-tuple-element.520), channel_id=1, source_target_pairs={{0,2},{2,4},{4,6},{1,3},{3,5},{5,7},{8,10},{10,12},{12,14},{9,11},... | collective-permute-start | bytes 1179656 | tf_op jit(solution)/shard_map/ppermute | solution.py:32
  1432.3 929.5 %all-reduce.49.cloned.1.call-start = ((), (), s32[]{:S(2)}) async-start(), calls=%async_computation.24 | async-start | bytes 42467328
  1538.3 288.6 %collective-permute-start.37 = (bf16[64,1,4,768]{3,0,2,1:T(8,128)(2,1)}, bf16[64,1,4,768]{3,0,2,1:T(8,128)(2,1)}, u32[]{:S(2)}, u32[]{:S(2)}) collective-permute-start(bf16[64,1,4,768]{3,0,2,1:T(8,128)(2,1)} %get-tuple-element.515), channel_id=1, source_target_pairs={{2,0},{4,2},{6,4},{3,1},{5,3},{7,5},{10,8},{12,10},{14,12},{11,9},... | collective-permute-start | bytes 1179656 | tf_op jit(solution)/shard_map/ppermute | solution.py:35
  1539.7 287.2 %collective-permute-start.36 = (bf16[64,1,4,768]{3,0,2,1:T(8,128)(2,1)}, bf16[64,1,4,768]{3,0,2,1:T(8,128)(2,1)}, u32[]{:S(2)}, u32[]{:S(2)}) collective-permute-start(bf16[64,1,4,768]{3,0,2,1:T(8,128)(2,1)} %get-tuple-element.516), channel_id=1, source_target_pairs={{0,2},{2,4},{4,6},{1,3},{3,5},{5,7},{8,10},{10,12},{12,14},{9,11},... | collective-permute-start | bytes 1179656 | tf_op jit(solution)/shard_map/ppermute | solution.py:32
  1545.0 289.1 %collective-permute-start.51 = (bf16[64,1,4,768]{3,0,2,1:T(8,128)(2,1)}, bf16[64,1,4,768]{3,0,2,1:T(8,128)(2,1)S(1)}, u32[]{:S(2)}, u32[]{:S(2)}) collective-permute-start(bf16[64,1,4,768]{3,0,2,1:T(8,128)(2,1)} %get-tuple-element.511), channel_id=1, source_target_pairs={{2,0},{4,2},{6,4},{3,1},{5,3},{7,5},{10,8},{12,10},{14,12},{11,9},... | collective-permute-start | bytes 1179656 | tf_op jit(solution)/shard_map/ppermute | solution.py:35
  1546.3 287.8 %collective-permute-start.50 = (bf16[64,1,4,768]{3,0,2,1:T(8,128)(2,1)}, bf16[64,1,4,768]{3,0,2,1:T(8,128)(2,1)}, u32[]{:S(2)}, u32[]{:S(2)}) collective-permute-start(bf16[64,1,4,768]{3,0,2,1:T(8,128)(2,1)} %get-tuple-element.512), channel_id=1, source_target_pairs={{0,2},{2,4},{4,6},{1,3},{3,5},{5,7},{8,10},{10,12},{12,14},{9,11},... | collective-permute-start | bytes 1179656 | tf_op jit(solution)/shard_map/ppermute | solution.py:32
  1825.6 548.9 %reduce-scatter.17.cloned.1.call-start = ((), (), s32[]{:S(2)}) async-start(), calls=%async_computation.17 | async-start | bytes 13271040
  2029.5 352.4 %reduce-scatter.11.cloned.1.call-start = ((), (), s32[]{:S(2)}) async-start(), calls=%async_computation.14 | async-start | bytes 4423680 | tf_op jit(solution)/shard_map/reduce_scatter | solution.py:400
  2058.2 323.7 %reduce-scatter.9.cloned.1.call-start = ((), (), s32[]{:S(2)}) async-start(), calls=%async_computation.13 | async-start | bytes 4423680 | tf_op jit(solution)/shard_map/reduce_scatter | solution.py:397
  2215.1 226.7 %reduce-scatter.15.cloned.1.call-start = ((), (), s32[]{:S(2)}) async-start(), calls=%async_computation.16 | async-start | bytes 11796480 | tf_op jit(solution)/shard_map/reduce_scatter | solution.py:418
  2275.0 278.8 %reduce-scatter.13.cloned.1.call-start = ((), (), s32[]{:S(2)}) async-start(), calls=%async_computation.15 | async-start | bytes 17694720 | tf_op jit(solution)/shard_map/reduce_scatter | solution.py:415
  2359.3 687.4 %all-reduce.37.cloned.1.call-start = ((), (), s32[]{:S(2)}) async-start(), calls=%async_computation.18 | async-start | bytes 31260672 | tf_op jit(solution)/shard_map/psum | solution.py:423
  (559 other events, 7630.5 us)
Sparse Core Ops, SparseCore 0:
  12.1 33.4 all-gather.8
  47.8 30.7 all-gather.18
  80.7 50.8 all-gather.16
  133.6 50.8 all-gather.14
  186.5 50.8 all-gather.12
  239.3 70.9 all-gather.10
  571.2 72.4 all-reduce.46
  745.8 73.4 all-reduce.44
  821.5 90.0 all-gather.20
  913.6 62.9 all-gather.22
  981.2 74.8 all-reduce.42
  1101.2 70.3 all-reduce.40
  1432.5 69.1 all-reduce.38
  1825.7 359.1 all-reduce.48
  2187.4 86.3 reduce-scatter.16
  2276.8 40.4 reduce-scatter.10
  2320.4 40.4 reduce-scatter.8
  2363.3 78.4 reduce-scatter.14
  2444.4 109.3 reduce-scatter.12
  2560.6 486.0 all-reduce.36
where the time goes:
time: 3190 us; the launch traced here: 3180 us
  local copies, waits for them, and re-layouts  1040 us (33%)
  waiting for transfers between devices  999 us (31%)
  other arithmetic  496 us (16%)
  matrix products  410 us (13%)
  starting transfers between devices  160 us (5%)
  blocking collectives  43.8 us (1%)
    psum x1, waiting for transfers between devices, reduce_end(): lax.psum(shards[0].astype(jnp.bfloat16), ('ha', 'wa')).astype(jnp.float32)  421 us
    psum x5, waiting for transfers between devices, spatial_sum(): lax.psum(summed.astype(jnp.bfloat16), ('ha', 'wa')).astype(jnp.float32)  259 us
    gather x8, local copies, waits for them, and re-layouts, to_slots(): jnp.take(gradients[k], tables[k][1], axis=ROW_DIMS[k])  238 us
    unnamed x1112, local copies, waits for them, and re-layouts  204 us
    gather x8, local copies, waits for them, and re-layouts, body(): jnp.take(gathered[k], tables[k][0], axis=ROW_DIMS[k])  162 us
    reduce_scatter x1, waiting for transfers between devices, reduce_end(): lax.psum_scatter(slots[6].astype(jnp.bfloat16), 'dp', scatter_dimension=0...  112 us
    ppermute x24, starting transfers between devices, padded_2(): lax.ppermute(lax.slice_in_dim(block, block.shape[dim] - width, None, axis...  109 us
    another operation x16, local copies, waits for them, and re-layouts, layer_backward(): mids = jnp.stack([mid_grad_a, mid_grad_b])  108 us
  transfers between devices with their start and end apart: 76, of which 21 were waited for; matrix products, arithmetic and copies ran while one was open for 45% of the time, Pallas kernels for 0%

commit v1 on v0

v1 whole, which is shorter than its diff:
```python
import functools

import jax
import jax.numpy as jnp
from jax import lax
from jax.experimental import pallas as pl
from jax.experimental.pallas import tpu as pltpu
from jax.sharding import PartitionSpec as P

NECK = 768
GROUP = 128
HEIGHT = 8
BREADTH = 8
CELLS = HEIGHT * BREADTH
LAYERS = 2
STEP_COUNT = 5

GAMMA = 1.7015043497085571
ALPHA = 0.2
CLIP = 0.01
RATE = 0.05
SMALL_RATE = 0.5
DECAY_ONE = 0.9
DECAY_TWO = 0.999
ADAM_EPS = 1e-08
WEIGHT_DECAY = 5e-05
STD_EPS = 0.0001
GELU_SCALE = 0.7978845608028654
GELU_CUBE = 0.044715
EVERY = ("dp", "ha", "wa")
MIB = 1 << 20

TAPS_ONE = tuple((0, t // 3 - 1, t % 3 - 1) for t in range(9))
TAPS_TWO = tuple(((t // 3 % 2) * 2 + t % 3 % 2, t // 3 // 2, t % 3 // 2) for t in range(9))

f32 = jnp.float32
bf16 = jnp.bfloat16


def gelu_act(v):
    return 0.5 * v * (1.0 + jnp.tanh(GELU_SCALE * (v + GELU_CUBE * v * v * v)))


def gelu_prime(v):
    th = jnp.tanh(GELU_SCALE * (v + GELU_CUBE * v * v * v))
    return 0.5 * (1.0 + th) + (0.5 * GELU_SCALE) * v * (1.0 - th * th) * (
        1.0 + 3.0 * GELU_CUBE * v * v
    )


def standardize(weight):
    fan_in = weight.shape[-1]
    centre = weight - jnp.mean(weight, axis=-1, keepdims=True)
    spread = jnp.mean(centre * centre, axis=-1, keepdims=True)
    return centre * lax.rsqrt(spread * fan_in + STD_EPS)


def owner_tables(shares):
    devices = shares.shape[0]
    ids = jnp.arange(devices, dtype=jnp.int32)
    starts = jnp.sum(jnp.where(ids[None, :] < ids[:, None], shares[None, :], 0), axis=1)
    part_ids = jnp.arange(4 * devices, dtype=jnp.int32)
    owner = jnp.sum((part_ids[:, None] >= (starts + shares)[None, :]).astype(jnp.int32), axis=1)
    first = jnp.sum(jnp.where(owner[:, None] == ids[None, :], starts[None, :], 0), axis=1)
    local = (part_ids - first).astype(jnp.int32)
    held = jnp.minimum(jnp.arange(6, dtype=jnp.int32)[None, :], shares[:, None] - 1)
    return owner, local, starts, (starts[:, None] + held).reshape(-1).astype(jnp.int32)


def known_mesh():
    return tuple(lax.axis_size(a) for a in EVERY) == (4, 4, 2)


def unit_slots(owner, local, part):
    return ((owner * 6 + local)[:, None] * part + jnp.arange(part)[None, :]).reshape(-1)


def gather_plain(entries, owner, local):
    full = []
    for array, lead, standard in entries:
        block = standardize(array[lead]) if standard else array[lead]
        every = lax.all_gather(block.astype(bf16), "dp", axis=0, tiled=True)
        full.append(jnp.take(every, unit_slots(owner, local, block.shape[0] // 6), axis=0))
    return full


def sum_plain(gradient, slot_part):
    part = gradient.shape[0] // (4 * lax.axis_size("dp"))
    units = (slot_part[:, None] * part + jnp.arange(part)[None, :]).reshape(-1)
    slots = jnp.take(gradient, units, axis=0)
    owned = lax.psum_scatter(slots, "dp", scatter_dimension=0, tiled=True)
    return lax.psum(owned, ("ha", "wa"))


def leads(shape):
    tuples = [()]
    for size in shape[:-2]:
        tuples = [t + (i,) for t in tuples for i in range(size)]
    return tuples


def packed_rows(part, width):
    return part * (-(-width // 128))


def pack_into(ref, at, block):
    part, width = block.shape
    for column in range(0, width, 128):
        lanes = min(128, width - column)
        piece = block[:, column : column + lanes]
        if lanes < 128:
            piece = jnp.concatenate([piece, jnp.zeros((part, 128 - lanes), piece.dtype)], axis=1)
        ref[at : at + part, :] = piece
        at += part
    return at


def read_packed(ref, at, part, width):
    pieces = []
    for column in range(0, width, 128):
        pieces.append(ref[at : at + part, : min(128, width - column)])
        at += part
    return (pieces[0] if len(pieces) == 1 else jnp.concatenate(pieces, axis=1)), at


def pack_weights_kernel(standard, *refs):
    out_ref = refs[-1]
    at = 0
    for ref, flag in zip(refs[:-1], standard):
        block = ref[...]
        at = pack_into(out_ref, at, (standardize(block) if flag else block).astype(bf16))


def pack_weights(entries):
    specs, rows = [], 0
    for array, lead, _ in entries:
        part, width = array.shape[-2] // 6, array.shape[-1]
        specs.append(
            pl.BlockSpec((None,) * len(lead) + (part, width), lambda j, lead=lead: lead + (j, 0))
        )
        rows += packed_rows(part, width)
    return pl.pallas_call(
        functools.partial(pack_weights_kernel, tuple(e[2] for e in entries)),
        grid=(6,),
        out_shape=jax.ShapeDtypeStruct((6, rows, 128), bf16),
        in_specs=specs,
        out_specs=pl.BlockSpec((None, rows, 128), lambda j: (j, 0, 0)),
        compiler_params=pltpu.CompilerParams(vmem_limit_bytes=40 * MIB),
        cost_estimate=pl.CostEstimate(
            flops=6 * rows * 128 * 8, bytes_accessed=6 * rows * 128 * 6, transcendentals=0
        ),
        name="pack_weights",
    )(*[e[0] for e in entries])


def unpack_kernel(counts, shapes, which_ref, *refs):
    sources = refs[counts : counts + counts]
    outs = refs[2 * counts :]
    for s, source in enumerate(sources):

        @pl.when(which_ref[pl.program_id(0)] == s)
        def _(source=source):
            at = 0
            for out, (part, width) in zip(outs, shapes):
                block, at = read_packed(source, at, part, width)
                out[...] = block


def unpack_weights(sources, which, places, shapes):
    count, parts = len(sources), which.shape[0]
    rows = sources[0].shape[1]
    grid_spec = pltpu.PrefetchScalarGridSpec(
        num_scalar_prefetch=1 + count,
        grid=(parts,),
        in_specs=[
            pl.BlockSpec((None, rows, 128), lambda i, *tables, s=s: (tables[1 + s][i], 0, 0))
            for s in range(count)
        ],
        out_specs=[pl.BlockSpec((p, w), lambda i, *tables: (i, 0)) for p, w in shapes],
    )
    return pl.pallas_call(
        functools.partial(unpack_kernel, count, shapes),
        grid_spec=grid_spec,
        out_shape=[jax.ShapeDtypeStruct((parts * p, w), bf16) for p, w in shapes],
        compiler_params=pltpu.CompilerParams(vmem_limit_bytes=40 * MIB),
        cost_estimate=pl.CostEstimate(
            flops=0, bytes_accessed=parts * rows * 128 * 4, transcendentals=0
        ),
        name="unpack_weights",
    )(which, *places, *sources)


def gather_packed(packed, halves, owner, local):
    me = lax.axis_index("dp")
    chip = [(i, i ^ 2) for i in range(4)]
    core = [(i, i ^ 1) for i in range(4)]
    buffers = [packed]
    if halves:
        side = lax.axis_index("wa")
        mine = lax.dynamic_slice_in_dim(packed, side * 3, 3, 0)
        near = lax.ppermute(mine, "dp", chip)
        far = lax.ppermute(near, "wa", [(0, 1), (1, 0)])
        buffers += [near, far]
    else:
        buffers += [lax.ppermute(packed, "dp", chip)]
    buffers += [lax.ppermute(b, "dp", core) for b in buffers]
    half = len(buffers) // 2
    apart = (owner // 2 != me // 2).astype(jnp.int32)
    if halves:
        which = jnp.where(apart == 1, jnp.where(local // 3 == side, 1, 2), 0)
        at = jnp.where(apart == 1, local % 3, local)
    else:
        which, at = apart, local
    which = (which + half * (owner % 2 != me % 2)).astype(jnp.int32)
    places = []
    parts = jnp.arange(owner.shape[0])
    for s in range(len(buffers)):
        found = jnp.where((which[None, :] == s) & (parts[None, :] <= parts[:, None]), at[None, :], 0)
        places.append(jnp.max(found, axis=1).astype(jnp.int32))
    return buffers, which, places


def pack_gradients_kernel(pad, part_ref, *refs):
    out_ref = refs[-1]
    at = 0
    for ref in refs[:-1]:
        at = pack_into(out_ref, at, ref[...].astype(bf16))
    if pad:
        out_ref[at : at + pad, :] = jnp.zeros((pad, 128), bf16)


def pack_gradients(gradients, slot_part, devices, unit):
    specs, rows = [], 0
    for gradient in gradients:
        part, width = gradient.shape[0] // (4 * devices), gradient.shape[1]
        specs.append(pl.BlockSpec((part, width), lambda s, parts: (parts[s], 0)))
        rows += packed_rows(part, width)
    pad = -rows % unit
    rows += pad
    slots = 6 * devices
    return pl.pallas_call(
        functools.partial(pack_gradients_kernel, pad),
        grid_spec=pltpu.PrefetchScalarGridSpec(
            num_scalar_prefetch=1,
            grid=(slots,),
            in_specs=specs,
            out_specs=pl.BlockSpec((None, rows, 128), lambda s, parts: (s, 0, 0)),
        ),
        out_shape=jax.ShapeDtypeStruct((slots, rows, 128), bf16),
        compiler_params=pltpu.CompilerParams(vmem_limit_bytes=40 * MIB),
        cost_estimate=pl.CostEstimate(
            flops=0, bytes_accessed=slots * rows * 128 * 4, transcendentals=0
        ),
        name="pack_gradients",
    )(slot_part, *gradients)


SPAN = 1280
AXES = ("x", "y", "near", "far")


def sum_kernel(orders, spans, packed, owned, own, core, one, two, three, four, sends, recvs, local_sems):
    dp, z, y = lax.axis_index("dp"), lax.axis_index("ha"), lax.axis_index("wa")
    bit = {"x": dp // 2, "core": dp % 2, "y": y, "near": z % 2, "far": z // 2}
    peer = {
        "x": {"dp": (dp + 2) % 4},
        "core": {"dp": dp + 1 - 2 * (dp % 2)},
        "y": {"wa": 1 - y},
        "near": {"ha": z + 1 - 2 * (z % 2)},
        "far": {"ha": (z + 2) % 4},
    }
    barrier = pltpu.get_barrier_semaphore()
    for other in peer.values():
        pl.semaphore_signal(barrier, inc=1, device_id=other, device_id_type=pl.DeviceIdType.MESH)
    pl.semaphore_wait(barrier, len(peer))

    buffers = [core, one, two, three, four]
    kinds = len(orders)

    def index(ref, chunk, names, fixed):
        return ref.at[(chunk,) + tuple(fixed[n] if n in fixed else slice(None) for n in names)]

    def remote(src, dst, stage, chunk, to):
        return pltpu.make_async_remote_copy(
            src_ref=src,
            dst_ref=dst,
            send_sem=sends.at[stage, chunk],
            recv_sem=recvs.at[stage, chunk],
            device_id=peer[to],
            device_id_type=pl.DeviceIdType.MESH,
        )

    def copy_of(stage, kind, chunk):
        order = orders[kind]
        if stage == 0:
            return remote(packed.at[:, 1 - bit["core"], chunk], core.at[chunk], 0, chunk, "core")
        if stage <= 4:
            before = [n for n in AXES if n not in order[: stage - 1]]
            axis = order[stage - 1]
            src = index(buffers[stage - 1], chunk, before, {axis: 1 - bit[axis]})
            return remote(src, buffers[stage].at[chunk], stage, chunk, axis)
        spread = [n for n in reversed(order) if n != "x"]
        axis = spread[stage - 5]
        fixed = {n: bit[n] for n in spread[stage - 5 :]}
        place = index(owned, chunk, AXES[1:], fixed)
        return remote(four.at[chunk] if stage == 5 else place, place, stage, chunk, axis)

    def load(chunk):
        slot = chunk % 2
        return pltpu.make_async_copy(
            packed.at[:, bit["core"], chunk], own.at[slot], local_sems.at[slot]
        )

    def store(chunk):
        place = owned.at[chunk, bit["y"], bit["near"], bit["far"]]
        return pltpu.make_async_copy(four.at[chunk], place, local_sems.at[2 + chunk])

    def add(target, names, other, prefix=()):
        for at in names:
            there = target[at].astype(f32) + other(at).astype(f32)
            target[at] = there.astype(bf16)

    def grid(count):
        return leads((2,) * count + (1, 1))

    def arrive(stage, kind, chunk):
        copy_of(stage, kind, chunk).wait_recv()
        order = orders[kind]
        if stage == 0:
            load(chunk).wait()
            add(core, [(chunk,) + t for t in grid(4)], lambda at: own[(chunk % 2,) + at[1:]])
        elif stage <= 4:
            before = [n for n in AXES if n not in order[: stage - 1]]
            axis = order[stage - 1]
            where = before.index(axis)

            def mine(at):
                rest = at[1:]
                return buffers[stage - 1][(chunk,) + rest[:where] + (bit[axis],) + rest[where:]]

            add(buffers[stage], [(chunk,) + t for t in grid(4 - stage)], mine)
            if stage == 4:
                store(chunk).start()
        if stage == 5:
            store(chunk).wait()

    ahead, last = 3, 7
    for chunk in range(ahead):
        copy_of(0, chunk % kinds, chunk).start()
    load(0).start()

    def step(s, q, first=False):
        @pl.when(s + ahead < spans)
        def _():
            copy_of(0, (q + ahead) % kinds, s + ahead).start()

        @pl.when(s + 1 < spans)
        def _():
            load(s + 1).start()

        for stage in range(last + 1):
            chunk = s - stage
            kind = (q - stage) % kinds

            @pl.when((chunk >= 0) & (chunk < spans))
            def _(stage=stage, chunk=chunk, kind=kind):
                arrive(stage, kind, chunk)
                if stage < last:
                    copy_of(stage + 1, kind, chunk).start()

    def steps(i, carry):
        for q in range(kinds):
            step(i * kinds + q, q)
        return carry

    lax.fori_loop(0, -(-(spans + last) // kinds), steps, 0)

    def sent(i, carry):
        for q in range(kinds):
            for stage in range(last + 1):
                copy_of(stage, q, i * kinds + q).wait_send()
        return carry

    lax.fori_loop(0, spans // kinds, sent, 0)


def sum_at_owners(packed):
    slots, rows, lanes = packed.shape
    spans = 6 * rows // SPAN
    r = SPAN // 8
    orders = (AXES,)
    owned = pl.pallas_call(
        functools.partial(sum_kernel, orders, spans),
        out_shape=jax.ShapeDtypeStruct((spans, 2, 2, 2, r, 128), bf16),
        in_specs=[pl.BlockSpec(memory_space=pl.ANY)],
        out_specs=pl.BlockSpec(memory_space=pl.ANY),
        scratch_shapes=[
            pltpu.VMEM((2, 2, 2, 2, 2, r, 128), bf16),
            pltpu.VMEM((spans, 2, 2, 2, 2, r, 128), bf16),
            pltpu.VMEM((spans, 2, 2, 2, r, 128), bf16),
            pltpu.VMEM((spans, 2, 2, r, 128), bf16),
            pltpu.VMEM((spans, 2, r, 128), bf16),
            pltpu.VMEM((spans, r, 128), bf16),
            pltpu.SemaphoreType.DMA((8, spans)),
            pltpu.SemaphoreType.DMA((8, spans)),
            pltpu.SemaphoreType.DMA((2 + spans,)),
        ],
        compiler_params=pltpu.CompilerParams(
            collective_id=1, has_side_effects=True, vmem_limit_bytes=56 * MIB
        ),
        cost_estimate=pl.CostEstimate(
            flops=slots * rows * 128, bytes_accessed=slots * rows * 128 * 4, transcendentals=0
        ),
        name="sum_at_owners",
    )(packed.reshape(2, 2, spans, 2, 2, 2, r, 128))
    return owned.reshape(6, rows, lanes)


def moved(image, down, right):
    if right:
        column = lax.broadcasted_iota(jnp.int32, image.shape, 1) + right
        image = pltpu.roll(image, (-right) % BREADTH, 1)
        image = jnp.where((column >= 0) & (column < BREADTH), image, 0.0)
    if down:
        edge = jnp.zeros((abs(down),) + image.shape[1:], image.dtype)
        if down > 0:
            image = jnp.concatenate([image[down:], edge], axis=0)
        else:
            image = jnp.concatenate([edge, image[:down]], axis=0)
    return image


def fill_taps(taps, sign, read, write):
    for phase in sorted({t[0] for t in taps}):
        image = read(phase).astype(f32).reshape(HEIGHT, BREADTH, GROUP)
        for right in sorted({t[2] for t in taps if t[0] == phase}):
            shifted = moved(image, 0, sign * right)
            for tap, (own, down, own_right) in enumerate(taps):
                if own == phase and own_right == right:
                    window = moved(shifted, sign * down, 0)
                    write(tap, window.reshape(CELLS, GROUP).astype(bf16))


def conv_kernel(taps, chunk, act_ref, w_ref, pre_ref, out_ref, cols):
    rows = chunk * CELLS

    def step(i, carry):
        base = pl.multiple_of(i * rows, rows)
        for n in range(chunk):

            def read(phase, n=n):
                return act_ref[phase, pl.ds(base + n * CELLS, CELLS), :]

            def write(tap, window, n=n):
                cols[n * CELLS : (n + 1) * CELLS, tap * GROUP : (tap + 1) * GROUP] = window

            fill_taps(taps, 1, read, write)
        pre = lax.dot_general(
            cols[...], w_ref[...], (((1,), (1,)), ((), ())), preferred_element_type=f32
        )
        pre_ref[pl.ds(base, rows), :] = pre
        out_ref[pl.ds(base, rows), :] = (gelu_act(pre) * GAMMA).astype(bf16)
        return carry

    lax.fori_loop(0, pre_ref.shape[0] // rows, step, 0)


def conv_forward(act, weight, taps):
    phases, cells, channels = act.shape
    chunk = 4
    return pl.pallas_call(
        functools.partial(conv_kernel, taps, chunk),
        grid=(channels // GROUP,),
        out_shape=[
            jax.ShapeDtypeStruct((cells, channels), f32),
            jax.ShapeDtypeStruct((cells, channels), bf16),
        ],
        in_specs=[
            pl.BlockSpec((phases, cells, GROUP), lambda g: (0, 0, g)),
            pl.BlockSpec((GROUP, 9 * GROUP), lambda g: (g, 0)),
        ],
        out_specs=[
            pl.BlockSpec((cells, GROUP), lambda g: (0, g)),
            pl.BlockSpec((cells, GROUP), lambda g: (0, g)),
        ],
        scratch_shapes=[pltpu.VMEM((chunk * CELLS, 9 * GROUP), bf16)],
        compiler_params=pltpu.CompilerParams(vmem_limit_bytes=32 * MIB),
        cost_estimate=pl.CostEstimate(
            flops=2 * cells * channels * 9 * GROUP,
            bytes_accessed=cells * channels * (6 + 2 * phases),
            transcendentals=cells * channels,
        ),
        name="conv_forward",
    )(act, weight)


def conv_back_kernel(taps, chunk, up_ref, act_ref, pre_ref, w_ref, down_ref, grad_ref, w_cols, up_cols, act_cols):
    rows = chunk * CELLS
    phases = act_ref.shape[0]
    order = [t for q in range(phases) for t in range(9) if taps[t][0] == q]
    place = {t: i for i, t in enumerate(order)}
    for t in range(9):
        w_cols[place[t] * GROUP : (place[t] + 1) * GROUP, :] = w_ref[:, t * GROUP : (t + 1) * GROUP]

    def step(i, carry):
        base = pl.multiple_of(i * rows, rows)
        for n in range(chunk):

            def read_act(phase, n=n):
                return act_ref[phase, pl.ds(base + n * CELLS, CELLS), :]

            def write_act(tap, window, n=n):
                act_cols[pl.ds(base + n * CELLS, CELLS), tap * GROUP : (tap + 1) * GROUP] = window

            fill_taps(taps, 1, read_act, write_act)
            flat = tuple((0, t[1], t[2]) for t in taps)

            def read_up(phase, n=n):
                return up_ref[pl.ds(base + n * CELLS, CELLS), :]

            def write_up(tap, window, n=n):
                at = place[tap] * GROUP
                up_cols[n * CELLS : (n + 1) * CELLS, at : at + GROUP] = window

            fill_taps(flat, -1, read_up, write_up)
        at = 0
        for phase in range(phases):
            size = sum(t[0] == phase for t in taps) * GROUP
            back = jnp.dot(
                up_cols[:, at : at + size], w_cols[at : at + size, :], preferred_element_type=f32
            )
            at += size
            pre = pre_ref[phase, pl.ds(base, rows), :]
            down_ref[phase, pl.ds(base, rows), :] = (gelu_prime(pre) * GAMMA * back).astype(bf16)
        return carry

    lax.fori_loop(0, up_ref.shape[0] // rows, step, 0)
    grad_ref[...] = lax.dot_general(
        up_ref[...], act_cols[...], (((0,), (0,)), ((), ())), preferred_element_type=f32
    ).astype(grad_ref.dtype)


def conv_backward(up, act, pre, weight, taps):
    phases, cells, channels = act.shape
    chunk = 4
    return pl.pallas_call(
        functools.partial(conv_back_kernel, taps, chunk),
        grid=(channels // GROUP,),
        out_shape=[
            jax.ShapeDtypeStruct((phases, cells, channels), bf16),
            jax.ShapeDtypeStruct((channels, 9 * GROUP), bf16),
        ],
        in_specs=[
            pl.BlockSpec((cells, GROUP), lambda g: (0, g)),
            pl.BlockSpec((phases, cells, GROUP), lambda g: (0, 0, g)),
            pl.BlockSpec((phases, cells, GROUP), lambda g: (0, 0, g)),
            pl.BlockSpec((GROUP, 9 * GROUP), lambda g: (g, 0)),
        ],
        out_specs=[
            pl.BlockSpec((phases, cells, GROUP), lambda g: (0, 0, g)),
            pl.BlockSpec((GROUP, 9 * GROUP), lambda g: (g, 0)),
        ],
        scratch_shapes=[
            pltpu.VMEM((9 * GROUP, GROUP), bf16),
            pltpu.VMEM((chunk * CELLS, 9 * GROUP), bf16),
            pltpu.VMEM((cells, 9 * GROUP), bf16),
        ],
        compiler_params=pltpu.CompilerParams(vmem_limit_bytes=48 * MIB),
        cost_estimate=pl.CostEstimate(
            flops=4 * cells * channels * 9 * GROUP,
            bytes_accessed=cells * channels * (2 + 8 * phases),
            transcendentals=cells * channels * phases,
        ),
        name="conv_backward",
    )(up, act, pre, weight)


def new_values(w, g, m, v, standard, clip):
    fan_in = w.shape[1]
    if standard:
        centre = w - jnp.mean(w, axis=-1, keepdims=True)
        spread = jnp.mean(centre * centre, axis=-1, keepdims=True)
        scale = lax.rsqrt(spread * fan_in + STD_EPS)
        along = jnp.sum(g * centre, axis=-1, keepdims=True)
        mean_g = jnp.mean(g, axis=-1, keepdims=True)
        g = scale * (g - mean_g) - (scale * scale * scale * along) * centre
    if clip:
        ceiling = CLIP * jnp.sqrt(jnp.sum(w * w, axis=-1, keepdims=True))
        norm = jnp.sqrt(jnp.sum(g * g, axis=-1, keepdims=True))
        g = g * (ceiling / jnp.maximum(norm, ceiling))
    m = DECAY_ONE * m + (1.0 - DECAY_ONE) * g
    v = DECAY_TWO * v + (1.0 - DECAY_TWO) * g * g
    m_hat = m * (1.0 / (1.0 - DECAY_ONE**STEP_COUNT))
    v_hat = v * (1.0 / (1.0 - DECAY_TWO**STEP_COUNT))
    return m, v, w - RATE * (m_hat / (jnp.sqrt(v_hat) + ADAM_EPS) + WEIGHT_DECAY * w)


def update_packed_kernel(shapes, share_ref, packed_ref, *refs):
    count = len(shapes)
    valid = pl.program_id(0) < share_ref[0]
    at = 0
    for k, shape in enumerate(shapes):
        part, width = shape[-2] // 6, shape[-1]
        for lead in leads(shape):
            g, at = read_packed(packed_ref, at, part, width)
            g = jnp.where(valid, g.astype(f32), 0.0)
            w, m, v = (refs[3 * k + i][lead] for i in range(3))
            for i, value in enumerate(new_values(w, g, m, v, True, True)):
                refs[3 * (count + k) + i][lead] = value


def update_packed(packed, members, share):
    specs, operands, shapes = [], [], []
    for weight, first, second in members:
        shape = weight.shape
        block = shape[:-2] + (shape[-2] // 6, shape[-1])
        zeros = (0,) * (len(shape) - 2)
        specs += [pl.BlockSpec(block, lambda j, zeros=zeros: zeros + (j, 0))] * 3
        operands += [weight, first, second]
        shapes.append(shape)
    total = sum(o.size for o in operands)
    outs = pl.pallas_call(
        functools.partial(update_packed_kernel, tuple(shapes)),
        grid=(6,),
        out_shape=[jax.ShapeDtypeStruct(o.shape, f32) for o in operands],
        in_specs=[
            pl.BlockSpec(memory_space=pltpu.SMEM),
            pl.BlockSpec((None,) + packed.shape[1:], lambda j: (j, 0, 0)),
        ]
        + specs,
        out_specs=specs,
        compiler_params=pltpu.CompilerParams(vmem_limit_bytes=58 * MIB),
        cost_estimate=pl.CostEstimate(
            flops=10 * total, bytes_accessed=9 * total, transcendentals=total // 3
        ),
        name="update_packed",
    )(share, packed, *operands)
    return [tuple(outs[3 * k : 3 * k + 3]) for k in range(len(members))]


def update_kernel(unit, standard, clip, block, share_ref, w_ref, g_ref, m_ref, v_ref, m_out, v_out, w_out):
    row = pl.program_id(0) * block + lax.broadcasted_iota(jnp.int32, (block, 1), 0)
    g = jnp.where(row % (6 * unit) < share_ref[0] * unit, g_ref[...].astype(f32), 0.0)
    m_out[...], v_out[...], w_out[...] = new_values(
        w_ref[...], g, m_ref[...], v_ref[...], standard, clip
    )


def update(weight, gradient, first, second, share, standard, clip):
    shape = weight.shape
    width = shape[-1]
    flat = [a.reshape(-1, width) for a in (weight, gradient, first, second)]
    rows = flat[0].shape[0]
    block = rows
    for size in range(192, 0, -16):
        if rows % size == 0:
            block = size
            break
    spec = pl.BlockSpec((block, width), lambda i: (i, 0))
    outs = pl.pallas_call(
        functools.partial(update_kernel, shape[-2] // 6, standard, clip, block),
        grid=(rows // block,),
        out_shape=[jax.ShapeDtypeStruct((rows, width), f32)] * 3,
        in_specs=[pl.BlockSpec(memory_space=pltpu.SMEM)] + [spec] * 4,
        out_specs=[spec] * 3,
        compiler_params=pltpu.CompilerParams(vmem_limit_bytes=48 * MIB),
        cost_estimate=pl.CostEstimate(
            flops=30 * rows * width, bytes_accessed=28 * rows * width, transcendentals=rows * width
        ),
        name="update",
    )(share, *flat)
    return tuple(o.reshape(shape) for o in outs)


def dot_t(left, right):
    return lax.dot_general(
        left, right, (((left.ndim - 1,), (1,)), ((), ())), preferred_element_type=f32
    )


def dot_n(left, right):
    return lax.dot_general(
        left, right, (((left.ndim - 1,), (0,)), ((), ())), preferred_element_type=f32
    )


def dot_sum(upstream, inputs):
    up = upstream.reshape(-1, upstream.shape[-1])
    low = inputs.reshape(-1, inputs.shape[-1])
    return lax.dot_general(up, low, (((0,), (0,)), ((), ())), preferred_element_type=f32)


def tail_forward(act_three, out_w, down_w, up_w):
    images = act_three.shape[0] // CELLS
    pre_four = dot_t(act_three, out_w).reshape(images, CELLS, -1)
    squeezed = (jnp.sum(pre_four, axis=1) / CELLS).astype(bf16)
    pre_down = dot_t(squeezed, down_w)
    act_down = gelu_act(pre_down).astype(bf16)
    gate_sig = jax.nn.sigmoid(dot_t(act_down, up_w))
    return pre_four, squeezed, pre_down, act_down, gate_sig


def tail_backward(grad_hidden, stored, down_w, up_w, gain):
    pre_four, squeezed, pre_down, act_down, gate_sig = stored
    gate = 2.0 * gate_sig
    raw_gate = jnp.sum(grad_hidden * pre_four, axis=1)
    gain_part = ALPHA * jnp.sum(raw_gate * gate)
    grad_gate = raw_gate * (ALPHA * gain)
    grad_up = (grad_gate * 2.0 * gate_sig * (1.0 - gate_sig)).astype(bf16)
    grad_down = (gelu_prime(pre_down) * dot_n(grad_up, up_w)).astype(bf16)
    grad_squeezed = dot_n(grad_down, down_w)
    grad_four = (
        grad_hidden * (ALPHA * gain * gate)[:, None, :] + (grad_squeezed / CELLS)[:, None, :]
    ).astype(bf16)
    factors = jnp.concatenate([grad_up, act_down, grad_down, squeezed], axis=1)
    return grad_four.reshape(-1, grad_four.shape[-1]), factors, gain_part


def body(
    images,
    labels,
    class_counts,
    owner_share,
    w_entry,
    first_entry,
    second_entry,
    w_in,
    first_in,
    second_in,
    w_mid,
    first_mid,
    second_mid,
    w_out,
    first_out,
    second_out,
    se_down,
    first_down,
    second_down,
    se_up,
    first_up,
    second_up,
    w_final,
    first_final,
    second_final,
    head,
    first_head,
    second_head,
    small_params,
    first_small,
    second_small,
):
    owner, local, starts, slot_part = owner_tables(owner_share)
    me = lax.axis_index("dp")
    devices = lax.axis_size("dp")
    my_share = lax.dynamic_slice_in_dim(owner_share, me, 1, 0)
    my_start = lax.dynamic_index_in_dim(starts, me, 0, keepdims=False)

    rows_n, cols_n = lax.axis_size("ha"), lax.axis_size("wa")
    spread = rows_n * cols_n
    micro, per_dp, tile_h, tile_w, in_width = images.shape
    count = micro * per_dp // spread
    tiles = images.reshape(spread, count, tile_h, tile_w, in_width)
    tiles = lax.all_to_all(tiles, ("ha", "wa"), 0, 0, tiled=True)
    tiles = tiles.reshape(
        rows_n, cols_n, count, tile_h // 2, 2, tile_w // 2, 2, in_width
    ).transpose(4, 6, 2, 0, 3, 1, 5, 7)
    cells = count * CELLS
    pixels = tiles.reshape(4, cells, in_width)
    spot = lax.axis_index("ha") * cols_n + lax.axis_index("wa")
    my_labels = lax.dynamic_slice_in_dim(labels.reshape(-1), spot * count, count, 0)

    def gather(entries, halves):
        if not known_mesh():
            return gather_plain(entries, owner, local)
        shapes = tuple((e[0].shape[-2] // 6, e[0].shape[-1]) for e in entries)
        buffers, which, places = gather_packed(pack_weights(entries), halves, owner, local)
        return unpack_weights(buffers, which, places, shapes)

    def block_entries(layer):
        first = (w_entry, (), True) if layer == 0 else (w_in, (layer - 1,), True)
        return [
            first,
            (w_mid, (layer, 0), True),
            (w_mid, (layer, 1), True),
            (w_out, (layer,), True),
            (se_down, (layer,), False),
            (se_up, (layer,), False),
        ]

    in_low, mid_low, out_low, down_low, up_low = ([None] * LAYERS for _ in range(5))
    for layer in range(LAYERS):
        in_low[layer], mid_a, mid_b, out_low[layer], down_low[layer], up_low[layer] = gather(
            block_entries(layer), layer > 0
        )
        mid_low[layer] = (mid_a, mid_b)
    final_low, head_low = gather([(w_final, (), True), (head, (), False)], True)
    entry_low = in_low[0]
    in_low[0] = entry_low[:NECK]
    skip_low = entry_low[NECK:]

    gains = small_params[:LAYERS]
    head_bias = small_params[LAYERS:]
    images_all = micro * per_dp * lax.axis_size("dp")
    class_weight = 1.0 / class_counts.astype(f32)

    kept = []
    hidden = None
    for layer in range(LAYERS):
        scale = GAMMA * (1.0 + layer * ALPHA * ALPHA) ** (-0.5)
        source = pixels.astype(f32) if layer == 0 else hidden
        act_zero = (gelu_act(source) * scale).astype(bf16)
        if layer:
            act_zero = act_zero.reshape(1, cells, -1)
        taps = TAPS_TWO if layer == 0 else TAPS_ONE
        pre_one = dot_t(act_zero, in_low[layer])
        act_one = (gelu_act(pre_one) * GAMMA).astype(bf16)
        pre_two, act_two = conv_forward(act_one, mid_low[layer][0], taps)
        pre_three, act_three = conv_forward(act_two[None], mid_low[layer][1], TAPS_ONE)
        tail = tail_forward(act_three, out_low[layer], down_low[layer], up_low[layer])
        branch = (ALPHA * gains[layer]) * tail[0] * (2.0 * tail[4])[:, None, :]
        pooled = None
        if layer == 0:
            pooled = (jnp.sum(act_zero.astype(f32), axis=0) * 0.25).astype(bf16)
            shortcut = dot_t(pooled, skip_low).reshape(branch.shape)
        else:
            shortcut = hidden.reshape(branch.shape)
        before = hidden
        hidden = (shortcut + branch).reshape(cells, -1)
        kept.append((before, act_zero, pre_one, act_one, pre_two, act_two, pre_three, act_three, tail, pooled))

    hidden_low = hidden.astype(bf16)
    pre_final = dot_t(hidden_low, final_low).reshape(count, CELLS, -1)
    pooled_final = (jnp.sum(gelu_act(pre_final) * GAMMA, axis=1) / CELLS).astype(bf16)
    logits = dot_n(pooled_final, head_low) + head_bias
    largest = jnp.max(logits, axis=1, keepdims=True)
    log_total = largest[:, 0] + jnp.log(jnp.sum(jnp.exp(logits - largest), axis=1))
    one_hot = (my_labels[:, None] == jnp.arange(logits.shape[1])[None, :]).astype(f32)
    picked = jnp.sum(one_hot * logits, axis=1)
    image_weight = jnp.sum(one_hot * class_weight[None, :], axis=1)
    loss_part = jnp.sum(image_weight * (log_total - picked))
    softmax_p = jnp.exp(logits - log_total[:, None])
    grad_logits = image_weight[:, None] * (softmax_p - one_hot) / images_all
    bias_part = jnp.sum(grad_logits, axis=0)
    grad_low = grad_logits.astype(bf16)
    head_factors = lax.all_gather(
        jnp.concatenate([pooled_final, grad_low], axis=1), EVERY, axis=0, tiled=True
    )
    grad_pooled = dot_t(grad_low, head_low) * (GAMMA / CELLS)
    grad_final = (gelu_prime(pre_final) * grad_pooled[:, None, :]).astype(bf16).reshape(cells, -1)
    final_grad = dot_sum(grad_final, hidden_low).astype(bf16)
    grad_hidden = dot_n(grad_final, final_low)

    in_grads = [None] * LAYERS
    mid_grads = [None] * LAYERS
    out_grads = [None] * LAYERS
    block_factors = [None] * LAYERS
    gain_parts = [None] * LAYERS
    for layer in reversed(range(LAYERS)):
        before, act_zero, pre_one, act_one, pre_two, act_two, pre_three, act_three, tail, pooled = kept[layer]
        taps = TAPS_TWO if layer == 0 else TAPS_ONE
        grad_four, factors, gain_parts[layer] = tail_backward(
            grad_hidden.reshape(count, CELLS, -1), tail, down_low[layer], up_low[layer], gains[layer]
        )
        block_factors[layer] = lax.all_gather(factors, EVERY, axis=0, tiled=True)
        out_grads[layer] = dot_sum(grad_four, act_three).astype(bf16)
        grad_three = (gelu_prime(pre_three) * GAMMA * dot_n(grad_four, out_low[layer])).astype(bf16)
        grad_two, mid_b = conv_backward(grad_three, act_two[None], pre_two[None], mid_low[layer][1], TAPS_ONE)
        grad_one, mid_a = conv_backward(grad_two[0], act_one, pre_one, mid_low[layer][0], taps)
        mid_grads[layer] = (mid_a, mid_b)
        in_grad = dot_sum(grad_one, act_zero).astype(bf16)
        if layer == 0:
            skip_grad = dot_sum(grad_hidden.astype(bf16), pooled).astype(bf16)
            in_grads[layer] = jnp.concatenate([in_grad, skip_grad], axis=0)
        else:
            in_grads[layer] = in_grad
            scale = GAMMA * (1.0 + layer * ALPHA * ALPHA) ** (-0.5)
            grad_zero = dot_n(grad_one[0], in_low[layer])
            grad_hidden = grad_hidden + gelu_prime(before) * scale * grad_zero

    def own_units(units, inputs):
        width = units.shape[1]
        part = width // starts.shape[0] // 4
        padded = jnp.pad(units, ((0, 0), (0, 4 * part)))
        mine = lax.dynamic_slice_in_dim(padded, my_start * part, 6 * part, 1)
        return dot_sum(mine, inputs)

    final_width = pooled_final.shape[1]
    head_own = own_units(head_factors[:, :final_width], head_factors[:, final_width:])
    wide, narrow = tail[0].shape[-1], tail[3].shape[-1]
    up_own, down_own = [], []
    for layer in range(LAYERS):
        every = block_factors[layer]
        ends = [wide, wide + narrow, wide + 2 * narrow, 2 * wide + 2 * narrow]
        up_own.append(own_units(every[:, : ends[0]], every[:, ends[0] : ends[1]]))
        down_own.append(own_units(every[:, ends[1] : ends[2]], every[:, ends[2] : ends[3]]))

    small = jnp.concatenate([loss_part[None], jnp.stack(gain_parts), bias_part])
    small = jnp.sum(lax.all_gather(small, EVERY, axis=0, tiled=False), axis=0)
    loss_sum = small[0]
    small_grad = small[1:]

    flat_mids = [g for pair in mid_grads for g in pair]
    local_grads = [final_grad, in_grads[0]] + in_grads[1:] + out_grads + flat_mids
    members = (
        (w_final, first_final, second_final),
        (w_entry, first_entry, second_entry),
        (w_in, first_in, second_in),
        (w_out, first_out, second_out),
        (w_mid, first_mid, second_mid),
    )
    if known_mesh():
        packed = pack_gradients(local_grads, slot_part, devices, SPAN)
        new = update_packed(sum_at_owners(packed), members, my_share)
    else:
        sums = [sum_plain(g, slot_part) for g in local_grads]
        new = []
        for weight, first, second in members:
            count = len(leads(weight.shape))
            total, sums = jnp.stack(sums[:count]), sums[count:]
            new.append(update(weight, total, first, second, my_share, True, True))
    final_new, entry_new, in_new, out_new, mid_new = new
    down_new = update(se_down, jnp.stack(down_own), first_down, second_down, my_share, False, True)
    up_new = update(se_up, jnp.stack(up_own), first_up, second_up, my_share, False, True)
    head_new = update(head, head_own, first_head, second_head, my_share, False, False)
    results = [loss_sum]
    for new in (entry_new, in_new, mid_new, out_new, down_new, up_new, final_new, head_new):
        results.extend(new)
    m = DECAY_ONE * first_small + (1.0 - DECAY_ONE) * small_grad
    v = DECAY_TWO * second_small + (1.0 - DECAY_TWO) * small_grad * small_grad
    m_hat = m / (1.0 - DECAY_ONE**STEP_COUNT)
    v_hat = v / (1.0 - DECAY_TWO**STEP_COUNT)
    results.extend(
        [
            m,
            v,
            small_params
            - SMALL_RATE * (m_hat / (jnp.sqrt(v_hat) + ADAM_EPS) + WEIGHT_DECAY * small_params),
        ]
    )
    return tuple(results)


def solution(mesh):
    owned = (
        [P("dp", None)] * 3
        + [P(None, "dp", None)] * 3
        + [P(None, None, "dp", None)] * 3
        + [P(None, "dp", None)] * 9
        + [P("dp", None)] * 6
        + [P()] * 3
    )
    return jax.shard_map(
        body,
        mesh=mesh,
        in_specs=tuple([P(None, "dp", "ha", "wa", None), P(None, "dp"), P(), P()] + owned),
        out_specs=tuple([P()] + owned),
        check_vma=False,
    )
```

time: 3190 us -> 1160 us (0.36)
  local copies, waits for them, and re-layouts: 1040 us -> 120 us
  waiting for transfers between devices: 999 us -> 244 us
  Pallas kernels: 0 us -> 567 us
  other arithmetic: 496 us -> 42 us
  matrix products: 410 us -> 145 us
  starting transfers between devices: 160 us -> 16.7 us
  blocking collectives: 43.8 us -> 0 us
    psum x6 -> x0, waiting for transfers between devices: 680 us -> none  [the longest x1 421 us: reduce_end(): lax.psum(shards[0].astype(jnp.bfloat16), ('ha', 'wa')).astype(jnp.float32)]
    pallas_call x0 -> x20, Pallas kernels: none -> 567 us  [the longest x1 293 us: sum_at_owners(): pl.pallas_call(functools.partial(sum_kernel, orders, spans), out_shape=ja...]
    gather x17 -> x0, local copies, waits for them, and re-layouts: 401 us -> none  [the longest x8 238 us: to_slots(): jnp.take(gradients[k], tables[k][1], axis=ROW_DIMS[k])]
    dot_general x278 -> x31, matrix products: 410 us -> 145 us  [the longest x11 58 us: dot_t(): lax.dot_general(left, right, (((left.ndim - 1,), (1,)), ((), ())), prefer...]
    ppermute x56 -> x13, waiting for transfers between devices: 53.9 us -> 244 us  [the longest x2 185 us: gather_packed(): near = lax.ppermute(mine, 'dp', chip)]
    reduce_scatter x4 -> x0, waiting for transfers between devices: 172 us -> none  [the longest x1 112 us: reduce_end(): lax.psum_scatter(slots[6].astype(jnp.bfloat16), 'dp', scatter_dimension=0...]
    ppermute x56 -> x13, starting transfers between devices: 158 us -> 10.4 us  [the longest x2 4.95 us: gather_packed(): near = lax.ppermute(mine, 'dp', chip)]
    another operation x24 -> x6, local copies, waits for them, and re-layouts: 148 us -> 2.95 us  [the longest x16 108 us: layer_backward(): mids = jnp.stack([mid_grad_a, mid_grad_b])]
  transfers between devices with their start and end apart: 76 -> 18, of which waited for: 21 -> 3; matrix products, arithmetic and copies ran while one was open for 45% -> 12% of each run, Pallas kernels for 0% -> 39%
where the time goes in v1:
time: 1160 us
  Pallas kernels  567 us (49%)
  waiting for transfers between devices  244 us (21%)
  matrix products  145 us (12%)
  local copies, waits for them, and re-layouts  120 us (10%)
  other arithmetic  42 us (4%)
  between operations  21.1 us (2%)
  starting transfers between devices  16.7 us (1%)
    pallas_call x1, Pallas kernels, sum_at_owners(): pl.pallas_call(functools.partial(sum_kernel, orders, spans), out_shape=ja...  293 us
    ppermute x2, waiting for transfers between devices, gather_packed(): near = lax.ppermute(mine, 'dp', chip)  185 us
    unnamed x189, local copies, waits for them, and re-layouts  73.4 us
    pallas_call x4, Pallas kernels, conv_backward(): pl.pallas_call(functools.partial(conv_back_kernel, taps, chunk), grid=(ch...  68.7 us
    ppermute x2, waiting for transfers between devices, gather_packed(): far = lax.ppermute(near, 'wa', [(0, 1), (1, 0)])  58.2 us
    dot_general x11, matrix products, dot_t(): lax.dot_general(left, right, (((left.ndim - 1,), (1,)), ((), ())), prefer...  58 us
    pallas_call x1, Pallas kernels, update_packed(): pl.pallas_call(functools.partial(update_packed_kernel, tuple(shapes)), gr...  48 us
    dot_general x11, matrix products, dot_sum(): lax.dot_general(up, low, (((0,), (0,)), ((), ())), preferred_element_type...  43.5 us
  transfers between devices with their start and end apart: 18, of which 3 were waited for; matrix products, arithmetic and copies ran while one was open for 12% of the time, Pallas kernels for 39%

profile of v1, /device:TPU:0, one launch (start us, length us, event | category | flops | bytes accessed | tf_op | source)
XLA Modules:
  0.0 1155.9 jit_solution(4613469560672557769)
XLA Ops:
  27.5 6.4 pack_weights.3.refs_4_
  60.4 21.0 %collective-permute-done.3.refs_7_ = bf16[3,3168,128]{2,1,0:T(8,128)(2,1)} collective-permute-done((bf16[3,3168,128]{2,1,0:T(8,128)(2,1)}, bf16[3,3168,128]{2,1,0:T(8,128)(2,1)}, u32[]{:S(2)}, u32[]{:S(2)}) %collective-permute-start.3) | collective-permute-done | bytes 2433056 | tf_op jit(solution)/shard_map/ppermute | solution.py:201
  83.5 164.4 %collective-permute-done.8.refs_7_ = bf16[3,3840,128]{2,1,0:T(8,128)(2,1)S(1)} collective-permute-done((bf16[3,3840,128]{2,1,0:T(8,128)(2,1)}, bf16[3,3840,128]{2,1,0:T(8,128)(2,1)S(1)}, u32[]{:S(2)}, u32[]{:S(2)}) %collective-permute-start.8) | collective-permute-done | bytes 2949152 | tf_op jit(solution)/shard_map/ppermute | solution.py:201
  255.0 58.2 %collective-permute-done.9.refs_8_ = bf16[3,3840,128]{2,1,0:T(8,128)(2,1)} collective-permute-done((bf16[3,3840,128]{2,1,0:T(8,128)(2,1)S(1)}, bf16[3,3840,128]{2,1,0:T(8,128)(2,1)}, u32[]{:S(2)}, u32[]{:S(2)}) %collective-permute-start.9) | collective-permute-done | bytes 2949152 | tf_op jit(solution)/shard_map/ppermute | solution.py:202
  314.3 11.7 %unpack_weights.4 = (bf16[768,1536]{1,0:T(8,128)(2,1)S(1)}, bf16[768,1152]{1,0:T(8,128)(2,1)S(1)}, bf16[768,1152]{1,0:T(8,128)(2,1)S(1)}, bf16[1536,768]{1,0:T(8...) custom-call(s32[16]{0:T(128)S(1)} %get-tuple-element.348.which_ref, ...), custom_call_target="tpu_custom_call" | custom-call | bytes 25952256 | tf_op jit(solution)/shard_map/unpack_weights/pallas_call | solution.py:181
  334.1 7.0 copy.123
  348.8 12.1 %copy.126 = f32[2,2,16,4,2,2,4,512]{7,6,5,4,3,2,1,0:T(4,128)} copy(f32[2,2,16,4,2,2,4,512]{7,2,1,6,0,4,5,3:T(8,128)} %bitcast.170) | data formatting | bytes 16777216 | tf_op jit(solution)/shard_map/convert_element_type | solution.py:810
  361.0 10.0 reshape.363
  371.0 17.1 %unpack_weights.5 = (bf16[3072,1536]{1,0:T(8,128)(2,1)}, bf16[3072,1000]{1,0:T(8,128)(2,1)}) custom-call(s32[16]{0:T(128)S(1)} %get-tuple-element.348.which_ref, s32[16]{0:T(128)S(1)} %get-tuple-element.339.refs_0_, s32[16]{0:T(128)S(1)} %get-tuple-element.335.refs_1_, s32[16]{0:T(128)S(1)} %get-tuple-element.336.refs_2_, s32[16]{0:T(128)S(1)} %get-tuple-element.337.refs_3_, ...), custom_call_target="tpu_custom_call" | custom-call | bytes 31457280 | tf_op jit(solution)/shard_map/unpack_weights/pallas_call | solution.py:181
  388.1 11.0 unpack_weights.3
  399.2 16.4 %fusion.5 = (bf16[4,1024,768]{2,1,0:T(8,128)(2,1)S(1)}, f32[4,1024,768]{2,1,0:T(8,128)}) fusion(bf16[2304,512]{1,0:T(8,128)(2,1)S(1)} %get-tuple-element.82, f32[4,1024,512]{2,1,0:T(8,128)} %reshape.363), kind=kOutput, calls=%fused_computation.8 | convolution fusion | flops 3273654272 | bytes 28049408 | tf_op jit(solution)/shard_map/dot_general | solution.py:676
  415.6 11.1 conv_forward.4
  428.4 9.8 conv_forward.5
  454.9 9.8 conv_forward.6
  466.3 9.8 conv_forward.7
  482.8 7.9 fusion.38
  490.8 18.9 %multiply_reduce_fusion = (f32[16,3072]{1,0:T(8,128)S(1)}, f32[16,64,3072]{2,1,0:T(8,128)}) fusion(bf16[16,64,1536]{2,1,0:T(8,128)(2,1)} %bitcast.188, bf16[3072,1536]{1,0:T(8,128)(2,1)} %get-tuple-element.98), kind=kOutput, calls=%fused_computation.16 | convolution fusion | flops 9695084544 | bytes 25362432 | tf_op jit(solution)/shard_map/dot_general | solution.py:676
  519.4 8.7 fusion.12
  528.2 15.0 %fusion.39 = (f32[16,1536]{1,0:T(8,128)S(1)}, f32[1024,1536]{1,0:T(8,128)S(1)}) fusion(f32[1024,1536]{1,0:T(8,128)} %get-tuple-element.382, bf16[1024,3072]{1,0:T(8,128)(2,1)} %bitcast.178, bf16[3072,1536]{1,0:T(8,128)(2,1)} %get-tuple-element.98), kind=kOutput, calls=%fused_computation.57 | convolution fusion | flops 9666797568 | bytes 28409856 | tf_op jit(solution)/shard_map/dot_general | solution.py:682
  551.6 16.0 %conv_backward.4 = (bf16[1,1024,768]{2,1,0:T(8,128)(2,1)S(1)}, bf16[768,1152]{1,0:T(8,128)(2,1)}) custom-call(bf16[1024,768]{1,0:T(8,128)(2,1)S(1)} %fusion.55.up_ref, bf16[1,1024,768]{2,1,0:T(8,128)(2,1)S(1)} %bitcast.166, f32[1,1024,768]{2,1,0:T(8,128)} %bitcast.164, bf16[768,1152]{1,0:T(8,128)(2,1)} %copy-done.31), custom_call_target="tpu_custom_call" | custom-call | flops 3623878656 | bytes 7864320 | tf_op jit(solution)/shard_map/conv_backward/pallas_call | solution.py:546
  567.6 16.0 %conv_backward.5 = (bf16[1,1024,768]{2,1,0:T(8,128)(2,1)S(1)}, bf16[768,1152]{1,0:T(8,128)(2,1)}) custom-call(bf16[1024,768]{1,0:T(8,128)(2,1)S(1)} %bitcast.167, bf16[1,1024,768]{2,1,0:T(8,128)(2,1)S(1)} %fusion.80.act_ref, f32[1,1024,768]{2,1,0:T(8,128)} %bitcast.187, bf16[768,1152]{1,0:T(8,128)(2,1)} %copy-done.29), custom_call_target="tpu_custom_call" | custom-call | flops 3623878656 | bytes 7864320 | tf_op jit(solution)/shard_map/conv_backward/pallas_call | solution.py:546
  583.5 12.6 %fusion.41 = (f32[16,1536]{1,0:T(8,128)}, f32[1024,1536]{1,0:T(8,128)}) fusion(f32[1024,1536]{1,0:T(8,128)} %copy-done.51, f32[1024,1536]{1,0:T(8,128)} %copy-done.52, bf16[768,1536]{1,0:T(8,128)(2,1)S(1)} %copy-done.25, bf16[1,1024,768]{2,1,0:T(8,128)(2,1)S(1)} %get-tuple-element.103, f32[1024,1536]{1,0:T(8,128)} %copy-done.49), kind=kOutput, calls=%fused_computation.62 | convolution fusion | flops 2448924672 | bytes 29196288 | tf_op jit(solution)/shard_map/dot_general | solution.py:682
  608.3 6.4 copy.131.m_ref
  633.3 16.1 %conv_backward.6 = (bf16[1,1024,768]{2,1,0:T(8,128)(2,1)S(1)}, bf16[768,1152]{1,0:T(8,128)(2,1)}) custom-call(bf16[1024,768]{1,0:T(8,128)(2,1)S(1)} %fusion.63.up_ref, bf16[1,1024,768]{2,1,0:T(8,128)(2,1)S(1)} %bitcast.163, f32[1,1024,768]{2,1,0:T(8,128)} %bitcast.161, bf16[768,1152]{1,0:T(8,128)(2,1)} %copy-done.28), custom_call_target="tpu_custom_call" | custom-call | flops 3623878656 | bytes 7864320 | tf_op jit(solution)/shard_map/conv_backward/pallas_call | solution.py:546
  649.4 20.6 %conv_backward.7 = (bf16[4,1024,768]{2,1,0:T(8,128)(2,1)}, bf16[768,1152]{1,0:T(8,128)(2,1)S(1)}) custom-call(bf16[1024,768]{1,0:T(8,128)(2,1)S(1)} %bitcast.160, bf16[4,1024,768]{2,1,0:T(8,128)(2,1)} %copy-done.7, f32[4,1024,768]{2,1,0:T(8,128)} %get-tuple-element.374.pre_ref, bf16[768,1152]{1,0:T(8,128)(2,1)S(1)} %copy-done.16), custom_call_target="tpu_custom_call" | custom-call | flops 3623878656 | bytes 26738688 | tf_op jit(solution)/shard_map/conv_backward/pallas_call | solution.py:546
  691.0 14.1 %convolution_convert_fusion.refs_0_ = bf16[3072,1536]{1,0:T(8,128)(2,1)} fusion(bf16[1024,3072]{1,0:T(8,128)(2,1)S(1)} %bitcast.181, bf16[1024,1536]{1,0:T(8,128)(2,1)} %fusion.38), kind=kOutput, calls=%fused_computation.19 | convolution fusion | flops 9668395008 | bytes 18874368 | tf_op jit(solution)/shard_map/dot_general | solution.py:690
  705.1 23.2 %pack_gradients.1 = bf16[24,6400,128]{2,1,0:T(8,128)(2,1)} custom-call(s32[24]{0:T(128)S(1)} %add.407.part_ref, bf16[3072,1536]{1,0:T(8,128)(2,1)} %convolution_convert_fusion.refs_0_, bf16[2304,512]{1,0:T(8,128)(2,1)S(1)} %pad_maximum_fusion.2.refs_1_, bf16[768,1536]{1,0:T(8,128)(2,1)S(1)} %convolution_convert_fusion.3.refs_2_, ...), custom_call_target="tpu_custom_call" | custom-call | bytes 78643200 | tf_op jit(solution)/shard_map/pack_gradients/pallas_call | solution.py:241
  728.3 292.6 %sum_at_owners.1 = bf16[30,2,2,2,160,128]{5,4,3,2,1,0:T(8,128)(2,1)} custom-call(bf16[2,2,30,2,2,2,160,128]{7,6,5,4,3,2,1,0:T(8,128)(2,1)} %bitcast.168), custom_call_target="tpu_custom_call" | custom-call | flops 19660800 | bytes 78643200 | tf_op jit(solution)/shard_map/sum_at_owners/pallas_call | solution.py:392
  1021.0 48.0 %update_packed.1 = (f32[1152,1536]{1,0:T(8,128)}, f32[1152,1536]{1,0:T(8,128)}, f32[1152,1536]{1,0:T(8,128)}, f32[864,512]{1,0:T(8,128)}, f32[864,512]{1,0:T(8,1...) custom-call(s32[1]{0:T(128)} %dynamic_slice.34.share_ref, ...), custom_call_target="tpu_custom_call" | custom-call | flops 145981440 | bytes 131383296 | tf_op jit(solution)/shard_map/update_packed/pallas_call | solution.py:622
  1078.6 12.7 %update.5 = (f32[1152,1000]{1,0:T(8,128)S(1)}, f32[1152,1000]{1,0:T(8,128)}, f32[1152,1000]{1,0:T(8,128)}) custom-call(s32[1]{0:T(128)} %dynamic_slice.34.share_ref, f32[1152,1000]{1,0:T(8,128)} %copy.127.refs_1_.w_ref, f32[1152,1000]{1,0:T(8,128)} %fusion.81.g_ref, f32[1152,1000]{1,0:T(8,128)} %copy.131.m_ref, f32[1152,1000]{1,0:T(8,128)} %copy.132.v_ref), custom_call_target="tpu_custom_call" | custom-call | flops 34560000 | bytes 32256000 | tf_op jit(solution)/shard_map/update/pallas_call | solution.py:660
  1125.4 12.0 %update.4 = (f32[1152,768]{1,0:T(8,128)}, f32[1152,768]{1,0:T(8,128)}, f32[1152,768]{1,0:T(8,128)}) custom-call(s32[1]{0:T(128)} %dynamic_slice.34.share_ref, f32[1152,768]{1,0:T(8,128)S(1)} %bitcast.158, f32[1152,768]{1,0:T(8,128)} %bitcast.175, f32[1152,768]{1,0:T(8,128)} %bitcast.183, f32[1152,768]{1,0:T(8,128)} %bitcast.184), custom_call_target="tpu_custom_call" | custom-call | flops 26542080 | bytes 24772608 | tf_op jit(solution)/shard_map/update/pallas_call | solution.py:660
  1137.4 11.6 %update.3 = (f32[576,1536]{1,0:T(8,128)}, f32[576,1536]{1,0:T(8,128)}, f32[576,1536]{1,0:T(8,128)}) custom-call(s32[1]{0:T(128)} %dynamic_slice.34.share_ref, f32[576,1536]{1,0:T(8,128)S(1)} %bitcast.159, f32[576,1536]{1,0:T(8,128)} %bitcast.174, f32[576,1536]{1,0:T(8,128)} %bitcast.185, f32[576,1536]{1,0:T(8,128)} %bitcast.186), custom_call_target="tpu_custom_call" | custom-call | flops 26542080 | bytes 24772608 | tf_op jit(solution)/shard_map/update/pallas_call | solution.py:660
  (318 shorter events, 206.4 us)
Async XLA Ops:
  24.5 56.9 %collective-permute-start.3 = (bf16[3,3168,128]{2,1,0:T(8,128)(2,1)}, bf16[3,3168,128]{2,1,0:T(8,128)(2,1)}, u32[]{:S(2)}, u32[]{:S(2)}) collective-permute-start(bf16[3,3168,128]{2,1,0:T(8,128)(2,1)} %constant_dynamic-slice_fusion.1), channel_id=1, source_target_pairs={{0,16},{8,24},{16,0},{24,8},{1,17},{9,25},{17,1},{25,9},{2,18},{10... | collective-permute-start | bytes 7299080 | tf_op jit(solution)/shard_map/ppermute | solution.py:201
  27.5 222.8 %collective-permute-start.5 = (bf16[6,3168,128]{2,1,0:T(8,128)(2,1)}, bf16[6,3168,128]{2,1,0:T(8,128)(2,1)}, u32[]{:S(2)}, u32[]{:S(2)}) collective-permute-start(bf16[6,3168,128]{2,1,0:T(8,128)(2,1)} %pack_weights.4.refs_6_), channel_id=1, source_target_pairs={{0,8},{8,0},{16,24},{24,16},{1,9},{9,1},{17,25},{25,17},{2,10},{10... | collective-permute-start | bytes 14598152 | tf_op jit(solution)/shard_map/ppermute | solution.py:206
  33.9 216.4 %collective-permute-start = (bf16[6,3168,128]{2,1,0:T(8,128)(2,1)}, bf16[6,3168,128]{2,1,0:T(8,128)(2,1)}, u32[]{:S(2)}, u32[]{:S(2)}) collective-permute-start(bf16[6,3168,128]{2,1,0:T(8,128)(2,1)} %pack_weights.3.refs_4_), channel_id=1, source_target_pairs={{0,16},{8,24},{16,0},{24,8},{1,17},{9,25},{17,1},{25,9},{2,18},{10... | collective-permute-start | bytes 14598152 | tf_op jit(solution)/shard_map/ppermute | solution.py:205
  52.2 195.7 %collective-permute-start.8 = (bf16[3,3840,128]{2,1,0:T(8,128)(2,1)}, bf16[3,3840,128]{2,1,0:T(8,128)(2,1)S(1)}, u32[]{:S(2)}, u32[]{:S(2)}) collective-permute-start(bf16[3,3840,128]{2,1,0:T(8,128)(2,1)} %constant_dynamic-slice_fusion), channel_id=1, source_target_pairs={{0,16},{8,24},{16,0},{24,8},{1,17},{9,25},{17,1},{25,9},{2,18},{10... | collective-permute-start | bytes 8847368 | tf_op jit(solution)/shard_map/ppermute | solution.py:201
  54.2 196.5 %copy-start.69 = (f32[1002]{0:T(1024)S(1)}, f32[1002]{0:T(1024)}, u32[]{:S(2)}) copy-start(f32[1002]{0:T(1024)} %param.59) | copy-start | bytes 12028
  54.2 199.8 %copy-start.82 = (s32[2,64]{1,0:T(2,128)S(1)}, s32[2,64]{1,0:T(2,128)}, u32[]{:S(2)}) copy-start(s32[2,64]{1,0:T(2,128)} %param.32) | copy-start | bytes 1540
  54.2 200.0 %copy-start.79 = (s32[4]{0:T(128)S(1)}, s32[4]{0:T(128)}, u32[]{:S(2)}) copy-start(s32[4]{0:T(128)} %param.34) | copy-start | bytes 52
  54.2 259.9 %copy-start.73 = (s32[1000]{0:T(1024)S(1)}, s32[1000]{0:T(1024)}, u32[]{:S(2)}) copy-start(s32[1000]{0:T(1024)} %param.33) | copy-start | bytes 12004
  54.2 279.8 %all-to-all-start = ((bf16[8,16,4,8,512]{4,3,2,1,0:T(8,128)(2,1)}), bf16[8,16,4,8,512]{4,3,2,1,0:T(8,128)(2,1)}, u32[]{:S(2)}, u32[]{:S(2)}) async-start(bf16[8,16,4,8,512]{4,3,2,1,0:T(8,128)(2,1)} %bitcast.182), calls=%async_computation | async-start | bytes 8388608 | tf_op jit(solution)/shard_map/all_to_all | solution.py:763
  60.2 1008.9 %all-reduce.5.cloned.1.call-start = ((), (), s32[]{:S(2)}) async-start(), calls=%async_computation.4 | async-start | bytes 262144
  81.4 168.3 %collective-permute-start.6 = (bf16[3,3168,128]{2,1,0:T(8,128)(2,1)}, bf16[3,3168,128]{2,1,0:T(8,128)(2,1)}, u32[]{:S(2)}, u32[]{:S(2)}) collective-permute-start(bf16[3,3168,128]{2,1,0:T(8,128)(2,1)} %collective-permute-done.3.refs_7_), channel_id=1, source_target_pairs={{0,8},{8,0},{16,24},{24,16},{1,9},{9,1},{17,25},{25,17},{2,10},{10... | collective-permute-start | bytes 7299080 | tf_op jit(solution)/shard_map/ppermute | solution.py:206
  81.4 168.3 %collective-permute-start.4 = (bf16[3,3168,128]{2,1,0:T(8,128)(2,1)}, bf16[3,3168,128]{2,1,0:T(8,128)(2,1)}, u32[]{:S(2)}, u32[]{:S(2)}) collective-permute-start(bf16[3,3168,128]{2,1,0:T(8,128)(2,1)} %collective-permute-done.3.refs_7_), channel_id=1, source_target_pairs={{0,1},{1,0},{2,3},{3,2},{4,5},{5,4},{6,7},{7,6},{8,9},{9,8},{10,11... | collective-permute-start | bytes 7299080 | tf_op jit(solution)/shard_map/ppermute | solution.py:202
  248.0 65.2 %collective-permute-start.9 = (bf16[3,3840,128]{2,1,0:T(8,128)(2,1)S(1)}, bf16[3,3840,128]{2,1,0:T(8,128)(2,1)}, u32[]{:S(2)}, u32[]{:S(2)}) collective-permute-start(bf16[3,3840,128]{2,1,0:T(8,128)(2,1)S(1)} %collective-permute-done.8.refs_7_), channel_id=1, source_target_pairs={{0,1},{1,0},{2,3},{3,2},{4,5},{5,4},{6,7},{7,6},{8,9},{9,8},{10,11... | collective-permute-start | bytes 8847368 | tf_op jit(solution)/shard_map/ppermute | solution.py:202
  249.7 121.2 %collective-permute-start.10 = (bf16[6,3840,128]{2,1,0:T(8,128)(2,1)}, bf16[6,3840,128]{2,1,0:T(8,128)(2,1)}, u32[]{:S(2)}, u32[]{:S(2)}) collective-permute-start(bf16[6,3840,128]{2,1,0:T(8,128)(2,1)} %copy-done.1), channel_id=1, source_target_pairs={{0,8},{8,0},{16,24},{24,16},{1,9},{9,1},{17,25},{25,17},{2,10},{10... | collective-permute-start | bytes 17694728 | tf_op jit(solution)/shard_map/ppermute | solution.py:206
  249.8 63.4 %collective-permute-start.7 = (bf16[3,3168,128]{2,1,0:T(8,128)(2,1)}, bf16[3,3168,128]{2,1,0:T(8,128)(2,1)}, u32[]{:S(2)}, u32[]{:S(2)}) collective-permute-start(bf16[3,3168,128]{2,1,0:T(8,128)(2,1)} %collective-permute-done.4.refs_8_), channel_id=1, source_target_pairs={{0,8},{8,0},{16,24},{24,16},{1,9},{9,1},{17,25},{25,17},{2,10},{10... | collective-permute-start | bytes 7299080 | tf_op jit(solution)/shard_map/ppermute | solution.py:206
  250.3 137.8 %collective-permute-start.1 = (bf16[6,3168,128]{2,1,0:T(8,128)(2,1)}, bf16[6,3168,128]{2,1,0:T(8,128)(2,1)}, u32[]{:S(2)}, u32[]{:S(2)}) collective-permute-start(bf16[6,3168,128]{2,1,0:T(8,128)(2,1)} %pack_weights.3.refs_4_), channel_id=1, source_target_pairs={{0,8},{8,0},{16,24},{24,16},{1,9},{9,1},{17,25},{25,17},{2,10},{10... | collective-permute-start | bytes 14598152 | tf_op jit(solution)/shard_map/ppermute | solution.py:206
  250.3 137.7 %collective-permute-start.2 = (bf16[6,3168,128]{2,1,0:T(8,128)(2,1)}, bf16[6,3168,128]{2,1,0:T(8,128)(2,1)}, u32[]{:S(2)}, u32[]{:S(2)}) collective-permute-start(bf16[6,3168,128]{2,1,0:T(8,128)(2,1)} %collective-permute-done.refs_5_), channel_id=1, source_target_pairs={{0,8},{8,0},{16,24},{24,16},{1,9},{9,1},{17,25},{25,17},{2,10},{10... | collective-permute-start | bytes 14598152 | tf_op jit(solution)/shard_map/ppermute | solution.py:206
  254.3 71.7 %copy-start.74 = (s32[4]{0:T(128)}, s32[4]{0:T(128)S(1)}, u32[]{:S(2)}) copy-start(s32[4]{0:T(128)S(1)} %select_reduce_fusion.13) | copy-start | bytes 52
  313.2 57.8 %collective-permute-start.11 = (bf16[3,3840,128]{2,1,0:T(8,128)(2,1)S(1)}, bf16[3,3840,128]{2,1,0:T(8,128)(2,1)}, u32[]{:S(2)}, u32[]{:S(2)}) collective-permute-start(bf16[3,3840,128]{2,1,0:T(8,128)(2,1)S(1)} %collective-permute-done.8.refs_7_), channel_id=1, source_target_pairs={{0,8},{8,0},{16,24},{24,16},{1,9},{9,1},{17,25},{25,17},{2,10},{10... | collective-permute-start | bytes 8847368 | tf_op jit(solution)/shard_map/ppermute | solution.py:206
  313.2 57.8 %collective-permute-start.12 = (bf16[3,3840,128]{2,1,0:T(8,128)(2,1)}, bf16[3,3840,128]{2,1,0:T(8,128)(2,1)}, u32[]{:S(2)}, u32[]{:S(2)}) collective-permute-start(bf16[3,3840,128]{2,1,0:T(8,128)(2,1)} %collective-permute-done.9.refs_8_), channel_id=1, source_target_pairs={{0,8},{8,0},{16,24},{24,16},{1,9},{9,1},{17,25},{25,17},{2,10},{10... | collective-permute-start | bytes 8847368 | tf_op jit(solution)/shard_map/ppermute | solution.py:206
  399.1 29.2 %copy-start.28 = (bf16[768,1152]{1,0:T(8,128)(2,1)}, bf16[768,1152]{1,0:T(8,128)(2,1)S(1)}, u32[]{:S(2)}) copy-start(bf16[768,1152]{1,0:T(8,128)(2,1)S(1)} %get-tuple-element.85.w_ref) | copy-start | bytes 5308420
  399.1 39.0 %copy-start.22 = (bf16[1536,768]{1,0:T(8,128)(2,1)}, bf16[1536,768]{1,0:T(8,128)(2,1)S(1)}, u32[]{:S(2)}) copy-start(bf16[1536,768]{1,0:T(8,128)(2,1)S(1)} %get-tuple-element.87) | copy-start | bytes 7077892
  399.2 43.1 %copy-start.8 = (bf16[1536,768]{1,0:T(8,128)(2,1)}, bf16[1536,768]{1,0:T(8,128)(2,1)S(1)}, u32[]{:S(2)}) copy-start(bf16[1536,768]{1,0:T(8,128)(2,1)S(1)} %get-tuple-element.89) | copy-start | bytes 7077892
  583.5 24.6 %copy-start.76 = (s32[4]{0:T(128)S(1)}, s32[4]{0:T(128)}, u32[]{:S(2)}) copy-start(s32[4]{0:T(128)} %get-tuple-element.361) | copy-start | bytes 52
  602.5 468.9 %all-gather.9.cloned.1.call-start = ((), (), s32[]{:S(2)}) async-start(), calls=%async_computation.3 | async-start | bytes 4325376 | tf_op jit(solution)/shard_map/all_gather | solution.py:845
  603.2 508.4 %all-gather.7.cloned.1.call-start = ((), (), s32[]{:S(2)}) async-start(), calls=%async_computation.2 | async-start | bytes 4866048 | tf_op jit(solution)/shard_map/all_gather | solution.py:864
  604.8 508.0 %all-gather.5.cloned.1.call-start = ((), (), s32[]{:S(2)}) async-start(), calls=%async_computation.1 | async-start | bytes 4866048 | tf_op jit(solution)/shard_map/all_gather | solution.py:864
  633.3 41.6 %slice-start.2 = ((s8[8388608]{0:T(1024)(128)(4,1)}), s8[4194304]{0:T(1024)(128)(4,1)S(1)}, s32[]{:S(2)}) async-start(s8[8388608]{0:T(1024)(128)(4,1)} %bitcast.176), calls=%async_computation.7 | async-start | bytes 8388608
  649.4 25.5 %slice-start.3 = ((s8[8388608]{0:T(1024)(128)(4,1)}), s8[4194304]{0:T(1024)(128)(4,1)S(1)}, s32[]{:S(2)}) async-start(s8[8388608]{0:T(1024)(128)(4,1)} %bitcast.176), calls=%async_computation.8 | async-start | bytes 8388608
  1021.0 49.7 %copy-start.70 = (f32[1002]{0:T(1024)S(1)}, f32[1002]{0:T(1024)}, u32[]{:S(2)}) copy-start(f32[1002]{0:T(1024)} %param.59) | copy-start | bytes 12028
  1021.0 49.7 %copy-start.71 = (f32[1002]{0:T(1024)S(1)}, f32[1002]{0:T(1024)}, u32[]{:S(2)}) copy-start(f32[1002]{0:T(1024)} %param.61) | copy-start | bytes 12028
  1021.0 49.7 %copy-start.72 = (f32[1002]{0:T(1024)S(1)}, f32[1002]{0:T(1024)}, u32[]{:S(2)}) copy-start(f32[1002]{0:T(1024)} %param.60) | copy-start | bytes 12028
  (81 other events, 465.9 us)
Sparse Core Ops, SparseCore 0:
  602.6 123.7 all-reduce.4
  729.5 71.9 all-gather.8
  804.4 83.8 all-gather.6
  891.1 78.9 all-gather.4

commit v2 on v1

--- a/solution.py
+++ b/solution.py
@@ -32,6 +32,8 @@
 
 TAPS_ONE = tuple((0, t // 3 - 1, t % 3 - 1) for t in range(9))
 TAPS_TWO = tuple(((t // 3 % 2) * 2 + t % 3 % 2, t // 3 // 2, t % 3 // 2) for t in range(9))
+
+CHUNK = 16
 
 f32 = jnp.float32
 bf16 = jnp.bfloat16
@@ -153,71 +155,101 @@
     )(*[e[0] for e in entries])
 
 
-def unpack_kernel(counts, shapes, which_ref, *refs):
-    sources = refs[counts : counts + counts]
-    outs = refs[2 * counts :]
-    for s, source in enumerate(sources):
-
-        @pl.when(which_ref[pl.program_id(0)] == s)
-        def _(source=source):
-            at = 0
-            for out, (part, width) in zip(outs, shapes):
-                block, at = read_packed(source, at, part, width)
-                out[...] = block
-
-
-def unpack_weights(sources, which, places, shapes):
+def unpack_kernel(count, shapes, which_ref, place_ref, *refs):
+    sources = refs[:count]
+    outs = refs[count : count + len(shapes)]
+    held, *rest = refs[count + len(shapes) :]
+    stages, (arrived, left) = rest[: len(shapes)], rest[len(shapes) :]
+    parts = which_ref.shape[0]
+
+    def fetch(i, carry):
+        for s, source in enumerate(sources):
+
+            @pl.when(which_ref[i] == s)
+            def _(source=source):
+                pltpu.make_async_copy(source.at[place_ref[i]], held.at[i], arrived.at[i]).start()
+
+        return carry
+
+    def spread(i, carry):
+        pltpu.make_async_copy(held.at[i], held.at[i], arrived.at[i]).wait()
+        at = 0
+        for k, (part, width) in enumerate(shapes):
+            rows = pl.ds(pl.multiple_of(i * part, part), part)
+            block, at = read_packed(held.at[i], at, part, width)
+            stages[k][rows, :] = block
+            pltpu.make_async_copy(stages[k].at[rows, :], outs[k].at[rows, :], left.at[k]).start()
+        return carry
+
+    lax.fori_loop(0, parts, fetch, 0)
+    lax.fori_loop(0, parts, spread, 0)
+    for k in range(len(shapes)):
+        pltpu.make_async_copy(stages[k], outs[k], left.at[k]).wait()
+
+
+def unpack_weights(sources, which, place, shapes):
     count, parts = len(sources), which.shape[0]
     rows = sources[0].shape[1]
-    grid_spec = pltpu.PrefetchScalarGridSpec(
-        num_scalar_prefetch=1 + count,
-        grid=(parts,),
-        in_specs=[
-            pl.BlockSpec((None, rows, 128), lambda i, *tables, s=s: (tables[1 + s][i], 0, 0))
-            for s in range(count)
-        ],
-        out_specs=[pl.BlockSpec((p, w), lambda i, *tables: (i, 0)) for p, w in shapes],
-    )
+    full = [(parts * p, w) for p, w in shapes]
     return pl.pallas_call(
         functools.partial(unpack_kernel, count, shapes),
-        grid_spec=grid_spec,
-        out_shape=[jax.ShapeDtypeStruct((parts * p, w), bf16) for p, w in shapes],
+        out_shape=[jax.ShapeDtypeStruct(f, bf16) for f in full],
+        in_specs=[pl.BlockSpec(memory_space=pltpu.SMEM)] * 2
+        + [pl.BlockSpec(memory_space=pl.ANY)] * count,
+        out_specs=[pl.BlockSpec(memory_space=pl.ANY)] * len(shapes),
+        scratch_shapes=[pltpu.VMEM((parts, rows, 128), bf16)]
+        + [pltpu.VMEM(f, bf16) for f in full]
+        + [pltpu.SemaphoreType.DMA((parts,)), pltpu.SemaphoreType.DMA((len(shapes),))],
         compiler_params=pltpu.CompilerParams(vmem_limit_bytes=40 * MIB),
         cost_estimate=pl.CostEstimate(
             flops=0, bytes_accessed=parts * rows * 128 * 4, transcendentals=0
         ),
         name="unpack_weights",
-    )(which, *places, *sources)
-
-
-def gather_packed(packed, halves, owner, local):
+    )(which, place, *sources)
+
+
+def after(value, *others):
+    return lax.optimization_barrier((value,) + others)[0]
+
+
+CHIP = [(i, i ^ 2) for i in range(4)]
+CORE = [(i, i ^ 1) for i in range(4)]
+
+
+class Gather:
+    def __init__(self, entries, whole=False):
+        self.shapes = tuple((e[0].shape[-2] // 6, e[0].shape[-1]) for e in entries)
+        self.own = pack_weights(entries)
+        self.whole = whole
+
+    def along_x(self, *others):
+        mine = self.own
+        if not self.whole:
+            mine = lax.dynamic_slice_in_dim(mine, lax.axis_index("wa") * 3, 3, 0)
+        self.near = lax.ppermute(after(mine, *others), "dp", CHIP)
+
+    def along_y(self):
+        self.far = lax.ppermute(self.near, "wa", [(0, 1), (1, 0)])
+
+    def cores(self):
+        buffers = [self.own, self.near] + ([] if self.whole else [self.far])
+        self.buffers = buffers + [lax.ppermute(b, "dp", CORE) for b in buffers]
+
+    def unpacked(self, tables):
+        return unpack_weights(self.buffers, *tables[self.whole], self.shapes)
+
+
+def source_tables(owner, local, whole):
     me = lax.axis_index("dp")
-    chip = [(i, i ^ 2) for i in range(4)]
-    core = [(i, i ^ 1) for i in range(4)]
-    buffers = [packed]
-    if halves:
-        side = lax.axis_index("wa")
-        mine = lax.dynamic_slice_in_dim(packed, side * 3, 3, 0)
-        near = lax.ppermute(mine, "dp", chip)
-        far = lax.ppermute(near, "wa", [(0, 1), (1, 0)])
-        buffers += [near, far]
+    side = lax.axis_index("wa")
+    away = owner // 2 != me // 2
+    if whole:
+        which, at, count = away.astype(jnp.int32), local, 2
     else:
-        buffers += [lax.ppermute(packed, "dp", chip)]
-    buffers += [lax.ppermute(b, "dp", core) for b in buffers]
-    half = len(buffers) // 2
-    apart = (owner // 2 != me // 2).astype(jnp.int32)
-    if halves:
-        which = jnp.where(apart == 1, jnp.where(local // 3 == side, 1, 2), 0)
-        at = jnp.where(apart == 1, local % 3, local)
-    else:
-        which, at = apart, local
-    which = (which + half * (owner % 2 != me % 2)).astype(jnp.int32)
-    places = []
-    parts = jnp.arange(owner.shape[0])
-    for s in range(len(buffers)):
-        found = jnp.where((which[None, :] == s) & (parts[None, :] <= parts[:, None]), at[None, :], 0)
-        places.append(jnp.max(found, axis=1).astype(jnp.int32))
-    return buffers, which, places
+        which = jnp.where(away, jnp.where(local // 3 == side, 1, 2), 0)
+        at, count = jnp.where(away, local % 3, local), 3
+    which = (which + count * (owner % 2 != me % 2)).astype(jnp.int32)
+    return which, at.astype(jnp.int32)
 
 
 def pack_gradients_kernel(pad, part_ref, *refs):
@@ -255,8 +287,10 @@
     )(slot_part, *gradients)
 
 
-SPAN = 1280
+SPAN = 1024
 AXES = ("x", "y", "near", "far")
+ORDERS = (AXES,)
+LAGS = (0, 1, 2, 3, 4, 5, 6, 7)
 
 
 def sum_kernel(orders, spans, packed, owned, own, core, one, two, three, four, sends, recvs, local_sems):
@@ -349,7 +383,7 @@
         copy_of(0, chunk % kinds, chunk).start()
     load(0).start()
 
-    def step(s, q, first=False):
+    def step(s, q):
         @pl.when(s + ahead < spans)
         def _():
             copy_of(0, (q + ahead) % kinds, s + ahead).start()
@@ -359,8 +393,8 @@
             load(s + 1).start()
 
         for stage in range(last + 1):
-            chunk = s - stage
-            kind = (q - stage) % kinds
+            chunk = s - LAGS[stage]
+            kind = (q - LAGS[stage]) % kinds
 
             @pl.when((chunk >= 0) & (chunk < spans))
             def _(stage=stage, chunk=chunk, kind=kind):
@@ -373,7 +407,7 @@
             step(i * kinds + q, q)
         return carry
 
-    lax.fori_loop(0, -(-(spans + last) // kinds), steps, 0)
+    lax.fori_loop(0, -(-(spans + LAGS[-1]) // kinds), steps, 0)
 
     def sent(i, carry):
         for q in range(kinds):
@@ -388,7 +422,7 @@
     slots, rows, lanes = packed.shape
     spans = 6 * rows // SPAN
     r = SPAN // 8
-    orders = (AXES,)
+    orders = ORDERS
     owned = pl.pallas_call(
         functools.partial(sum_kernel, orders, spans),
         out_shape=jax.ShapeDtypeStruct((spans, 2, 2, 2, r, 128), bf16),
@@ -416,6 +450,48 @@
     return owned.reshape(6, rows, lanes)
 
 
+def prepare_kernel(tiles_ref, place_ref, act_ref, pooled_ref):
+    sources, tile_h, tile_w, width = tiles_ref.shape
+    pixels = tiles_ref[...].astype(f32).reshape(sources * tile_h * tile_w, width).astype(bf16)
+    image = jnp.dot(place_ref[...], pixels, preferred_element_type=f32)
+    act = (gelu_act(image) * GAMMA).astype(bf16).reshape(4, CELLS, width)
+    act_ref[...] = act
+    total = act[0].astype(f32) + act[1].astype(f32) + act[2].astype(f32) + act[3].astype(f32)
+    pooled_ref[...] = (total * 0.25).astype(bf16)
+
+
+def prepare(tiles, rows_n, cols_n):
+    sources, count, tile_h, tile_w, width = tiles.shape
+    pixels = 4 * CELLS
+    down = jnp.arange(sources)[:, None, None] // cols_n * tile_h + jnp.arange(tile_h)[None, :, None]
+    along = jnp.arange(sources)[:, None, None] % cols_n * tile_w + jnp.arange(tile_w)[None, None, :]
+    target = ((down % 2 * 2 + along % 2) * HEIGHT + down // 2) * BREADTH + along // 2
+    place = (jnp.arange(pixels)[:, None] == target.reshape(1, pixels)).astype(bf16)
+    return pl.pallas_call(
+        prepare_kernel,
+        grid=(count,),
+        out_shape=[
+            jax.ShapeDtypeStruct((4, count * CELLS, width), bf16),
+            jax.ShapeDtypeStruct((count * CELLS, width), bf16),
+        ],
+        in_specs=[
+            pl.BlockSpec((sources, None, tile_h, tile_w, width), lambda n: (0, n, 0, 0, 0)),
+            pl.BlockSpec((pixels, pixels), lambda n: (0, 0)),
+        ],
+        out_specs=[
+            pl.BlockSpec((4, CELLS, width), lambda n: (0, n, 0)),
+            pl.BlockSpec((CELLS, width), lambda n: (n, 0)),
+        ],
+        compiler_params=pltpu.CompilerParams(vmem_limit_bytes=32 * MIB),
+        cost_estimate=pl.CostEstimate(
+            flops=2 * count * pixels * pixels * width,
+            bytes_accessed=5 * count * pixels * width,
+            transcendentals=count * pixels * width,
+        ),
+        name="prepare",
+    )(tiles, place)
+
+
 def moved(image, down, right):
     if right:
         column = lax.broadcasted_iota(jnp.int32, image.shape, 1) + right
@@ -467,7 +543,7 @@
 
 def conv_forward(act, weight, taps):
     phases, cells, channels = act.shape
-    chunk = 4
+    chunk = min(CHUNK, cells // CELLS)
     return pl.pallas_call(
         functools.partial(conv_kernel, taps, chunk),
         grid=(channels // GROUP,),
@@ -542,7 +618,7 @@
 
 def conv_backward(up, act, pre, weight, taps):
     phases, cells, channels = act.shape
-    chunk = 4
+    chunk = min(CHUNK, cells // CELLS)
     return pl.pallas_call(
         functools.partial(conv_back_kernel, taps, chunk),
         grid=(channels // GROUP,),
@@ -590,9 +666,9 @@
         g = g * (ceiling / jnp.maximum(norm, ceiling))
     m = DECAY_ONE * m + (1.0 - DECAY_ONE) * g
     v = DECAY_TWO * v + (1.0 - DECAY_TWO) * g * g
-    m_hat = m * (1.0 / (1.0 - DECAY_ONE**STEP_COUNT))
-    v_hat = v * (1.0 / (1.0 - DECAY_TWO**STEP_COUNT))
-    return m, v, w - RATE * (m_hat / (jnp.sqrt(v_hat) + ADAM_EPS) + WEIGHT_DECAY * w)
+    root = v * lax.rsqrt(v) * (1.0 - DECAY_TWO**STEP_COUNT) ** -0.5 + ADAM_EPS
+    step = (RATE / (1.0 - DECAY_ONE**STEP_COUNT)) * m * pl.reciprocal(root)
+    return m, v, (1.0 - RATE * WEIGHT_DECAY) * w - step
 
 
 def update_packed_kernel(shapes, share_ref, packed_ref, *refs):
@@ -638,6 +714,57 @@
     return [tuple(outs[3 * k : 3 * k + 3]) for k in range(len(members))]
 
 
+def update_factors_kernel(unit, turned, block, share_ref, units_ref, inputs_ref, w_ref, m_ref, v_ref, m_out, v_out, w_out, g_all):
+    step = pl.program_id(1)
+
+    @pl.when(step == 0)
+    def _():
+        left, right = (inputs_ref, units_ref) if turned else (units_ref, inputs_ref)
+        g_all[...] = lax.dot_general(
+            left[...], right[...], (((0,), (0,)), ((), ())), preferred_element_type=f32
+        )
+
+    rows = pl.ds(pl.multiple_of(step * block, 8), block)
+    shape = w_ref.shape
+    index = lax.broadcasted_iota(jnp.int32, shape if turned else (block, 1), 1 if turned else 0)
+    index += 0 if turned else step * block
+    g = jnp.where(index < share_ref[0] * unit, g_all[rows, :], 0.0)
+    m_out[...], v_out[...], w_out[...] = new_values(
+        w_ref[...], g, m_ref[...], v_ref[...], False, not turned
+    )
+
+
+def update_factors(weight, units, gathered, columns, first, second, share, turned=False):
+    count, rows, width = weight.shape
+    images = units.shape[1]
+    start, across, stride = columns
+    block = 504 if turned else rows
+    steps = -(-rows // block)
+    spec = pl.BlockSpec((None, block, width), lambda k, i: (k, i, 0))
+    owned = (width if turned else rows) // 6
+    made = (across, width) if turned else (rows, across)
+    return pl.pallas_call(
+        functools.partial(update_factors_kernel, owned, turned, block),
+        grid=(count, steps),
+        out_shape=[jax.ShapeDtypeStruct(weight.shape, f32)] * 3,
+        in_specs=[
+            pl.BlockSpec(memory_space=pltpu.SMEM),
+            pl.BlockSpec((None, images, units.shape[2]), lambda k, i: (k, 0, 0)),
+            pl.BlockSpec((images, across), lambda k, i: (0, start + stride * k)),
+        ]
+        + [spec] * 3,
+        out_specs=[spec] * 3,
+        scratch_shapes=[pltpu.VMEM(made, f32)],
+        compiler_params=pltpu.CompilerParams(vmem_limit_bytes=56 * MIB),
+        cost_estimate=pl.CostEstimate(
+            flops=count * rows * width * (2 * images + 15),
+            bytes_accessed=24 * count * rows * width,
+            transcendentals=count * rows * width,
+        ),
+        name="update_factors",
+    )(share, units, gathered, weight, first, second)
+
+
 def update_kernel(unit, standard, clip, block, share_ref, w_ref, g_ref, m_ref, v_ref, m_out, v_out, w_out):
     row = pl.program_id(0) * block + lax.broadcasted_iota(jnp.int32, (block, 1), 0)
     g = jnp.where(row % (6 * unit) < share_ref[0] * unit, g_ref[...].astype(f32), 0.0)
@@ -672,6 +799,22 @@
     return tuple(o.reshape(shape) for o in outs)
 
 
+def split_small(values, rows):
+    values = jnp.pad(values, (0, -values.shape[0] % (128 * rows))).reshape(rows, -1)
+    terms = []
+    for _ in range(3):
+        term = lax.reduce_precision(values, 8, 7)
+        terms.append(term.astype(bf16))
+        values = values - term
+    return terms
+
+
+def join_small(terms, rows):
+    width = terms.shape[1] // 3
+    total = jnp.sum(terms.astype(f32).reshape(-1, rows, 3 * width), axis=0)
+    return (total[:, :width] + total[:, width : 2 * width] + total[:, 2 * width :]).reshape(-1)
+
+
 def dot_t(left, right):
     return lax.dot_general(
         left, right, (((left.ndim - 1,), (1,)), ((), ())), preferred_element_type=f32
@@ -712,7 +855,7 @@
     grad_four = (
         grad_hidden * (ALPHA * gain * gate)[:, None, :] + (grad_squeezed / CELLS)[:, None, :]
     ).astype(bf16)
-    factors = jnp.concatenate([grad_up, act_down, grad_down, squeezed], axis=1)
+    factors = [grad_up, act_down, grad_down, squeezed]
     return grad_four.reshape(-1, grad_four.shape[-1]), factors, gain_part
 
 
@@ -761,25 +904,11 @@
     count = micro * per_dp // spread
     tiles = images.reshape(spread, count, tile_h, tile_w, in_width)
     tiles = lax.all_to_all(tiles, ("ha", "wa"), 0, 0, tiled=True)
-    tiles = tiles.reshape(
-        rows_n, cols_n, count, tile_h // 2, 2, tile_w // 2, 2, in_width
-    ).transpose(4, 6, 2, 0, 3, 1, 5, 7)
-    cells = count * CELLS
-    pixels = tiles.reshape(4, cells, in_width)
     spot = lax.axis_index("ha") * cols_n + lax.axis_index("wa")
     my_labels = lax.dynamic_slice_in_dim(labels.reshape(-1), spot * count, count, 0)
 
-    def gather(entries, halves):
-        if not known_mesh():
-            return gather_plain(entries, owner, local)
-        shapes = tuple((e[0].shape[-2] // 6, e[0].shape[-1]) for e in entries)
-        buffers, which, places = gather_packed(pack_weights(entries), halves, owner, local)
-        return unpack_weights(buffers, which, places, shapes)
-
     def block_entries(layer):
-        first = (w_entry, (), True) if layer == 0 else (w_in, (layer - 1,), True)
         return [
-            first,
             (w_mid, (layer, 0), True),
             (w_mid, (layer, 1), True),
             (w_out, (layer,), True),
@@ -787,16 +916,49 @@
             (se_up, (layer,), False),
         ]
 
-    in_low, mid_low, out_low, down_low, up_low = ([None] * LAYERS for _ in range(5))
-    for layer in range(LAYERS):
-        in_low[layer], mid_a, mid_b, out_low[layer], down_low[layer], up_low[layer] = gather(
-            block_entries(layer), layer > 0
-        )
-        mid_low[layer] = (mid_a, mid_b)
-    final_low, head_low = gather([(w_final, (), True), (head, (), False)], True)
-    entry_low = in_low[0]
-    in_low[0] = entry_low[:NECK]
-    skip_low = entry_low[NECK:]
+    groups = [
+        [(w_entry, (), True)],
+        block_entries(0),
+        [(w_in, (0,), True)] + block_entries(1),
+        [(w_final, (), True)],
+        [(head, (), False)],
+    ]
+    staged = known_mesh()
+    if staged:
+        tables = {flag: source_tables(owner, local, flag) for flag in (True, False)}
+        moves = [Gather(groups[0], True), Gather(groups[1])]
+        moves[0].along_x()
+        moves[1].along_x(moves[0].near)
+        moves[0].cores()
+        for entries in groups[2:]:
+            entries[0] = (after(entries[0][0], moves[0].near),) + entries[0][1:]
+            moves.append(Gather(entries))
+        moves[1].near = after(moves[1].near, *[m.own for m in moves[2:]])
+        moves[1].along_y()
+        moves[2].along_x(moves[1].near)
+    cells = count * CELLS
+    if staged:
+        act_zero, pooled = prepare(tiles, rows_n, cols_n)
+    else:
+        pixels = tiles.reshape(
+            rows_n, cols_n, count, tile_h // 2, 2, tile_w // 2, 2, in_width
+        ).transpose(4, 6, 2, 0, 3, 1, 5, 7).reshape(4, cells, in_width)
+        act_zero = (gelu_act(pixels.astype(f32)) * GAMMA).astype(bf16)
+        pooled = (jnp.sum(act_zero.astype(f32), axis=0) * 0.25).astype(bf16)
+
+    def hold(value, *arrivals):
+        if not staged:
+            return value
+        kept = [getattr(moves[k], name) for k, name in arrivals]
+        value, *kept = lax.optimization_barrier((value, *kept))
+        for (k, name), buffer in zip(arrivals, kept):
+            setattr(moves[k], name, buffer)
+        return value
+
+    def weights_of(group):
+        if staged:
+            return moves[group].unpacked(tables)
+        return gather_plain(groups[group], owner, local)
 
     gains = small_params[:LAYERS]
     head_bias = small_params[LAYERS:]
@@ -804,33 +966,61 @@
     class_weight = 1.0 / class_counts.astype(f32)
 
     kept = []
+    weights = []
     hidden = None
     for layer in range(LAYERS):
-        scale = GAMMA * (1.0 + layer * ALPHA * ALPHA) ** (-0.5)
-        source = pixels.astype(f32) if layer == 0 else hidden
-        act_zero = (gelu_act(source) * scale).astype(bf16)
         if layer:
-            act_zero = act_zero.reshape(1, cells, -1)
+            scale = GAMMA * (1.0 + layer * ALPHA * ALPHA) ** (-0.5)
+            act_zero = (gelu_act(hidden) * scale).astype(bf16).reshape(1, cells, -1)
         taps = TAPS_TWO if layer == 0 else TAPS_ONE
-        pre_one = dot_t(act_zero, in_low[layer])
+        if layer == 0:
+            (entry_low,) = weights_of(0)
+            in_low, skip_low = entry_low[:NECK], entry_low[NECK:]
+        else:
+            in_low, *others = weights_of(1 + layer)
+        pre_one = dot_t(act_zero, in_low)
         act_one = (gelu_act(pre_one) * GAMMA).astype(bf16)
-        pre_two, act_two = conv_forward(act_one, mid_low[layer][0], taps)
-        pre_three, act_three = conv_forward(act_two[None], mid_low[layer][1], TAPS_ONE)
-        tail = tail_forward(act_three, out_low[layer], down_low[layer], up_low[layer])
+        if layer == 0:
+            act_one = hold(act_one, (1, "far"), (2, "near"))
+            if staged:
+                moves[1].cores()
+                moves[2].along_y()
+                moves[3].along_x(moves[2].near)
+            others = weights_of(1)
+        mid_a, mid_b, out_low, down_low, up_low = others
+        weights.append((in_low, mid_a, mid_b, out_low, down_low, up_low))
+        pre_two, act_two = conv_forward(act_one, mid_a, taps)
+        if layer == 1:
+            act_two = hold(act_two, (4, "near"))
+            if staged:
+                moves[4].along_y()
+        pre_three, act_three = conv_forward(act_two[None], mid_b, TAPS_ONE)
+        if layer == 1:
+            act_three = hold(act_three, (3, "far"))
+            if staged:
+                moves[3].cores()
+        tail = tail_forward(act_three, out_low, down_low, up_low)
         branch = (ALPHA * gains[layer]) * tail[0] * (2.0 * tail[4])[:, None, :]
-        pooled = None
         if layer == 0:
-            pooled = (jnp.sum(act_zero.astype(f32), axis=0) * 0.25).astype(bf16)
             shortcut = dot_t(pooled, skip_low).reshape(branch.shape)
         else:
             shortcut = hidden.reshape(branch.shape)
         before = hidden
         hidden = (shortcut + branch).reshape(cells, -1)
+        if layer == 0:
+            hidden = hold(hidden, (2, "far"), (3, "near"))
+            if staged:
+                moves[2].cores()
+                moves[3].along_y()
+                moves[4].along_x(moves[3].near)
         kept.append((before, act_zero, pre_one, act_one, pre_two, act_two, pre_three, act_three, tail, pooled))
-
-    hidden_low = hidden.astype(bf16)
+    (final_low,) = weights_of(3)
+    hidden_low = hold(hidden.astype(bf16), (4, "far"))
+    if staged:
+        moves[4].cores()
     pre_final = dot_t(hidden_low, final_low).reshape(count, CELLS, -1)
     pooled_final = (jnp.sum(gelu_act(pre_final) * GAMMA, axis=1) / CELLS).astype(bf16)
+    (head_low,) = weights_of(4)
     logits = dot_n(pooled_final, head_low) + head_bias
     largest = jnp.max(logits, axis=1, keepdims=True)
     log_total = largest[:, 0] + jnp.log(jnp.sum(jnp.exp(logits - largest), axis=1))
@@ -842,31 +1032,41 @@
     grad_logits = image_weight[:, None] * (softmax_p - one_hot) / images_all
     bias_part = jnp.sum(grad_logits, axis=0)
     grad_low = grad_logits.astype(bf16)
-    head_factors = lax.all_gather(
-        jnp.concatenate([pooled_final, grad_low], axis=1), EVERY, axis=0, tiled=True
-    )
     grad_pooled = dot_t(grad_low, head_low) * (GAMMA / CELLS)
     grad_final = (gelu_prime(pre_final) * grad_pooled[:, None, :]).astype(bf16).reshape(cells, -1)
     final_grad = dot_sum(grad_final, hidden_low).astype(bf16)
     grad_hidden = dot_n(grad_final, final_low)
+    if staged:
+        packed = pack_gradients([final_grad], slot_part, devices, 16)
+        packed, grad_hidden = lax.optimization_barrier((packed, grad_hidden))
+        final_part = lax.psum_scatter(
+            packed.reshape(devices, -1, 128), "dp", scatter_dimension=0, tiled=False
+        )
+        final_sum = lax.psum(final_part, ("ha", "wa")).reshape(6, -1, 128)
 
     in_grads = [None] * LAYERS
     mid_grads = [None] * LAYERS
     out_grads = [None] * LAYERS
-    block_factors = [None] * LAYERS
+    all_factors = [pooled_final, grad_low]
     gain_parts = [None] * LAYERS
     for layer in reversed(range(LAYERS)):
         before, act_zero, pre_one, act_one, pre_two, act_two, pre_three, act_three, tail, pooled = kept[layer]
+        in_low, mid_a, mid_b, out_low, down_low, up_low = weights[layer]
         taps = TAPS_TWO if layer == 0 else TAPS_ONE
         grad_four, factors, gain_parts[layer] = tail_backward(
-            grad_hidden.reshape(count, CELLS, -1), tail, down_low[layer], up_low[layer], gains[layer]
+            grad_hidden.reshape(count, CELLS, -1), tail, down_low, up_low, gains[layer]
         )
-        block_factors[layer] = lax.all_gather(factors, EVERY, axis=0, tiled=True)
+        all_factors = factors + all_factors
+        if layer == 0:
+            small = jnp.concatenate([loss_part[None], jnp.stack(gain_parts), bias_part])
+            all_factors = jnp.concatenate(all_factors + split_small(small, count), axis=1)
+            all_factors, grad_four = lax.optimization_barrier((all_factors, grad_four))
+            gathered = lax.all_gather(all_factors, EVERY, axis=0, tiled=True)
         out_grads[layer] = dot_sum(grad_four, act_three).astype(bf16)
-        grad_three = (gelu_prime(pre_three) * GAMMA * dot_n(grad_four, out_low[layer])).astype(bf16)
-        grad_two, mid_b = conv_backward(grad_three, act_two[None], pre_two[None], mid_low[layer][1], TAPS_ONE)
-        grad_one, mid_a = conv_backward(grad_two[0], act_one, pre_one, mid_low[layer][0], taps)
-        mid_grads[layer] = (mid_a, mid_b)
+        grad_three = (gelu_prime(pre_three) * GAMMA * dot_n(grad_four, out_low)).astype(bf16)
+        grad_two, mid_grad_b = conv_backward(grad_three, act_two[None], pre_two[None], mid_b, TAPS_ONE)
+        grad_one, mid_grad_a = conv_backward(grad_two[0], act_one, pre_one, mid_a, taps)
+        mid_grads[layer] = (mid_grad_a, mid_grad_b)
         in_grad = dot_sum(grad_one, act_zero).astype(bf16)
         if layer == 0:
             skip_grad = dot_sum(grad_hidden.astype(bf16), pooled).astype(bf16)
@@ -874,54 +1074,70 @@
         else:
             in_grads[layer] = in_grad
             scale = GAMMA * (1.0 + layer * ALPHA * ALPHA) ** (-0.5)
-            grad_zero = dot_n(grad_one[0], in_low[layer])
+            grad_zero = dot_n(grad_one[0], in_low)
             grad_hidden = grad_hidden + gelu_prime(before) * scale * grad_zero
 
-    def own_units(units, inputs):
-        width = units.shape[1]
-        part = width // starts.shape[0] // 4
-        padded = jnp.pad(units, ((0, 0), (0, 4 * part)))
-        mine = lax.dynamic_slice_in_dim(padded, my_start * part, 6 * part, 1)
-        return dot_sum(mine, inputs)
-
-    final_width = pooled_final.shape[1]
-    head_own = own_units(head_factors[:, :final_width], head_factors[:, final_width:])
-    wide, narrow = tail[0].shape[-1], tail[3].shape[-1]
-    up_own, down_own = [], []
-    for layer in range(LAYERS):
-        every = block_factors[layer]
-        ends = [wide, wide + narrow, wide + 2 * narrow, 2 * wide + 2 * narrow]
-        up_own.append(own_units(every[:, : ends[0]], every[:, ends[0] : ends[1]]))
-        down_own.append(own_units(every[:, ends[1] : ends[2]], every[:, ends[2] : ends[3]]))
-
-    small = jnp.concatenate([loss_part[None], jnp.stack(gain_parts), bias_part])
-    small = jnp.sum(lax.all_gather(small, EVERY, axis=0, tiled=False), axis=0)
+    def own_units(span):
+        part = span[1] // starts.shape[0] // 4
+        return lax.dynamic_slice_in_dim(gathered, span[0] + my_start * part, 6 * part, 1)
+
+    wide, narrow, final_width = tail[0].shape[-1], tail[3].shape[-1], pooled_final.shape[1]
+    spans = []
+    at = 0
+    for width in [wide, narrow, narrow, wide] * LAYERS + [final_width, logits.shape[1]]:
+        spans.append((at, width))
+        at += width
+
+    small = join_small(gathered[:, at:], count)
     loss_sum = small[0]
-    small_grad = small[1:]
+    small_grad = small[1 : 1 + small_params.shape[0]]
 
     flat_mids = [g for pair in mid_grads for g in pair]
-    local_grads = [final_grad, in_grads[0]] + in_grads[1:] + out_grads + flat_mids
+    local_grads = in_grads + out_grads + flat_mids
     members = (
-        (w_final, first_final, second_final),
         (w_entry, first_entry, second_entry),
         (w_in, first_in, second_in),
         (w_out, first_out, second_out),
         (w_mid, first_mid, second_mid),
+        (w_final, first_final, second_final),
     )
-    if known_mesh():
+    if staged:
         packed = pack_gradients(local_grads, slot_part, devices, SPAN)
-        new = update_packed(sum_at_owners(packed), members, my_share)
+        packed = after(packed, final_part)
+        new = update_packed(sum_at_owners(packed), members[:-1], my_share)
+        new += update_packed(final_sum, members[-1:], my_share)
     else:
-        sums = [sum_plain(g, slot_part) for g in local_grads]
+        sums = [sum_plain(g, slot_part) for g in local_grads + [final_grad]]
         new = []
         for weight, first, second in members:
             count = len(leads(weight.shape))
             total, sums = jnp.stack(sums[:count]), sums[count:]
             new.append(update(weight, total, first, second, my_share, True, True))
-    final_new, entry_new, in_new, out_new, mid_new = new
-    down_new = update(se_down, jnp.stack(down_own), first_down, second_down, my_share, False, True)
-    up_new = update(se_up, jnp.stack(up_own), first_up, second_up, my_share, False, True)
-    head_new = update(head, head_own, first_head, second_head, my_share, False, False)
+    entry_new, in_new, out_new, mid_new, final_new = new
+    def owned(first_span):
+        return jnp.stack([own_units(spans[4 * k + first_span]) for k in range(LAYERS)])
+
+    def blocks(first_span):
+        (at, across), (then, _) = spans[first_span], spans[4 + first_span]
+        return at // across, across, (then - at) // across
+
+    up_new = update_factors(
+        se_up, owned(0), gathered, blocks(1), first_up, second_up, my_share
+    )
+    down_new = update_factors(
+        se_down, owned(2), gathered, blocks(3), first_down, second_down, my_share
+    )
+    head_new = update_factors(
+        head.T[None],
+        own_units(spans[-2])[None],
+        gathered,
+        (spans[-1][0] // 1024, 1024, 0),
+        first_head.T[None],
+        second_head.T[None],
+        my_share,
+        turned=True,
+    )
+    head_new = [a[0].T for a in head_new]
     results = [loss_sum]
     for new in (entry_new, in_new, mid_new, out_new, down_new, up_new, final_new, head_new):
         results.extend(new)

time: 1160 us -> 875 us (0.75)
  waiting for transfers between devices: 244 us -> 63 us
  local copies, waits for them, and re-layouts: 120 us -> 60.7 us
  Pallas kernels: 567 us -> 517 us
  matrix products: 145 us -> 131 us
    ppermute x13 -> x23, waiting for transfers between devices: 244 us -> 52.9 us  [the longest x4 27.4 us: along_y(): self.far = lax.ppermute(self.near, 'wa', [(0, 1), (1, 0)])]
    pallas_call x1, Pallas kernels: 293 us -> 242 us  [sum_at_owners(): pl.pallas_call(functools.partial(sum_kernel, orders, spans), out_shape=ja...]
    unnamed x189 -> x232, local copies, waits for them, and re-layouts: 73.4 us -> 32.5 us
    convert_element_type x5 -> x0, local copies, waits for them, and re-layouts: 33.2 us -> none  [the longest x3 29.1 us: body(): source = pixels.astype(f32) if layer == 0 else hidden]
    pallas_call x6 -> x9, Pallas kernels: 76.1 us -> 95.2 us  [the longest x5 50.8 us: unpack_weights(): pl.pallas_call(functools.partial(unpack_kernel, count, shapes), out_shape...]
    pallas_call x4, Pallas kernels: 68.7 us -> 53.9 us  [conv_backward(): pl.pallas_call(functools.partial(conv_back_kernel, taps, chunk), grid=(ch...]
    pallas_call x4, Pallas kernels: 40.3 us -> 26.5 us  [conv_forward(): pl.pallas_call(functools.partial(conv_kernel, taps, chunk), grid=(channel...]
    dot_general x11 -> x6, matrix products: 43.5 us -> 30 us  [dot_sum(): lax.dot_general(up, low, (((0,), (0,)), ((), ())), preferred_element_type...]
  transfers between devices with their start and end apart: 18 -> 27, of which waited for: 3 -> 8; matrix products, arithmetic and copies ran while one was open for 12% -> 19% of each run, Pallas kernels for 39% -> 55%
where the time goes in v2:
time: 875 us; the launch traced here: 865 us
  Pallas kernels  517 us (59%)
  matrix products  131 us (15%)
  waiting for transfers between devices  63 us (7%)
  local copies, waits for them, and re-layouts  60.7 us (7%)
  other arithmetic  43.7 us (5%)
  starting transfers between devices  25.7 us (3%)
  between operations  23.8 us (3%)
    pallas_call x1, Pallas kernels, sum_at_owners(): pl.pallas_call(functools.partial(sum_kernel, orders, spans), out_shape=ja...  242 us
    dot_general x11, matrix products, dot_t(): lax.dot_general(left, right, (((left.ndim - 1,), (1,)), ((), ())), prefer...  57.3 us
    pallas_call x4, Pallas kernels, conv_backward(): pl.pallas_call(functools.partial(conv_back_kernel, taps, chunk), grid=(ch...  53.9 us
    pallas_call x2, Pallas kernels, update_packed(): pl.pallas_call(functools.partial(update_packed_kernel, tuple(shapes)), gr...  51.5 us
    pallas_call x5, Pallas kernels, unpack_weights(): pl.pallas_call(functools.partial(unpack_kernel, count, shapes), out_shape...  50.8 us
    dot_general x9, matrix products, dot_n(): lax.dot_general(left, right, (((left.ndim - 1,), (0,)), ((), ())), prefer...  44 us
    pallas_call x3, Pallas kernels, update_factors(): pl.pallas_call(functools.partial(update_factors_kernel, owned, turned, bl...  32.9 us
    unnamed x232, local copies, waits for them, and re-layouts  32.5 us
  transfers between devices with their start and end apart: 27, of which 8 were waited for; matrix products, arithmetic and copies ran while one was open for 19% of the time, Pallas kernels for 55%

profile of v2, /device:TPU:0, one launch (start us, length us, event | category | flops | bytes accessed | tf_op | source)
XLA Modules:
  0.0 864.7 jit_solution(12858784100155846781)
XLA Ops:
  8.0 7.6 all-to-all-start
  34.5 6.8 collective-permute-done.refs_1_
  71.5 14.1 %collective-permute-done.3.refs_1_ = bf16[3,2592,128]{2,1,0:T(8,128)(2,1)} collective-permute-done((bf16[3,2592,128]{2,1,0:T(8,128)(2,1)}, bf16[3,2592,128]{2,1,0:T(8,128)(2,1)}, u32[]{:S(2)}, u32[]{:S(2)}) %collective-permute-start.3) | collective-permute-done | bytes 1990688 | tf_op jit(solution)/shard_map/ppermute | solution.py:229
  98.9 10.0 %all-to-all-done.tiles_ref = bf16[8,16,4,8,512]{4,3,2,1,0:T(8,128)(2,1)} async-done(((bf16[8,16,4,8,512]{4,3,2,1,0:T(8,128)(2,1)}), bf16[8,16,4,8,512]{4,3,2,1,0:T(8,128)(2,1)}, u32[]{:S(2)}, u32[]{:S(2)}) %all-to-all-start) | async-done | bytes 4194336 | tf_op jit(solution)/shard_map/all_to_all | solution.py:906
  108.9 11.5 %prepare.1 = (bf16[4,1024,512]{2,1,0:T(8,128)(2,1)S(1)}, bf16[1024,512]{1,0:T(8,128)(2,1)S(1)}) custom-call(bf16[8,16,4,8,512]{4,3,2,1,0:T(8,128)(2,1)} %all-to-all-done.tiles_ref, bf16[256,256]{1,0:T(8,128)(2,1)S(1)} %fusion.74.place_ref), custom_call_target="tpu_custom_call" | custom-call | flops 1073741824 | bytes 10485760 | tf_op jit(solution)/shard_map/prepare/pallas_call | solution.py:470
  120.4 10.6 %fusion.5 = (bf16[4,1024,768]{2,1,0:T(8,128)(2,1)S(1)}, f32[4,1024,768]{2,1,0:T(8,128)}) fusion(bf16[4,1024,512]{2,1,0:T(8,128)(2,1)S(1)} %get-tuple-element.107, bf16[2304,512]{1,0:T(8,128)(2,1)} %copy-done.22), kind=kOutput, calls=%fused_computation.9 | convolution fusion | flops 3252682752 | bytes 23855104 | tf_op jit(solution)/shard_map/dot_general | solution.py:819
  131.0 8.3 collective-permute-done.4.refs_2_
  149.3 11.3 %unpack_weights.6 = (bf16[768,1152]{1,0:T(8,128)(2,1)S(1)}, bf16[768,1152]{1,0:T(8,128)(2,1)S(1)}, bf16[1536,768]{1,0:T(8,128)(2,1)S(1)}, bf16[768,1536]{1,0:T(8,128)(2,1)}, bf16[1536,768]{1,0:T(8,128)(2,1)}) custom-call(s32[16]{0:T(128)S(1)} %get-tuple-element.207.which_ref, s32[16]{0:T(128)S(1)} %get-tuple-element.189.place_ref, ...), custom_call_target="tpu_custom_call" | custom-call | bytes 21233664 | tf_op jit(solution)/shard_map/unpack_weights/pallas_call | solution.py:194
  160.7 7.2 conv_forward.4
  188.9 6.8 collective-permute-done.9.refs_2_
  203.4 19.7 %unpack_weights.7 = (bf16[768,1536]{1,0:T(8,128)(2,1)S(1)}, bf16[768,1152]{1,0:T(8,128)(2,1)S(1)}, bf16[768,1152]{1,0:T(8,128)(2,1)S(1)}, bf16[1536,768]{1,0:T(8...) custom-call(s32[16]{0:T(128)S(1)} %get-tuple-element.207.which_ref, ...), custom_call_target="tpu_custom_call" | custom-call | bytes 25952256 | tf_op jit(solution)/shard_map/unpack_weights/pallas_call | solution.py:194
  254.7 7.6 bitcast_reduce_fusion
  268.9 12.3 %collective-permute-done.16.refs_2_ = bf16[3,1536,128]{2,1,0:T(8,128)(2,1)S(1)} collective-permute-done((bf16[3,1536,128]{2,1,0:T(8,128)(2,1)}, bf16[3,1536,128]{2,1,0:T(8,128)(2,1)S(1)}, u32[]{:S(2)}, u32[]{:S(2)}) %collective-permute-start.16) | collective-permute-done | bytes 1179680 | tf_op jit(solution)/shard_map/ppermute | solution.py:232
  281.7 7.8 unpack_weights.8
  289.5 18.1 %fusion.18 = (f32[16,3072]{1,0:T(8,128)S(1)}, f32[1024,3072]{1,0:T(8,128)}) fusion(bf16[1024,1536]{1,0:T(8,128)(2,1)S(1)} %fusion.30, bf16[3072,1536]{1,0:T(8,128)(2,1)} %unpack_weights.8), kind=kOutput, calls=%fused_computation.22 | convolution fusion | flops 9695084544 | bytes 25362432 | tf_op jit(solution)/shard_map/dot_general | solution.py:819
  321.1 10.0 %fusion.12 = bf16[1024,3072]{1,0:T(8,128)(2,1)S(1)} fusion(f32[1024,3072]{1,0:T(8,128)} %get-tuple-element.231, f32[16,3072]{1,0:T(8,128)S(1)} %convolution_multiply_fusion), kind=kLoop, calls=%fused_computation.16 | loop fusion | flops 56623104 | bytes 19070976 | tf_op jit(solution)/shard_map/convert_element_type | solution.py:1036
  331.2 11.9 %fusion.115 = f32[1024,1536]{1,0:T(8,128)} fusion(bf16[1024,3072]{1,0:T(8,128)(2,1)S(1)} %fusion.12, bf16[3072,1536]{1,0:T(8,128)(2,1)S(1)} %bitcast.189), kind=kOutput, calls=%fused_computation.238 | convolution fusion | flops 9663676416 | bytes 22020096 | tf_op jit(solution)/shard_map/dot_general | solution.py:825
  343.0 10.6 %convolution_convert_fusion.refs_0_ = bf16[3072,1536]{1,0:T(8,128)(2,1)S(1)} fusion(bf16[1024,3072]{1,0:T(8,128)(2,1)S(1)} %fusion.12, bf16[1024,1536]{1,0:T(8,128)(2,1)S(1)} %fusion.30), kind=kOutput, calls=%fused_computation.23 | convolution fusion | flops 9668395008 | bytes 18874368 | tf_op jit(solution)/shard_map/dot_general | solution.py:833
  353.7 11.7 %pack_gradients.2 = bf16[24,2304,128]{2,1,0:T(8,128)(2,1)} custom-call(s32[24]{0:T(128)S(1)} %add.421.part_ref, bf16[3072,1536]{1,0:T(8,128)(2,1)S(1)} %convolution_convert_fusion.refs_0_), custom_call_target="tpu_custom_call" | custom-call | bytes 28311552 | tf_op jit(solution)/shard_map/pack_gradients/pallas_call | solution.py:273
  366.8 7.3 fusion.31
  390.9 11.9 %conv_backward.4 = (bf16[1,1024,768]{2,1,0:T(8,128)(2,1)S(1)}, bf16[768,1152]{1,0:T(8,128)(2,1)}) custom-call(bf16[1024,768]{1,0:T(8,128)(2,1)S(1)} %fusion.47.up_ref, bf16[1,1024,768]{2,1,0:T(8,128)(2,1)S(1)} %bitcast.178, f32[1,1024,768]{2,1,0:T(8,128)} %bitcast.176, bf16[768,1152]{1,0:T(8,128)(2,1)} %copy-done.48), custom_call_target="tpu_custom_call" | custom-call | flops 3623878656 | bytes 7864320 | tf_op jit(solution)/shard_map/conv_backward/pallas_call | solution.py:622
  402.9 11.9 %conv_backward.5 = (bf16[1,1024,768]{2,1,0:T(8,128)(2,1)S(1)}, bf16[768,1152]{1,0:T(8,128)(2,1)}) custom-call(bf16[1024,768]{1,0:T(8,128)(2,1)S(1)} %bitcast.179, bf16[1,1024,768]{2,1,0:T(8,128)(2,1)S(1)} %copy-done.32, f32[1,1024,768]{2,1,0:T(8,128)} %bitcast.196, bf16[768,1152]{1,0:T(8,128)(2,1)} %copy-done.47), custom_call_target="tpu_custom_call" | custom-call | flops 3623878656 | bytes 7864320 | tf_op jit(solution)/shard_map/conv_backward/pallas_call | solution.py:622
  414.9 11.5 %fusion.33 = (f32[16,1536]{1,0:T(8,128)S(1)}, f32[1024,1536]{1,0:T(8,128)}) fusion(f32[1024,1536]{1,0:T(8,128)} %get-tuple-element.219, f32[1024,1536]{1,0:T(8,128)} %fusion.115, bf16[768,1536]{1,0:T(8,128)(2,1)S(1)} %copy-done.43, bf16[1,1024,768]{2,1,0:T(8,128)(2,1)S(1)} %get-tuple-element.147, f32[1024,1536]{1,0:T(8,128)S(1)} %bitcast.185), kind=kOutput, calls=%fused_computation.50 | convolution fusion | flops 2448924672 | bytes 29196288 | tf_op jit(solution)/shard_map/dot_general | solution.py:825
  448.4 12.1 %conv_backward.6 = (bf16[1,1024,768]{2,1,0:T(8,128)(2,1)S(1)}, bf16[768,1152]{1,0:T(8,128)(2,1)}) custom-call(bf16[1024,768]{1,0:T(8,128)(2,1)S(1)} %fusion.55.up_ref, bf16[1,1024,768]{2,1,0:T(8,128)(2,1)S(1)} %bitcast.175, f32[1,1024,768]{2,1,0:T(8,128)} %bitcast.173, bf16[768,1152]{1,0:T(8,128)(2,1)} %copy-done.46), custom_call_target="tpu_custom_call" | custom-call | flops 3623878656 | bytes 7864320 | tf_op jit(solution)/shard_map/conv_backward/pallas_call | solution.py:622
  460.5 18.1 %conv_backward.7 = (bf16[4,1024,768]{2,1,0:T(8,128)(2,1)}, bf16[768,1152]{1,0:T(8,128)(2,1)S(1)}) custom-call(bf16[1024,768]{1,0:T(8,128)(2,1)S(1)} %bitcast.172, bf16[4,1024,768]{2,1,0:T(8,128)(2,1)} %copy-done.6, f32[4,1024,768]{2,1,0:T(8,128)} %get-tuple-element.217.pre_ref, bf16[768,1152]{1,0:T(8,128)(2,1)S(1)} %copy-done.21), custom_call_target="tpu_custom_call" | custom-call | flops 3623878656 | bytes 26738688 | tf_op jit(solution)/shard_map/conv_backward/pallas_call | solution.py:622
  501.5 17.6 %pack_gradients.3 = bf16[24,4096,128]{2,1,0:T(8,128)(2,1)} custom-call(s32[24]{0:T(128)S(1)} %add.421.part_ref, bf16[2304,512]{1,0:T(8,128)(2,1)S(1)} %pad_maximum_fusion.refs_0_, bf16[768,1536]{1,0:T(8,128)(2,1)S(1)} %convolution_convert_fusion.3.refs_1_, bf16[1536,768]{1,0:T(8,128)(2,1)S(1)} %convolution_convert_fusion.2.refs_2_, ...), custom_call_target="tpu_custom_call" | custom-call | bytes 50331648 | tf_op jit(solution)/shard_map/pack_gradients/pallas_call | solution.py:273
  519.0 241.9 %sum_at_owners.1 = bf16[24,2,2,2,128,128]{5,4,3,2,1,0:T(8,128)(2,1)} custom-call(bf16[2,2,24,2,2,2,128,128]{7,6,5,4,3,2,1,0:T(8,128)(2,1)} %bitcast.180), custom_call_target="tpu_custom_call" | custom-call | flops 12582912 | bytes 50331648 | tf_op jit(solution)/shard_map/sum_at_owners/pallas_call | solution.py:426
  761.0 31.0 %update_packed.2 = (f32[864,512]{1,0:T(8,128)}, f32[864,512]{1,0:T(8,128)}, f32[864,512]{1,0:T(8,128)}, f32[1,288,1536]{2,1,0:T(8,128)}, f32[1,288,1536]{2,1,0:T...) custom-call(s32[1]{0:T(128)} %dynamic_slice.42.share_ref, ...), custom_call_target="tpu_custom_call" | custom-call | flops 92897280 | bytes 83607552 | tf_op jit(solution)/shard_map/update_packed/pallas_call | solution.py:698
  797.1 9.9 %update_factors.4 = (f32[2,576,768]{2,1,0:T(8,128)}, f32[2,576,768]{2,1,0:T(8,128)}, f32[2,576,768]{2,1,0:T(8,128)}) custom-call(s32[1]{0:T(128)} %dynamic_slice.42.share_ref, bf16[2,512,576]{2,1,0:T(8,128)(2,1)} %pad_maximum_fusion.1.units_ref, bf16[512,13672]{1,0:T(8,128)(2,1)} %all-gather.2.cloned.1.call-done.inputs_ref, f32[2,576,768]{2,1,0:T(8,128)} %w_ref.3, ...), custom_call_target="tpu_custom_call" | custom-call | flops 919240704 | bytes 21233664 | tf_op jit(solution)/shard_map/update_factors/pallas_call | solution.py:746
  809.6 10.4 %update_factors.3 = (f32[2,288,1536]{2,1,0:T(8,128)}, f32[2,288,1536]{2,1,0:T(8,128)}, f32[2,288,1536]{2,1,0:T(8,128)}) custom-call(s32[1]{0:T(128)} %dynamic_slice.42.share_ref, bf16[2,512,288]{2,1,0:T(8,128)(2,1)} %pad_maximum_fusion.2.units_ref, bf16[512,13672]{1,0:T(8,128)(2,1)} %all-gather.2.cloned.1.call-done.inputs_ref, f32[2,288,1536]{2,1,0:T(8,128)} %w_ref.2, ...), custom_call_target="tpu_custom_call" | custom-call | flops 919240704 | bytes 21233664 | tf_op jit(solution)/shard_map/update_factors/pallas_call | solution.py:746
  823.1 12.5 %update_factors.5 = (f32[1,1000,1152]{2,1,0:T(8,128)}, f32[1,1000,1152]{2,1,0:T(8,128)}, f32[1,1000,1152]{2,1,0:T(8,128)}) custom-call(s32[1]{0:T(128)} %dynamic_slice.42.share_ref, bf16[1,512,1152]{2,1,0:T(8,128)(2,1)} %dynamic-slice_bitcast_fusion.units_ref, bf16[512,13672]{1,0:T(8,128)(2,1)} %all-gather.2.cloned.1.call-done.inputs_ref, ...), custom_call_target="tpu_custom_call" | custom-call | flops 1196928000 | bytes 27648000 | tf_op jit(solution)/shard_map/update_factors/pallas_call | solution.py:746
  836.4 20.5 %update_packed.3 = (f32[1152,1536]{1,0:T(8,128)}, f32[1152,1536]{1,0:T(8,128)}, f32[1152,1536]{1,0:T(8,128)}) custom-call(s32[1]{0:T(128)} %dynamic_slice.42.share_ref, bf16[6,2304,128]{2,1,0:T(8,128)(2,1)} %all-reduce.3.cloned.1.call-done.packed_ref, f32[1152,1536]{1,0:T(8,128)} %refs_0_.9, f32[1152,1536]{1,0:T(8,128)} %refs_1_.7, f32[1152,1536]{1,0:T(8,128)} %refs_2_.7), custom_call_target="tpu_custom_call" | custom-call | flops 53084160 | bytes 47775744 | tf_op jit(solution)/shard_map/update_packed/pallas_call | solution.py:698
  (370 shorter events, 220.4 us)
Async XLA Ops:
  8.0 100.9 %all-to-all-start = ((bf16[8,16,4,8,512]{4,3,2,1,0:T(8,128)(2,1)}), bf16[8,16,4,8,512]{4,3,2,1,0:T(8,128)(2,1)}, u32[]{:S(2)}, u32[]{:S(2)}) async-start(bf16[8,16,4,8,512]{4,3,2,1,0:T(8,128)(2,1)} %bitcast.194), calls=%async_computation | async-start | bytes 8388608 | tf_op jit(solution)/shard_map/all_to_all | solution.py:906
  15.6 473.8 %reduce-scatter.2.cloned.1.call-start = ((), (), s32[]{:S(2)}) async-start(), calls=%async_computation.3 | async-start | bytes 17694720 | tf_op jit(solution)/shard_map/reduce_scatter | solution.py:1042
  19.9 21.4 %collective-permute-start = (bf16[6,576,128]{2,1,0:T(8,128)(2,1)}, bf16[6,576,128]{2,1,0:T(8,128)(2,1)}, u32[]{:S(2)}, u32[]{:S(2)}) collective-permute-start(bf16[6,576,128]{2,1,0:T(8,128)(2,1)} %pack_weights.5.refs_0_), channel_id=1, source_target_pairs={{0,16},{8,24},{16,0},{24,8},{1,17},{9,25},{17,1},{25,9},{2,18},{10... | collective-permute-start | bytes 2654216 | tf_op jit(solution)/shard_map/ppermute | solution.py:229
  41.3 44.2 %collective-permute-start.3 = (bf16[3,2592,128]{2,1,0:T(8,128)(2,1)}, bf16[3,2592,128]{2,1,0:T(8,128)(2,1)}, u32[]{:S(2)}, u32[]{:S(2)}) collective-permute-start(bf16[3,2592,128]{2,1,0:T(8,128)(2,1)} %constant_dynamic-slice_fusion.3), channel_id=1, source_target_pairs={{0,16},{8,24},{16,0},{24,8},{1,17},{9,25},{17,1},{25,9},{2,18},{10... | collective-permute-start | bytes 5971976 | tf_op jit(solution)/shard_map/ppermute | solution.py:229
  42.8 46.1 %collective-permute-start.1 = (bf16[6,576,128]{2,1,0:T(8,128)(2,1)}, bf16[6,576,128]{2,1,0:T(8,128)(2,1)}, u32[]{:S(2)}, u32[]{:S(2)}) collective-permute-start(bf16[6,576,128]{2,1,0:T(8,128)(2,1)} %pack_weights.5.refs_0_), channel_id=1, source_target_pairs={{0,8},{8,0},{16,24},{24,16},{1,9},{9,1},{17,25},{25,17},{2,10},{10... | collective-permute-start | bytes 2654216 | tf_op jit(solution)/shard_map/ppermute | solution.py:236
  42.8 102.1 %collective-permute-start.6 = (bf16[6,2592,128]{2,1,0:T(8,128)(2,1)}, bf16[6,2592,128]{2,1,0:T(8,128)(2,1)}, u32[]{:S(2)}, u32[]{:S(2)}) collective-permute-start(bf16[6,2592,128]{2,1,0:T(8,128)(2,1)} %pack_weights.6.refs_0_), channel_id=1, source_target_pairs={{0,8},{8,0},{16,24},{24,16},{1,9},{9,1},{17,25},{25,17},{2,10},{10... | collective-permute-start | bytes 11943944 | tf_op jit(solution)/shard_map/ppermute | solution.py:236
  85.6 53.7 %collective-permute-start.5 = (bf16[3,3168,128]{2,1,0:T(8,128)(2,1)}, bf16[3,3168,128]{2,1,0:T(8,128)(2,1)}, u32[]{:S(2)}, u32[]{:S(2)}) collective-permute-start(bf16[3,3168,128]{2,1,0:T(8,128)(2,1)} %constant_dynamic-slice_fusion.2), channel_id=1, source_target_pairs={{0,16},{8,24},{16,0},{24,8},{1,17},{9,25},{17,1},{25,9},{2,18},{10... | collective-permute-start | bytes 7299080 | tf_op jit(solution)/shard_map/ppermute | solution.py:229
  87.1 2.6 collective-permute-start.2
  87.2 52.1 %collective-permute-start.4 = (bf16[3,2592,128]{2,1,0:T(8,128)(2,1)}, bf16[3,2592,128]{2,1,0:T(8,128)(2,1)}, u32[]{:S(2)}, u32[]{:S(2)}) collective-permute-start(bf16[3,2592,128]{2,1,0:T(8,128)(2,1)} %collective-permute-done.3.refs_1_), channel_id=1, source_target_pairs={{0,1},{1,0},{2,3},{3,2},{4,5},{5,4},{6,7},{7,6},{8,9},{9,8},{10,11... | collective-permute-start | bytes 5971976 | tf_op jit(solution)/shard_map/ppermute | solution.py:232
  98.6 46.3 %collective-permute-start.7 = (bf16[3,2592,128]{2,1,0:T(8,128)(2,1)}, bf16[3,2592,128]{2,1,0:T(8,128)(2,1)}, u32[]{:S(2)}, u32[]{:S(2)}) collective-permute-start(bf16[3,2592,128]{2,1,0:T(8,128)(2,1)} %collective-permute-done.3.refs_1_), channel_id=1, source_target_pairs={{0,8},{8,0},{16,24},{24,16},{1,9},{9,1},{17,25},{25,17},{2,10},{10... | collective-permute-start | bytes 5971976 | tf_op jit(solution)/shard_map/ppermute | solution.py:236
  120.4 63.5 %copy-start.33 = (bf16[1024,512]{1,0:T(8,128)(2,1)}, bf16[1024,512]{1,0:T(8,128)(2,1)S(1)}, u32[]{:S(2)}) copy-start(bf16[1024,512]{1,0:T(8,128)(2,1)S(1)} %get-tuple-element.106) | copy-start | bytes 3145732
  131.0 29.7 %copy-start.6 = (bf16[4,1024,768]{2,1,0:T(8,128)(2,1)}, bf16[4,1024,768]{2,1,0:T(8,128)(2,1)S(1)}, u32[]{:S(2)}) copy-start(bf16[4,1024,768]{2,1,0:T(8,128)(2,1)S(1)} %get-tuple-element.114.act_ref) | copy-start | bytes 18874372
  139.3 7.2 collective-permute-start.8
  139.4 58.6 %collective-permute-start.11 = (bf16[6,3168,128]{2,1,0:T(8,128)(2,1)}, bf16[6,3168,128]{2,1,0:T(8,128)(2,1)}, u32[]{:S(2)}, u32[]{:S(2)}) collective-permute-start(bf16[6,3168,128]{2,1,0:T(8,128)(2,1)} %pack_weights.7.refs_0_), channel_id=1, source_target_pairs={{0,8},{8,0},{16,24},{24,16},{1,9},{9,1},{17,25},{25,17},{2,10},{10... | collective-permute-start | bytes 14598152 | tf_op jit(solution)/shard_map/ppermute | solution.py:236
  139.8 55.9 %collective-permute-start.9 = (bf16[3,3168,128]{2,1,0:T(8,128)(2,1)}, bf16[3,3168,128]{2,1,0:T(8,128)(2,1)}, u32[]{:S(2)}, u32[]{:S(2)}) collective-permute-start(bf16[3,3168,128]{2,1,0:T(8,128)(2,1)} %collective-permute-done.5.refs_1_), channel_id=1, source_target_pairs={{0,1},{1,0},{2,3},{3,2},{4,5},{5,4},{6,7},{7,6},{8,9},{9,8},{10,11... | collective-permute-start | bytes 7299080 | tf_op jit(solution)/shard_map/ppermute | solution.py:232
  144.9 53.2 %collective-permute-start.12 = (bf16[3,3168,128]{2,1,0:T(8,128)(2,1)}, bf16[3,3168,128]{2,1,0:T(8,128)(2,1)}, u32[]{:S(2)}, u32[]{:S(2)}) collective-permute-start(bf16[3,3168,128]{2,1,0:T(8,128)(2,1)} %collective-permute-done.5.refs_1_), channel_id=1, source_target_pairs={{0,8},{8,0},{16,24},{24,16},{1,9},{9,1},{17,25},{25,17},{2,10},{10... | collective-permute-start | bytes 7299080 | tf_op jit(solution)/shard_map/ppermute | solution.py:236
  144.9 43.9 %collective-permute-start.10 = (bf16[3,2304,128]{2,1,0:T(8,128)(2,1)}, bf16[3,2304,128]{2,1,0:T(8,128)(2,1)}, u32[]{:S(2)}, u32[]{:S(2)}) collective-permute-start(bf16[3,2304,128]{2,1,0:T(8,128)(2,1)} %constant_dynamic-slice_fusion.1), channel_id=1, source_target_pairs={{0,16},{8,24},{16,0},{24,8},{1,17},{9,25},{17,1},{25,9},{2,18},{10... | collective-permute-start | bytes 5308424 | tf_op jit(solution)/shard_map/ppermute | solution.py:229
  188.8 34.3 %copy-start.64 = (f32[1024,1536]{1,0:T(8,128)}, f32[1024,1536]{1,0:T(8,128)S(1)}, u32[]{:S(2)}) copy-start(f32[1024,1536]{1,0:T(8,128)S(1)} %fusion.32) | copy-start | bytes 18874372
  195.7 7.7 collective-permute-start.13
  195.7 85.5 %collective-permute-start.17 = (bf16[6,2304,128]{2,1,0:T(8,128)(2,1)S(1)}, bf16[6,2304,128]{2,1,0:T(8,128)(2,1)}, u32[]{:S(2)}, u32[]{:S(2)}) collective-permute-start(bf16[6,2304,128]{2,1,0:T(8,128)(2,1)S(1)} %copy-done.8), channel_id=1, source_target_pairs={{0,8},{8,0},{16,24},{24,16},{1,9},{9,1},{17,25},{25,17},{2,10},{10... | collective-permute-start | bytes 10616840 | tf_op jit(solution)/shard_map/ppermute | solution.py:236
  196.2 51.3 %collective-permute-start.15 = (bf16[3,2304,128]{2,1,0:T(8,128)(2,1)}, bf16[3,2304,128]{2,1,0:T(8,128)(2,1)}, u32[]{:S(2)}, u32[]{:S(2)}) collective-permute-start(bf16[3,2304,128]{2,1,0:T(8,128)(2,1)} %collective-permute-done.10.refs_1_), channel_id=1, source_target_pairs={{0,1},{1,0},{2,3},{3,2},{4,5},{5,4},{6,7},{7,6},{8,9},{9,8},{10,11... | collective-permute-start | bytes 5308424 | tf_op jit(solution)/shard_map/ppermute | solution.py:232
  198.0 83.7 %collective-permute-start.18 = (bf16[3,2304,128]{2,1,0:T(8,128)(2,1)}, bf16[3,2304,128]{2,1,0:T(8,128)(2,1)}, u32[]{:S(2)}, u32[]{:S(2)}) collective-permute-start(bf16[3,2304,128]{2,1,0:T(8,128)(2,1)} %collective-permute-done.10.refs_1_), channel_id=1, source_target_pairs={{0,8},{8,0},{16,24},{24,16},{1,9},{9,1},{17,25},{25,17},{2,10},{10... | collective-permute-start | bytes 5308424 | tf_op jit(solution)/shard_map/ppermute | solution.py:236
  198.1 39.9 %collective-permute-start.14 = (bf16[3,1536,128]{2,1,0:T(8,128)(2,1)S(1)}, bf16[3,1536,128]{2,1,0:T(8,128)(2,1)}, u32[]{:S(2)}, u32[]{:S(2)}) collective-permute-start(bf16[3,1536,128]{2,1,0:T(8,128)(2,1)S(1)} %constant_dynamic-slice_fusion), channel_id=1, source_target_pairs={{0,16},{8,24},{16,0},{24,8},{1,17},{9,25},{17,1},{25,9},{2,18},{10... | collective-permute-start | bytes 3538952 | tf_op jit(solution)/shard_map/ppermute | solution.py:229
  247.4 34.3 %collective-permute-start.19 = (bf16[3,2304,128]{2,1,0:T(8,128)(2,1)}, bf16[3,2304,128]{2,1,0:T(8,128)(2,1)}, u32[]{:S(2)}, u32[]{:S(2)}) collective-permute-start(bf16[3,2304,128]{2,1,0:T(8,128)(2,1)} %collective-permute-done.15.refs_2_), channel_id=1, source_target_pairs={{0,8},{8,0},{16,24},{24,16},{1,9},{9,1},{17,25},{25,17},{2,10},{10... | collective-permute-start | bytes 5308424 | tf_op jit(solution)/shard_map/ppermute | solution.py:236
  252.5 66.1 %copy-start.89 = (f32[16]{0:T(128)}, f32[16]{0:T(128)S(1)}, u32[]{:S(2)}) copy-start(f32[16]{0:T(128)S(1)} %select_reduce_fusion.1) | copy-start | bytes 196
  252.5 55.1 %collective-permute-start.20 = (bf16[6,1536,128]{2,1,0:T(8,128)(2,1)}, bf16[6,1536,128]{2,1,0:T(8,128)(2,1)S(1)}, u32[]{:S(2)}, u32[]{:S(2)}) collective-permute-start(bf16[6,1536,128]{2,1,0:T(8,128)(2,1)} %copy-done.10), channel_id=1, source_target_pairs={{0,8},{8,0},{16,24},{24,16},{1,9},{9,1},{17,25},{25,17},{2,10},{10... | collective-permute-start | bytes 7077896 | tf_op jit(solution)/shard_map/ppermute | solution.py:236
  253.0 28.2 %collective-permute-start.16 = (bf16[3,1536,128]{2,1,0:T(8,128)(2,1)}, bf16[3,1536,128]{2,1,0:T(8,128)(2,1)S(1)}, u32[]{:S(2)}, u32[]{:S(2)}) collective-permute-start(bf16[3,1536,128]{2,1,0:T(8,128)(2,1)} %collective-permute-done.14.refs_1_), channel_id=1, source_target_pairs={{0,1},{1,0},{2,3},{3,2},{4,5},{5,4},{6,7},{7,6},{8,9},{9,8},{10,11... | collective-permute-start | bytes 3538952 | tf_op jit(solution)/shard_map/ppermute | solution.py:232
  281.2 26.5 %collective-permute-start.21 = (bf16[3,1536,128]{2,1,0:T(8,128)(2,1)}, bf16[3,1536,128]{2,1,0:T(8,128)(2,1)S(1)}, u32[]{:S(2)}, u32[]{:S(2)}) collective-permute-start(bf16[3,1536,128]{2,1,0:T(8,128)(2,1)} %collective-permute-done.14.refs_1_), channel_id=1, source_target_pairs={{0,8},{8,0},{16,24},{24,16},{1,9},{9,1},{17,25},{25,17},{2,10},{10... | collective-permute-start | bytes 3538952 | tf_op jit(solution)/shard_map/ppermute | solution.py:236
  281.2 26.5 %collective-permute-start.22 = (bf16[3,1536,128]{2,1,0:T(8,128)(2,1)S(1)}, bf16[3,1536,128]{2,1,0:T(8,128)(2,1)S(1)}, u32[]{:S(2)}, u32[]{:S(2)}) collective-permute-start(bf16[3,1536,128]{2,1,0:T(8,128)(2,1)S(1)} %collective-permute-done.16.refs_2_), channel_id=1, source_target_pairs={{0,8},{8,0},{16,24},{24,16},{1,9},{9,1},{17,25},{25,17},{2,10},{10... | collective-permute-start | bytes 3538952 | tf_op jit(solution)/shard_map/ppermute | solution.py:236
  365.4 426.7 %all-gather.2.cloned.1.call-start = ((), (), s32[]{:S(2)}) async-start(), calls=%async_computation.2 | async-start | bytes 14462976 | tf_op jit(solution)/shard_map/all_gather | solution.py:1064
  438.3 398.1 %all-reduce.3.cloned.1.call-start = ((), (), s32[]{:S(2)}) async-start(), calls=%async_computation.4 | async-start | bytes 7077888 | tf_op jit(solution)/shard_map/psum | solution.py:1045
  448.4 30.2 %slice-start.7 = ((s8[6291456]{0:T(1024)(128)(4,1)}), s8[2097152]{0:T(1024)(128)(4,1)S(1)}, s32[]{:S(2)}) async-start(s8[6291456]{0:T(1024)(128)(4,1)} %bitcast.190), calls=%async_computation.12 | async-start | bytes 4194304
  (111 other events, 899.5 us)
Sparse Core Ops, SparseCore 0:
  365.5 109.3 reduce-scatter.1
  489.6 250.9 all-reduce.2
Sparse Core Ops, SparseCore 1:
  438.4 192.0 all-gather.1

commit v3 on v2

--- a/solution.py
+++ b/solution.py
@@ -40,14 +40,14 @@
 
 
 def gelu_act(v):
-    return 0.5 * v * (1.0 + jnp.tanh(GELU_SCALE * (v + GELU_CUBE * v * v * v)))
+    half = 0.5 * v
+    return half + half * jnp.tanh(v * (GELU_SCALE + (GELU_SCALE * GELU_CUBE) * (v * v)))
 
 
 def gelu_prime(v):
-    th = jnp.tanh(GELU_SCALE * (v + GELU_CUBE * v * v * v))
-    return 0.5 * (1.0 + th) + (0.5 * GELU_SCALE) * v * (1.0 - th * th) * (
-        1.0 + 3.0 * GELU_CUBE * v * v
-    )
+    cube = (GELU_SCALE * GELU_CUBE) * (v * v)
+    th = jnp.tanh(v * (GELU_SCALE + cube))
+    return 0.5 + 0.5 * (th + v * (1.0 - th * th) * (GELU_SCALE + 3.0 * cube))
 
 
 def standardize(weight):
@@ -66,7 +66,8 @@
     first = jnp.sum(jnp.where(owner[:, None] == ids[None, :], starts[None, :], 0), axis=1)
     local = (part_ids - first).astype(jnp.int32)
     held = jnp.minimum(jnp.arange(6, dtype=jnp.int32)[None, :], shares[:, None] - 1)
-    return owner, local, starts, (starts[:, None] + held).reshape(-1).astype(jnp.int32)
+    slot_part = (starts[:, None] + held).reshape(-1).astype(jnp.int32)
+    return owner, local, starts, (slot_part, (ids[:, None] * 6 + held).reshape(-1))
 
 
 def known_mesh():
@@ -171,18 +172,21 @@
 
         return carry
 
-    def spread(i, carry):
-        pltpu.make_async_copy(held.at[i], held.at[i], arrived.at[i]).wait()
-        at = 0
+    def spread(group, carry):
+        for j in range(4):
+            i = group * 4 + j
+            pltpu.make_async_copy(held.at[i], held.at[i], arrived.at[i]).wait()
+            at = 0
+            for k, (part, width) in enumerate(shapes):
+                block, at = read_packed(held.at[i], at, part, width)
+                stages[k][pl.ds(pl.multiple_of(i * part, part), part), :] = block
         for k, (part, width) in enumerate(shapes):
-            rows = pl.ds(pl.multiple_of(i * part, part), part)
-            block, at = read_packed(held.at[i], at, part, width)
-            stages[k][rows, :] = block
+            rows = pl.ds(pl.multiple_of(group * 4 * part, part), 4 * part)
             pltpu.make_async_copy(stages[k].at[rows, :], outs[k].at[rows, :], left.at[k]).start()
         return carry
 
     lax.fori_loop(0, parts, fetch, 0)
-    lax.fori_loop(0, parts, spread, 0)
+    lax.fori_loop(0, parts // 4, spread, 0)
     for k in range(len(shapes)):
         pltpu.make_async_copy(stages[k], outs[k], left.at[k]).wait()
 
@@ -252,7 +256,7 @@
     return which, at.astype(jnp.int32)
 
 
-def pack_gradients_kernel(pad, part_ref, *refs):
+def pack_gradients_kernel(pad, part_ref, slot_ref, *refs):
     out_ref = refs[-1]
     at = 0
     for ref in refs[:-1]:
@@ -265,7 +269,7 @@
     specs, rows = [], 0
     for gradient in gradients:
         part, width = gradient.shape[0] // (4 * devices), gradient.shape[1]
-        specs.append(pl.BlockSpec((part, width), lambda s, parts: (parts[s], 0)))
+        specs.append(pl.BlockSpec((part, width), lambda s, parts, held: (parts[s], 0)))
         rows += packed_rows(part, width)
     pad = -rows % unit
     rows += pad
@@ -273,10 +277,10 @@
     return pl.pallas_call(
         functools.partial(pack_gradients_kernel, pad),
         grid_spec=pltpu.PrefetchScalarGridSpec(
-            num_scalar_prefetch=1,
+            num_scalar_prefetch=2,
             grid=(slots,),
             in_specs=specs,
-            out_specs=pl.BlockSpec((None, rows, 128), lambda s, parts: (s, 0, 0)),
+            out_specs=pl.BlockSpec((None, rows, 128), lambda s, parts, held: (held[s], 0, 0)),
         ),
         out_shape=jax.ShapeDtypeStruct((slots, rows, 128), bf16),
         compiler_params=pltpu.CompilerParams(vmem_limit_bytes=40 * MIB),
@@ -284,7 +288,7 @@
             flops=0, bytes_accessed=slots * rows * 128 * 4, transcendentals=0
         ),
         name="pack_gradients",
-    )(slot_part, *gradients)
+    )(*slot_part, *gradients)
 
 
 SPAN = 1024
@@ -534,7 +538,7 @@
         pre = lax.dot_general(
             cols[...], w_ref[...], (((1,), (1,)), ((), ())), preferred_element_type=f32
         )
-        pre_ref[pl.ds(base, rows), :] = pre
+        pre_ref[pl.ds(base, rows), :] = pre.astype(bf16)
         out_ref[pl.ds(base, rows), :] = (gelu_act(pre) * GAMMA).astype(bf16)
         return carry
 
@@ -548,7 +552,7 @@
         functools.partial(conv_kernel, taps, chunk),
         grid=(channels // GROUP,),
         out_shape=[
-            jax.ShapeDtypeStruct((cells, channels), f32),
+            jax.ShapeDtypeStruct((cells, channels), bf16),
             jax.ShapeDtypeStruct((cells, channels), bf16),
         ],
         in_specs=[
@@ -606,7 +610,7 @@
                 up_cols[:, at : at + size], w_cols[at : at + size, :], preferred_element_type=f32
             )
             at += size
-            pre = pre_ref[phase, pl.ds(base, rows), :]
+            pre = pre_ref[phase, pl.ds(base, rows), :].astype(f32)
             down_ref[phase, pl.ds(base, rows), :] = (gelu_prime(pre) * GAMMA * back).astype(bf16)
         return carry
 
@@ -836,11 +840,12 @@
 def tail_forward(act_three, out_w, down_w, up_w):
     images = act_three.shape[0] // CELLS
     pre_four = dot_t(act_three, out_w).reshape(images, CELLS, -1)
+    kept_four = pre_four.astype(bf16)
     squeezed = (jnp.sum(pre_four, axis=1) / CELLS).astype(bf16)
     pre_down = dot_t(squeezed, down_w)
     act_down = gelu_act(pre_down).astype(bf16)
     gate_sig = jax.nn.sigmoid(dot_t(act_down, up_w))
-    return pre_four, squeezed, pre_down, act_down, gate_sig
+    return kept_four, squeezed, pre_down, act_down, gate_sig
 
 
 def tail_backward(grad_hidden, stored, down_w, up_w, gain):
@@ -907,19 +912,16 @@
     spot = lax.axis_index("ha") * cols_n + lax.axis_index("wa")
     my_labels = lax.dynamic_slice_in_dim(labels.reshape(-1), spot * count, count, 0)
 
-    def block_entries(layer):
-        return [
-            (w_mid, (layer, 0), True),
-            (w_mid, (layer, 1), True),
-            (w_out, (layer,), True),
-            (se_down, (layer,), False),
-            (se_up, (layer,), False),
-        ]
+    def middle(layer):
+        return [(w_mid, (layer, 0), True), (w_mid, (layer, 1), True)]
+
+    def rest(layer):
+        return [(w_out, (layer,), True), (se_down, (layer,), False), (se_up, (layer,), False)]
 
     groups = [
         [(w_entry, (), True)],
-        block_entries(0),
-        [(w_in, (0,), True)] + block_entries(1),
+        middle(0) + rest(0),
+        [(w_in, (0,), True)] + middle(1) + rest(1),
         [(w_final, (), True)],
         [(head, (), False)],
     ]
@@ -946,13 +948,20 @@
         act_zero = (gelu_act(pixels.astype(f32)) * GAMMA).astype(bf16)
         pooled = (jnp.sum(act_zero.astype(f32), axis=0) * 0.25).astype(bf16)
 
-    def hold(value, *arrivals):
+    def hold(value, arrivals, *then):
         if not staged:
             return value
-        kept = [getattr(moves[k], name) for k, name in arrivals]
-        value, *kept = lax.optimization_barrier((value, *kept))
-        for (k, name), buffer in zip(arrivals, kept):
+        came = [getattr(moves[k], name) for k, name in arrivals]
+        value, *came = lax.optimization_barrier((value, *came))
+        for (k, name), buffer in zip(arrivals, came):
             setattr(moves[k], name, buffer)
+        for step, k in then:
+            if step == "x":
+                moves[k].along_x(moves[k - 1].near)
+            elif step == "y":
+                moves[k].along_y()
+            else:
+                moves[k].cores()
         return value
 
     def weights_of(group):
@@ -977,49 +986,40 @@
             (entry_low,) = weights_of(0)
             in_low, skip_low = entry_low[:NECK], entry_low[NECK:]
         else:
-            in_low, *others = weights_of(1 + layer)
+            in_low, *others = weights_of(2)
         pre_one = dot_t(act_zero, in_low)
         act_one = (gelu_act(pre_one) * GAMMA).astype(bf16)
         if layer == 0:
-            act_one = hold(act_one, (1, "far"), (2, "near"))
-            if staged:
-                moves[1].cores()
-                moves[2].along_y()
-                moves[3].along_x(moves[2].near)
+            act_one = hold(
+                act_one, [(1, "far"), (2, "near")], ("cores", 1), ("y", 2), ("x", 3)
+            )
             others = weights_of(1)
+        else:
+            act_one = hold(act_one, [(4, "near")], ("y", 4))
         mid_a, mid_b, out_low, down_low, up_low = others
         weights.append((in_low, mid_a, mid_b, out_low, down_low, up_low))
         pre_two, act_two = conv_forward(act_one, mid_a, taps)
-        if layer == 1:
-            act_two = hold(act_two, (4, "near"))
-            if staged:
-                moves[4].along_y()
         pre_three, act_three = conv_forward(act_two[None], mid_b, TAPS_ONE)
-        if layer == 1:
-            act_three = hold(act_three, (3, "far"))
-            if staged:
-                moves[3].cores()
+        if layer == 0:
+            act_three = hold(act_three, [(3, "near")], ("x", 4))
         tail = tail_forward(act_three, out_low, down_low, up_low)
         branch = (ALPHA * gains[layer]) * tail[0] * (2.0 * tail[4])[:, None, :]
         if layer == 0:
             shortcut = dot_t(pooled, skip_low).reshape(branch.shape)
         else:
             shortcut = hidden.reshape(branch.shape)
-        before = hidden
+        before = None if hidden is None else hidden.astype(bf16)
         hidden = (shortcut + branch).reshape(cells, -1)
         if layer == 0:
-            hidden = hold(hidden, (2, "far"), (3, "near"))
-            if staged:
-                moves[2].cores()
-                moves[3].along_y()
-                moves[4].along_x(moves[3].near)
-        kept.append((before, act_zero, pre_one, act_one, pre_two, act_two, pre_three, act_three, tail, pooled))
+            hidden = hold(hidden, [(2, "far")], ("cores", 2), ("y", 3))
+        else:
+            hidden = hold(hidden, [(3, "far")], ("cores", 3))
+        kept.append((before, act_zero, pre_one.astype(bf16), act_one, pre_two, act_two, pre_three, act_three, tail, pooled))
     (final_low,) = weights_of(3)
-    hidden_low = hold(hidden.astype(bf16), (4, "far"))
-    if staged:
-        moves[4].cores()
+    hidden_low = hidden.astype(bf16)
     pre_final = dot_t(hidden_low, final_low).reshape(count, CELLS, -1)
     pooled_final = (jnp.sum(gelu_act(pre_final) * GAMMA, axis=1) / CELLS).astype(bf16)
+    pooled_final = hold(pooled_final, [(4, "far")], ("cores", 4))
     (head_low,) = weights_of(4)
     logits = dot_n(pooled_final, head_low) + head_bias
     largest = jnp.max(logits, axis=1, keepdims=True)
@@ -1033,7 +1033,7 @@
     bias_part = jnp.sum(grad_logits, axis=0)
     grad_low = grad_logits.astype(bf16)
     grad_pooled = dot_t(grad_low, head_low) * (GAMMA / CELLS)
-    grad_final = (gelu_prime(pre_final) * grad_pooled[:, None, :]).astype(bf16).reshape(cells, -1)
+    grad_final = (gelu_prime(pre_final.astype(bf16).astype(f32)) * grad_pooled[:, None, :]).astype(bf16).reshape(cells, -1)
     final_grad = dot_sum(grad_final, hidden_low).astype(bf16)
     grad_hidden = dot_n(grad_final, final_low)
     if staged:
@@ -1063,7 +1063,7 @@
             all_factors, grad_four = lax.optimization_barrier((all_factors, grad_four))
             gathered = lax.all_gather(all_factors, EVERY, axis=0, tiled=True)
         out_grads[layer] = dot_sum(grad_four, act_three).astype(bf16)
-        grad_three = (gelu_prime(pre_three) * GAMMA * dot_n(grad_four, out_low)).astype(bf16)
+        grad_three = (gelu_prime(pre_three.astype(f32)) * GAMMA * dot_n(grad_four, out_low)).astype(bf16)
         grad_two, mid_grad_b = conv_backward(grad_three, act_two[None], pre_two[None], mid_b, TAPS_ONE)
         grad_one, mid_grad_a = conv_backward(grad_two[0], act_one, pre_one, mid_a, taps)
         mid_grads[layer] = (mid_grad_a, mid_grad_b)
@@ -1075,7 +1075,7 @@
             in_grads[layer] = in_grad
             scale = GAMMA * (1.0 + layer * ALPHA * ALPHA) ** (-0.5)
             grad_zero = dot_n(grad_one[0], in_low)
-            grad_hidden = grad_hidden + gelu_prime(before) * scale * grad_zero
+            grad_hidden = grad_hidden + gelu_prime(before.astype(f32)) * scale * grad_zero
 
     def own_units(span):
         part = span[1] // starts.shape[0] // 4
@@ -1107,7 +1107,7 @@
         new = update_packed(sum_at_owners(packed), members[:-1], my_share)
         new += update_packed(final_sum, members[-1:], my_share)
     else:
-        sums = [sum_plain(g, slot_part) for g in local_grads + [final_grad]]
+        sums = [sum_plain(g, slot_part[0]) for g in local_grads + [final_grad]]
         new = []
         for weight, first, second in members:
             count = len(leads(weight.shape))

time: 875 us -> 850 us (0.971)
  Pallas kernels: 517 us -> 493 us
    pallas_call x5, Pallas kernels: 50.8 us -> 29.4 us  [unpack_weights(): pl.pallas_call(functools.partial(unpack_kernel, count, shapes), out_shape...]
    ppermute x5, waiting for transfers between devices: 20.9 us -> 35.2 us  [along_x(): self.near = lax.ppermute(after(mine, *others), 'dp', CHIP)]
    ppermute x4, waiting for transfers between devices: 27.4 us -> 15.7 us  [along_y(): self.far = lax.ppermute(self.near, 'wa', [(0, 1), (1, 0)])]
    unnamed x232 -> x202, local copies, waits for them, and re-layouts: 32.5 us -> 22.8 us
  transfers between devices with their start and end apart: 27 -> 27, of which waited for: 8 -> 10; matrix products, arithmetic and copies ran while one was open for 19% -> 20% of each run, Pallas kernels for 55% -> 55%
where the time goes in v3:
time: 850 us; the launch traced here: 839 us
  Pallas kernels  493 us (58%)
  matrix products  132 us (16%)
  waiting for transfers between devices  69.4 us (8%)
  local copies, waits for them, and re-layouts  54 us (6%)
  other arithmetic  43.3 us (5%)
  starting transfers between devices  23.9 us (3%)
  between operations  23 us (3%)
    pallas_call x1, Pallas kernels, sum_at_owners(): pl.pallas_call(functools.partial(sum_kernel, orders, spans), out_shape=ja...  244 us
    dot_general x11, matrix products, dot_t(): lax.dot_general(left, right, (((left.ndim - 1,), (1,)), ((), ())), prefer...  57.7 us
    pallas_call x4, Pallas kernels, conv_backward(): pl.pallas_call(functools.partial(conv_back_kernel, taps, chunk), grid=(ch...  52.8 us
    pallas_call x2, Pallas kernels, update_packed(): pl.pallas_call(functools.partial(update_packed_kernel, tuple(shapes)), gr...  51.2 us
    dot_general x9, matrix products, dot_n(): lax.dot_general(left, right, (((left.ndim - 1,), (0,)), ((), ())), prefer...  40.7 us
    ppermute x5, waiting for transfers between devices, along_x(): self.near = lax.ppermute(after(mine, *others), 'dp', CHIP)  35.2 us
    dot_general x6, matrix products, dot_sum(): lax.dot_general(up, low, (((0,), (0,)), ((), ())), preferred_element_type...  33.6 us
    pallas_call x3, Pallas kernels, update_factors(): pl.pallas_call(functools.partial(update_factors_kernel, owned, turned, bl...  32.5 us
  transfers between devices with their start and end apart: 27, of which 10 were waited for; matrix products, arithmetic and copies ran while one was open for 20% of the time, Pallas kernels for 55%

profile of v3, /device:TPU:0, one launch (start us, length us, event | category | flops | bytes accessed | tf_op | source)
XLA Modules:
  0.0 839.2 jit_solution(7533008534400019896)
XLA Ops:
  8.0 7.6 all-to-all-start
  34.5 6.8 collective-permute-done.refs_1_
  62.5 6.8 pack_weights.7.refs_0_
  72.5 13.0 %collective-permute-done.3.refs_1_ = bf16[3,2592,128]{2,1,0:T(8,128)(2,1)} collective-permute-done((bf16[3,2592,128]{2,1,0:T(8,128)(2,1)}, bf16[3,2592,128]{2,1,0:T(8,128)(2,1)}, u32[]{:S(2)}, u32[]{:S(2)}) %collective-permute-start.3) | collective-permute-done | bytes 1990688 | tf_op jit(solution)/shard_map/ppermute | solution.py:233
  93.1 15.8 %all-to-all-done.tiles_ref = bf16[8,16,4,8,512]{4,3,2,1,0:T(8,128)(2,1)} async-done(((bf16[8,16,4,8,512]{4,3,2,1,0:T(8,128)(2,1)}), bf16[8,16,4,8,512]{4,3,2,1,0:T(8,128)(2,1)}, u32[]{:S(2)}, u32[]{:S(2)}) %all-to-all-start) | async-done | bytes 4194336 | tf_op jit(solution)/shard_map/all_to_all | solution.py:911
  108.9 11.4 %prepare.1 = (bf16[4,1024,512]{2,1,0:T(8,128)(2,1)S(1)}, bf16[1024,512]{1,0:T(8,128)(2,1)S(1)}) custom-call(bf16[8,16,4,8,512]{4,3,2,1,0:T(8,128)(2,1)} %all-to-all-done.tiles_ref, bf16[256,256]{1,0:T(8,128)(2,1)S(1)} %fusion.88.place_ref), custom_call_target="tpu_custom_call" | custom-call | flops 1073741824 | bytes 10485760 | tf_op jit(solution)/shard_map/prepare/pallas_call | solution.py:474
  121.3 8.8 %fusion.123 = (bf16[4,1024,768]{2,1,0:T(8,128)(2,1)}, bf16[4,1024,768]{2,1,0:T(8,128)(2,1)S(1)}) fusion(bf16[4,1024,512]{2,1,0:T(8,128)(2,1)S(1)} %get-tuple-element.108, bf16[2304,512]{1,0:T(8,128)(2,1)S(1)} %unpack_weights.5), kind=kOutput, calls=%fused_computation.250 | convolution fusion | flops 3252682752 | bytes 17563648 | tf_op jit(solution)/shard_map/dot_general | solution.py:823
  130.1 9.2 %collective-permute-done.4.refs_2_ = bf16[3,2592,128]{2,1,0:T(8,128)(2,1)} collective-permute-done((bf16[3,2592,128]{2,1,0:T(8,128)(2,1)}, bf16[3,2592,128]{2,1,0:T(8,128)(2,1)}, u32[]{:S(2)}, u32[]{:S(2)}) %collective-permute-start.4) | collective-permute-done | bytes 1990688 | tf_op jit(solution)/shard_map/ppermute | solution.py:236
  149.0 7.1 unpack_weights.6
  156.2 7.3 conv_forward.4
  163.5 6.4 conv_forward.5
  169.9 12.1 %collective-permute-done.9.refs_1_ = bf16[3,2304,128]{2,1,0:T(8,128)(2,1)} collective-permute-done((bf16[3,2304,128]{2,1,0:T(8,128)(2,1)}, bf16[3,2304,128]{2,1,0:T(8,128)(2,1)}, u32[]{:S(2)}, u32[]{:S(2)}) %collective-permute-start.9) | collective-permute-done | bytes 1769504 | tf_op jit(solution)/shard_map/ppermute | solution.py:233
  205.8 7.4 unpack_weights.7
  213.2 12.9 %convert_bitcast_fusion = (bf16[1,1024,768]{2,1,0:T(8,128)(2,1)}, bf16[1,1024,768]{2,1,0:T(8,128)(2,1)S(1)}) fusion(bf16[768,1536]{1,0:T(8,128)(2,1)S(1)} %get-tuple-element.129, f32[1024,1536]{1,0:T(8,128)} %fusion.36), kind=kOutput, calls=%fused_computation.118 | convolution fusion | flops 2437939200 | bytes 11796480 | tf_op jit(solution)/shard_map/dot_general | solution.py:823
  260.4 6.7 unpack_weights.8
  267.1 16.8 %fusion.16 = (f32[16,3072]{1,0:T(8,128)S(1)}, bf16[1024,3072]{1,0:T(8,128)(2,1)}) fusion(bf16[1024,1536]{1,0:T(8,128)(2,1)S(1)} %copy-done.65, bf16[3072,1536]{1,0:T(8,128)(2,1)} %unpack_weights.8), kind=kOutput, calls=%fused_computation.21 | convolution fusion | flops 9695084544 | bytes 19070976 | tf_op jit(solution)/shard_map/dot_general | solution.py:823
  304.0 6.9 fusion.9
  311.0 11.8 %fusion.128 = f32[1024,1536]{1,0:T(8,128)} fusion(bf16[1024,3072]{1,0:T(8,128)(2,1)S(1)} %fusion.9, bf16[3072,1536]{1,0:T(8,128)(2,1)S(1)} %bitcast.187), kind=kOutput, calls=%fused_computation.253 | convolution fusion | flops 9663676416 | bytes 22020096 | tf_op jit(solution)/shard_map/dot_general | solution.py:829
  322.8 10.5 %convolution_convert_fusion.refs_0_ = bf16[3072,1536]{1,0:T(8,128)(2,1)S(1)} fusion(bf16[1024,3072]{1,0:T(8,128)(2,1)S(1)} %fusion.9, bf16[1024,1536]{1,0:T(8,128)(2,1)S(1)} %copy-done.66), kind=kOutput, calls=%fused_computation.22 | convolution fusion | flops 9668395008 | bytes 18874368 | tf_op jit(solution)/shard_map/dot_general | solution.py:837
  333.3 9.6 %pack_gradients.2 = bf16[24,2304,128]{2,1,0:T(8,128)(2,1)} custom-call(s32[24]{0:T(128)S(1)} %add.441.part_ref, s32[24]{0:T(128)S(1)} %add.444.slot_ref, bf16[3072,1536]{1,0:T(8,128)(2,1)S(1)} %convolution_convert_fusion.refs_0_), custom_call_target="tpu_custom_call" | custom-call | bytes 28311552 | tf_op jit(solution)/shard_map/pack_gradients/pallas_call | solution.py:277
  364.0 12.6 %conv_backward.4 = (bf16[1,1024,768]{2,1,0:T(8,128)(2,1)S(1)}, bf16[768,1152]{1,0:T(8,128)(2,1)}) custom-call(bf16[1024,768]{1,0:T(8,128)(2,1)S(1)} %fusion.58.up_ref, bf16[1,1024,768]{2,1,0:T(8,128)(2,1)S(1)} %bitcast.178, bf16[1,1024,768]{2,1,0:T(8,128)(2,1)} %bitcast.176, bf16[768,1152]{1,0:T(8,128)(2,1)} %copy-done.37), custom_call_target="tpu_custom_call" | custom-call | flops 3623878656 | bytes 7864320 | tf_op jit(solution)/shard_map/conv_backward/pallas_call | solution.py:626
  376.6 11.6 %conv_backward.5 = (bf16[1,1024,768]{2,1,0:T(8,128)(2,1)S(1)}, bf16[768,1152]{1,0:T(8,128)(2,1)}) custom-call(bf16[1024,768]{1,0:T(8,128)(2,1)S(1)} %bitcast.179, bf16[1,1024,768]{2,1,0:T(8,128)(2,1)S(1)} %copy-done.50, bf16[1,1024,768]{2,1,0:T(8,128)(2,1)} %get-tuple-element.199.pre_ref, bf16[768,1152]{1,0:T(8,128)(2,1)} %copy-done.36), custom_call_target="tpu_custom_call" | custom-call | flops 3623878656 | bytes 7864320 | tf_op jit(solution)/shard_map/conv_backward/pallas_call | solution.py:626
  388.3 9.8 %multiply_reduce_fusion = (f32[16,1536]{1,0:T(8,128)S(1)}, f32[1024,1536]{1,0:T(8,128)}) fusion(bf16[1024,1536]{1,0:T(8,128)(2,1)S(1)} %copy-done.62, f32[1024,1536]{1,0:T(8,128)} %fusion.128, bf16[768,1536]{1,0:T(8,128)(2,1)S(1)} %copy-done.32, bf16[1,1024,768]{2,1,0:T(8,128)(2,1)S(1)} %get-tuple-element.149, f32[1024,1536]{1,0:T(8,128)S(1)} %bitcast.183), kind=kOutput, calls=%fused_computation.57 | convolution fusion | flops 2448924672 | bytes 26050560 | tf_op jit(solution)/shard_map/dot_general | solution.py:829
  421.2 11.8 %conv_backward.6 = (bf16[1,1024,768]{2,1,0:T(8,128)(2,1)S(1)}, bf16[768,1152]{1,0:T(8,128)(2,1)}) custom-call(bf16[1024,768]{1,0:T(8,128)(2,1)S(1)} %fusion.49.up_ref, bf16[1,1024,768]{2,1,0:T(8,128)(2,1)S(1)} %bitcast.175, bf16[1,1024,768]{2,1,0:T(8,128)(2,1)} %bitcast.173, bf16[768,1152]{1,0:T(8,128)(2,1)} %copy-done.35), custom_call_target="tpu_custom_call" | custom-call | flops 3623878656 | bytes 7864320 | tf_op jit(solution)/shard_map/conv_backward/pallas_call | solution.py:626
  433.0 16.8 %conv_backward.7 = (bf16[4,1024,768]{2,1,0:T(8,128)(2,1)}, bf16[768,1152]{1,0:T(8,128)(2,1)S(1)}) custom-call(bf16[1024,768]{1,0:T(8,128)(2,1)S(1)} %bitcast.172, bf16[4,1024,768]{2,1,0:T(8,128)(2,1)} %copy-done.6, bf16[4,1024,768]{2,1,0:T(8,128)(2,1)} %get-tuple-element.197.pre_ref, bf16[768,1152]{1,0:T(8,128)(2,1)S(1)} %copy-done.16), custom_call_target="tpu_custom_call" | custom-call | flops 3623878656 | bytes 26738688 | tf_op jit(solution)/shard_map/conv_backward/pallas_call | solution.py:626
  476.2 15.4 %pack_gradients.3 = bf16[24,4096,128]{2,1,0:T(8,128)(2,1)} custom-call(s32[24]{0:T(128)S(1)} %add.441.part_ref, s32[24]{0:T(128)S(1)} %add.444.slot_ref, bf16[2304,512]{1,0:T(8,128)(2,1)S(1)} %pad_maximum_fusion.refs_0_, bf16[768,1536]{1,0:T(8,128)(2,1)S(1)} %convolution_convert_fusion.3.refs_1_, bf16[1536,768]{1,0:T(8,128)(2,1)S(1)} %convolution_convert_fusion.2.refs_2_, ...), custom_call_target="tpu_custom_call" | custom-call | bytes 50331648 | tf_op jit(solution)/shard_map/pack_gradients/pallas_call | solution.py:277
  491.6 244.5 %sum_at_owners.1 = bf16[24,2,2,2,128,128]{5,4,3,2,1,0:T(8,128)(2,1)} custom-call(bf16[2,2,24,2,2,2,128,128]{7,6,5,4,3,2,1,0:T(8,128)(2,1)} %bitcast.180), custom_call_target="tpu_custom_call" | custom-call | flops 12582912 | bytes 50331648 | tf_op jit(solution)/shard_map/sum_at_owners/pallas_call | solution.py:430
  736.1 30.9 %update_packed.2 = (f32[864,512]{1,0:T(8,128)}, f32[864,512]{1,0:T(8,128)}, f32[864,512]{1,0:T(8,128)}, f32[1,288,1536]{2,1,0:T(8,128)}, f32[1,288,1536]{2,1,0:T...) custom-call(s32[1]{0:T(128)} %dynamic_slice.42.share_ref, ...), custom_call_target="tpu_custom_call" | custom-call | flops 92897280 | bytes 83607552 | tf_op jit(solution)/shard_map/update_packed/pallas_call | solution.py:702
  772.1 9.8 %update_factors.4 = (f32[2,576,768]{2,1,0:T(8,128)}, f32[2,576,768]{2,1,0:T(8,128)}, f32[2,576,768]{2,1,0:T(8,128)}) custom-call(s32[1]{0:T(128)} %dynamic_slice.42.share_ref, bf16[2,512,576]{2,1,0:T(8,128)(2,1)} %pad_maximum_fusion.1.units_ref, bf16[512,13672]{1,0:T(8,128)(2,1)} %all-gather.2.cloned.1.call-done.inputs_ref, f32[2,576,768]{2,1,0:T(8,128)} %w_ref.3, ...), custom_call_target="tpu_custom_call" | custom-call | flops 919240704 | bytes 21233664 | tf_op jit(solution)/shard_map/update_factors/pallas_call | solution.py:750
  784.5 10.3 %update_factors.3 = (f32[2,288,1536]{2,1,0:T(8,128)}, f32[2,288,1536]{2,1,0:T(8,128)}, f32[2,288,1536]{2,1,0:T(8,128)}) custom-call(s32[1]{0:T(128)} %dynamic_slice.42.share_ref, bf16[2,512,288]{2,1,0:T(8,128)(2,1)} %pad_maximum_fusion.2.units_ref, bf16[512,13672]{1,0:T(8,128)(2,1)} %all-gather.2.cloned.1.call-done.inputs_ref, f32[2,288,1536]{2,1,0:T(8,128)} %w_ref.2, ...), custom_call_target="tpu_custom_call" | custom-call | flops 919240704 | bytes 21233664 | tf_op jit(solution)/shard_map/update_factors/pallas_call | solution.py:750
  797.8 12.4 %update_factors.5 = (f32[1,1000,1152]{2,1,0:T(8,128)}, f32[1,1000,1152]{2,1,0:T(8,128)}, f32[1,1000,1152]{2,1,0:T(8,128)}) custom-call(s32[1]{0:T(128)} %dynamic_slice.42.share_ref, bf16[1,512,1152]{2,1,0:T(8,128)(2,1)} %dynamic-slice_bitcast_fusion.units_ref, bf16[512,13672]{1,0:T(8,128)(2,1)} %all-gather.2.cloned.1.call-done.inputs_ref, ...), custom_call_target="tpu_custom_call" | custom-call | flops 1196928000 | bytes 27648000 | tf_op jit(solution)/shard_map/update_factors/pallas_call | solution.py:750
  811.0 20.3 %update_packed.3 = (f32[1152,1536]{1,0:T(8,128)}, f32[1152,1536]{1,0:T(8,128)}, f32[1152,1536]{1,0:T(8,128)}) custom-call(s32[1]{0:T(128)} %dynamic_slice.42.share_ref, bf16[6,2304,128]{2,1,0:T(8,128)(2,1)} %all-reduce.3.cloned.1.call-done.packed_ref, f32[1152,1536]{1,0:T(8,128)} %refs_0_.9, f32[1152,1536]{1,0:T(8,128)} %refs_1_.7, f32[1152,1536]{1,0:T(8,128)} %refs_2_.7), custom_call_target="tpu_custom_call" | custom-call | flops 53084160 | bytes 47775744 | tf_op jit(solution)/shard_map/update_packed/pallas_call | solution.py:702
  (338 shorter events, 215.3 us)
Async XLA Ops:
  8.0 100.9 %all-to-all-start = ((bf16[8,16,4,8,512]{4,3,2,1,0:T(8,128)(2,1)}), bf16[8,16,4,8,512]{4,3,2,1,0:T(8,128)(2,1)}, u32[]{:S(2)}, u32[]{:S(2)}) async-start(bf16[8,16,4,8,512]{4,3,2,1,0:T(8,128)(2,1)} %bitcast.190), calls=%async_computation | async-start | bytes 8388608 | tf_op jit(solution)/shard_map/all_to_all | solution.py:911
  15.6 448.4 %reduce-scatter.2.cloned.1.call-start = ((), (), s32[]{:S(2)}) async-start(), calls=%async_computation.3 | async-start | bytes 17694720 | tf_op jit(solution)/shard_map/reduce_scatter | solution.py:1042
  19.9 21.4 %collective-permute-start = (bf16[6,576,128]{2,1,0:T(8,128)(2,1)}, bf16[6,576,128]{2,1,0:T(8,128)(2,1)}, u32[]{:S(2)}, u32[]{:S(2)}) collective-permute-start(bf16[6,576,128]{2,1,0:T(8,128)(2,1)} %pack_weights.5.refs_0_), channel_id=1, source_target_pairs={{0,16},{8,24},{16,0},{24,8},{1,17},{9,25},{17,1},{25,9},{2,18},{10... | collective-permute-start | bytes 2654216 | tf_op jit(solution)/shard_map/ppermute | solution.py:233
  41.3 44.2 %collective-permute-start.3 = (bf16[3,2592,128]{2,1,0:T(8,128)(2,1)}, bf16[3,2592,128]{2,1,0:T(8,128)(2,1)}, u32[]{:S(2)}, u32[]{:S(2)}) collective-permute-start(bf16[3,2592,128]{2,1,0:T(8,128)(2,1)} %constant_dynamic-slice_fusion.3), channel_id=1, source_target_pairs={{0,16},{8,24},{16,0},{24,8},{1,17},{9,25},{17,1},{25,9},{2,18},{10... | collective-permute-start | bytes 5971976 | tf_op jit(solution)/shard_map/ppermute | solution.py:233
  42.8 46.4 %collective-permute-start.1 = (bf16[6,576,128]{2,1,0:T(8,128)(2,1)}, bf16[6,576,128]{2,1,0:T(8,128)(2,1)}, u32[]{:S(2)}, u32[]{:S(2)}) collective-permute-start(bf16[6,576,128]{2,1,0:T(8,128)(2,1)} %pack_weights.5.refs_0_), channel_id=1, source_target_pairs={{0,8},{8,0},{16,24},{24,16},{1,9},{9,1},{17,25},{25,17},{2,10},{10... | collective-permute-start | bytes 2654216 | tf_op jit(solution)/shard_map/ppermute | solution.py:240
  42.8 99.5 %collective-permute-start.6 = (bf16[6,2592,128]{2,1,0:T(8,128)(2,1)}, bf16[6,2592,128]{2,1,0:T(8,128)(2,1)}, u32[]{:S(2)}, u32[]{:S(2)}) collective-permute-start(bf16[6,2592,128]{2,1,0:T(8,128)(2,1)} %pack_weights.6.refs_0_), channel_id=1, source_target_pairs={{0,8},{8,0},{16,24},{24,16},{1,9},{9,1},{17,25},{25,17},{2,10},{10... | collective-permute-start | bytes 11943944 | tf_op jit(solution)/shard_map/ppermute | solution.py:240
  45.0 42.6 %copy-start.89 = (s32[4]{0:T(128)}, s32[4]{0:T(128)S(1)}, u32[]{:S(2)}) copy-start(s32[4]{0:T(128)S(1)} %select_reduce_fusion.3) | copy-start | bytes 52
  85.6 53.7 %collective-permute-start.5 = (bf16[3,3168,128]{2,1,0:T(8,128)(2,1)}, bf16[3,3168,128]{2,1,0:T(8,128)(2,1)}, u32[]{:S(2)}, u32[]{:S(2)}) collective-permute-start(bf16[3,3168,128]{2,1,0:T(8,128)(2,1)} %constant_dynamic-slice_fusion.2), channel_id=1, source_target_pairs={{0,16},{8,24},{16,0},{24,8},{1,17},{9,25},{17,1},{25,9},{2,18},{10... | collective-permute-start | bytes 7299080 | tf_op jit(solution)/shard_map/ppermute | solution.py:233
  87.6 2.6 collective-permute-start.2
  87.7 51.5 %collective-permute-start.4 = (bf16[3,2592,128]{2,1,0:T(8,128)(2,1)}, bf16[3,2592,128]{2,1,0:T(8,128)(2,1)}, u32[]{:S(2)}, u32[]{:S(2)}) collective-permute-start(bf16[3,2592,128]{2,1,0:T(8,128)(2,1)} %collective-permute-done.3.refs_1_), channel_id=1, source_target_pairs={{0,1},{1,0},{2,3},{3,2},{4,5},{5,4},{6,7},{7,6},{8,9},{9,8},{10,11... | collective-permute-start | bytes 5971976 | tf_op jit(solution)/shard_map/ppermute | solution.py:236
  92.8 37.3 %copy-start.17 = (bf16[2304,512]{1,0:T(8,128)(2,1)}, bf16[2304,512]{1,0:T(8,128)(2,1)S(1)}, u32[]{:S(2)}) copy-start(bf16[2304,512]{1,0:T(8,128)(2,1)S(1)} %unpack_weights.5) | copy-start | bytes 7077892
  92.8 53.2 %collective-permute-start.7 = (bf16[3,2592,128]{2,1,0:T(8,128)(2,1)}, bf16[3,2592,128]{2,1,0:T(8,128)(2,1)}, u32[]{:S(2)}, u32[]{:S(2)}) collective-permute-start(bf16[3,2592,128]{2,1,0:T(8,128)(2,1)} %collective-permute-done.3.refs_1_), channel_id=1, source_target_pairs={{0,8},{8,0},{16,24},{24,16},{1,9},{9,1},{17,25},{25,17},{2,10},{10... | collective-permute-start | bytes 5971976 | tf_op jit(solution)/shard_map/ppermute | solution.py:240
  139.3 6.9 collective-permute-start.8
  140.7 41.3 %collective-permute-start.9 = (bf16[3,2304,128]{2,1,0:T(8,128)(2,1)}, bf16[3,2304,128]{2,1,0:T(8,128)(2,1)}, u32[]{:S(2)}, u32[]{:S(2)}) collective-permute-start(bf16[3,2304,128]{2,1,0:T(8,128)(2,1)} %constant_dynamic-slice_fusion.1), channel_id=1, source_target_pairs={{0,16},{8,24},{16,0},{24,8},{1,17},{9,25},{17,1},{25,9},{2,18},{10... | collective-permute-start | bytes 5308424 | tf_op jit(solution)/shard_map/ppermute | solution.py:233
  142.2 60.1 %collective-permute-start.11 = (bf16[6,3168,128]{2,1,0:T(8,128)(2,1)}, bf16[6,3168,128]{2,1,0:T(8,128)(2,1)}, u32[]{:S(2)}, u32[]{:S(2)}) collective-permute-start(bf16[6,3168,128]{2,1,0:T(8,128)(2,1)} %pack_weights.7.refs_0_), channel_id=1, source_target_pairs={{0,8},{8,0},{16,24},{24,16},{1,9},{9,1},{17,25},{25,17},{2,10},{10... | collective-permute-start | bytes 14598152 | tf_op jit(solution)/shard_map/ppermute | solution.py:240
  142.3 56.1 %collective-permute-start.10 = (bf16[3,3168,128]{2,1,0:T(8,128)(2,1)}, bf16[3,3168,128]{2,1,0:T(8,128)(2,1)}, u32[]{:S(2)}, u32[]{:S(2)}) collective-permute-start(bf16[3,3168,128]{2,1,0:T(8,128)(2,1)} %collective-permute-done.5.refs_1_), channel_id=1, source_target_pairs={{0,1},{1,0},{2,3},{3,2},{4,5},{5,4},{6,7},{7,6},{8,9},{9,8},{10,11... | collective-permute-start | bytes 7299080 | tf_op jit(solution)/shard_map/ppermute | solution.py:236
  146.0 56.5 %collective-permute-start.12 = (bf16[3,3168,128]{2,1,0:T(8,128)(2,1)}, bf16[3,3168,128]{2,1,0:T(8,128)(2,1)}, u32[]{:S(2)}, u32[]{:S(2)}) collective-permute-start(bf16[3,3168,128]{2,1,0:T(8,128)(2,1)} %collective-permute-done.5.refs_1_), channel_id=1, source_target_pairs={{0,8},{8,0},{16,24},{24,16},{1,9},{9,1},{17,25},{25,17},{2,10},{10... | collective-permute-start | bytes 7299080 | tf_op jit(solution)/shard_map/ppermute | solution.py:240
  198.5 5.9 collective-permute-start.13
  200.9 28.6 %collective-permute-start.14 = (bf16[3,1536,128]{2,1,0:T(8,128)(2,1)}, bf16[3,1536,128]{2,1,0:T(8,128)(2,1)S(1)}, u32[]{:S(2)}, u32[]{:S(2)}) collective-permute-start(bf16[3,1536,128]{2,1,0:T(8,128)(2,1)} %constant_dynamic-slice_fusion), channel_id=1, source_target_pairs={{0,16},{8,24},{16,0},{24,8},{1,17},{9,25},{17,1},{25,9},{2,18},{10... | collective-permute-start | bytes 3538952 | tf_op jit(solution)/shard_map/ppermute | solution.py:233
  202.0 55.1 %collective-permute-start.16 = (bf16[6,2304,128]{2,1,0:T(8,128)(2,1)S(1)}, bf16[6,2304,128]{2,1,0:T(8,128)(2,1)S(1)}, u32[]{:S(2)}, u32[]{:S(2)}) collective-permute-start(bf16[6,2304,128]{2,1,0:T(8,128)(2,1)S(1)} %copy-done.8), channel_id=1, source_target_pairs={{0,8},{8,0},{16,24},{24,16},{1,9},{9,1},{17,25},{25,17},{2,10},{10... | collective-permute-start | bytes 10616840 | tf_op jit(solution)/shard_map/ppermute | solution.py:240
  202.3 56.5 %collective-permute-start.17 = (bf16[3,2304,128]{2,1,0:T(8,128)(2,1)}, bf16[3,2304,128]{2,1,0:T(8,128)(2,1)}, u32[]{:S(2)}, u32[]{:S(2)}) collective-permute-start(bf16[3,2304,128]{2,1,0:T(8,128)(2,1)} %collective-permute-done.9.refs_1_), channel_id=1, source_target_pairs={{0,8},{8,0},{16,24},{24,16},{1,9},{9,1},{17,25},{25,17},{2,10},{10... | collective-permute-start | bytes 5308424 | tf_op jit(solution)/shard_map/ppermute | solution.py:240
  202.6 53.8 %collective-permute-start.15 = (bf16[3,2304,128]{2,1,0:T(8,128)(2,1)}, bf16[3,2304,128]{2,1,0:T(8,128)(2,1)}, u32[]{:S(2)}, u32[]{:S(2)}) collective-permute-start(bf16[3,2304,128]{2,1,0:T(8,128)(2,1)} %collective-permute-done.9.refs_1_), channel_id=1, source_target_pairs={{0,1},{1,0},{2,3},{3,2},{4,5},{5,4},{6,7},{7,6},{8,9},{9,8},{10,11... | collective-permute-start | bytes 5308424 | tf_op jit(solution)/shard_map/ppermute | solution.py:236
  213.2 30.2 %copy-start.33 = (bf16[1536,768]{1,0:T(8,128)(2,1)}, bf16[1536,768]{1,0:T(8,128)(2,1)S(1)}, u32[]{:S(2)}) copy-start(bf16[1536,768]{1,0:T(8,128)(2,1)S(1)} %get-tuple-element.137) | copy-start | bytes 7077892
  213.2 34.7 %copy-start.10 = (bf16[768,1536]{1,0:T(8,128)(2,1)}, bf16[768,1536]{1,0:T(8,128)(2,1)S(1)}, u32[]{:S(2)}) copy-start(bf16[768,1536]{1,0:T(8,128)(2,1)S(1)} %get-tuple-element.138) | copy-start | bytes 7077892
  213.2 36.0 %copy-start.12 = (bf16[1536,768]{1,0:T(8,128)(2,1)}, bf16[1536,768]{1,0:T(8,128)(2,1)S(1)}, u32[]{:S(2)}) copy-start(bf16[1536,768]{1,0:T(8,128)(2,1)S(1)} %get-tuple-element.139) | copy-start | bytes 7077892
  256.4 4.0 collective-permute-start.18
  256.5 34.0 %collective-permute-start.20 = (bf16[6,1536,128]{2,1,0:T(8,128)(2,1)}, bf16[6,1536,128]{2,1,0:T(8,128)(2,1)S(1)}, u32[]{:S(2)}, u32[]{:S(2)}) collective-permute-start(bf16[6,1536,128]{2,1,0:T(8,128)(2,1)} %pack_weights.9.refs_0_), channel_id=1, source_target_pairs={{0,8},{8,0},{16,24},{24,16},{1,9},{9,1},{17,25},{25,17},{2,10},{10... | collective-permute-start | bytes 7077896 | tf_op jit(solution)/shard_map/ppermute | solution.py:240
  257.0 33.5 %collective-permute-start.21 = (bf16[3,1536,128]{2,1,0:T(8,128)(2,1)S(1)}, bf16[3,1536,128]{2,1,0:T(8,128)(2,1)}, u32[]{:S(2)}, u32[]{:S(2)}) collective-permute-start(bf16[3,1536,128]{2,1,0:T(8,128)(2,1)S(1)} %collective-permute-done.14.refs_1_), channel_id=1, source_target_pairs={{0,8},{8,0},{16,24},{24,16},{1,9},{9,1},{17,25},{25,17},{2,10},{10... | collective-permute-start | bytes 3538952 | tf_op jit(solution)/shard_map/ppermute | solution.py:240
  257.1 28.4 %collective-permute-start.19 = (bf16[3,1536,128]{2,1,0:T(8,128)(2,1)S(1)}, bf16[3,1536,128]{2,1,0:T(8,128)(2,1)}, u32[]{:S(2)}, u32[]{:S(2)}) collective-permute-start(bf16[3,1536,128]{2,1,0:T(8,128)(2,1)S(1)} %collective-permute-done.14.refs_1_), channel_id=1, source_target_pairs={{0,1},{1,0},{2,3},{3,2},{4,5},{5,4},{6,7},{7,6},{8,9},{9,8},{10,11... | collective-permute-start | bytes 3538952 | tf_op jit(solution)/shard_map/ppermute | solution.py:236
  285.5 5.1 collective-permute-start.22
  342.9 424.1 %all-gather.2.cloned.1.call-start = ((), (), s32[]{:S(2)}) async-start(), calls=%async_computation.2 | async-start | bytes 14462976 | tf_op jit(solution)/shard_map/all_gather | solution.py:1064
  411.9 399.1 %all-reduce.3.cloned.1.call-start = ((), (), s32[]{:S(2)}) async-start(), calls=%async_computation.4 | async-start | bytes 7077888 | tf_op jit(solution)/shard_map/psum | solution.py:1045
  (96 other events, 811.3 us)
Sparse Core Ops, SparseCore 0:
  343.1 109.7 reduce-scatter.1
  464.2 259.9 all-reduce.2
Sparse Core Ops, SparseCore 1:
  412.0 203.0 all-gather.1

commit v4 on v3

--- a/solution.py
+++ b/solution.py
@@ -221,39 +221,32 @@
 
 
 class Gather:
-    def __init__(self, entries, whole=False):
+    def __init__(self, entries):
         self.shapes = tuple((e[0].shape[-2] // 6, e[0].shape[-1]) for e in entries)
         self.own = pack_weights(entries)
-        self.whole = whole
 
     def along_x(self, *others):
-        mine = self.own
-        if not self.whole:
-            mine = lax.dynamic_slice_in_dim(mine, lax.axis_index("wa") * 3, 3, 0)
+        mine = lax.dynamic_slice_in_dim(self.own, lax.axis_index("wa") * 3, 3, 0)
         self.near = lax.ppermute(after(mine, *others), "dp", CHIP)
 
     def along_y(self):
         self.far = lax.ppermute(self.near, "wa", [(0, 1), (1, 0)])
 
     def cores(self):
-        buffers = [self.own, self.near] + ([] if self.whole else [self.far])
+        buffers = [self.own, self.near, self.far]
         self.buffers = buffers + [lax.ppermute(b, "dp", CORE) for b in buffers]
 
     def unpacked(self, tables):
-        return unpack_weights(self.buffers, *tables[self.whole], self.shapes)
-
-
-def source_tables(owner, local, whole):
+        return unpack_weights(self.buffers, *tables, self.shapes)
+
+
+def source_tables(owner, local):
     me = lax.axis_index("dp")
     side = lax.axis_index("wa")
     away = owner // 2 != me // 2
-    if whole:
-        which, at, count = away.astype(jnp.int32), local, 2
-    else:
-        which = jnp.where(away, jnp.where(local // 3 == side, 1, 2), 0)
-        at, count = jnp.where(away, local % 3, local), 3
-    which = (which + count * (owner % 2 != me % 2)).astype(jnp.int32)
-    return which, at.astype(jnp.int32)
+    which = jnp.where(away, jnp.where(local // 3 == side, 1, 2), 0)
+    which = which + 3 * (owner % 2 != me % 2)
+    return which.astype(jnp.int32), jnp.where(away, local % 3, local).astype(jnp.int32)
 
 
 def pack_gradients_kernel(pad, part_ref, slot_ref, *refs):
@@ -927,15 +920,16 @@
     ]
     staged = known_mesh()
     if staged:
-        tables = {flag: source_tables(owner, local, flag) for flag in (True, False)}
-        moves = [Gather(groups[0], True), Gather(groups[1])]
+        tables = source_tables(owner, local)
+        moves = [Gather(groups[0]), Gather(groups[1])]
         moves[0].along_x()
         moves[1].along_x(moves[0].near)
-        moves[0].cores()
+        moves[0].along_y()
         for entries in groups[2:]:
             entries[0] = (after(entries[0][0], moves[0].near),) + entries[0][1:]
             moves.append(Gather(entries))
-        moves[1].near = after(moves[1].near, *[m.own for m in moves[2:]])
+        moves[1].near = after(moves[1].near, moves[0].far, *[m.own for m in moves[2:]])
+        moves[0].cores()
         moves[1].along_y()
         moves[2].along_x(moves[1].near)
     cells = count * CELLS
@@ -994,14 +988,12 @@
                 act_one, [(1, "far"), (2, "near")], ("cores", 1), ("y", 2), ("x", 3)
             )
             others = weights_of(1)
-        else:
-            act_one = hold(act_one, [(4, "near")], ("y", 4))
         mid_a, mid_b, out_low, down_low, up_low = others
         weights.append((in_low, mid_a, mid_b, out_low, down_low, up_low))
         pre_two, act_two = conv_forward(act_one, mid_a, taps)
         pre_three, act_three = conv_forward(act_two[None], mid_b, TAPS_ONE)
-        if layer == 0:
-            act_three = hold(act_three, [(3, "near")], ("x", 4))
+        if layer:
+            act_three = hold(act_three, [(4, "near")], ("y", 4))
         tail = tail_forward(act_three, out_low, down_low, up_low)
         branch = (ALPHA * gains[layer]) * tail[0] * (2.0 * tail[4])[:, None, :]
         if layer == 0:
@@ -1011,7 +1003,7 @@
         before = None if hidden is None else hidden.astype(bf16)
         hidden = (shortcut + branch).reshape(cells, -1)
         if layer == 0:
-            hidden = hold(hidden, [(2, "far")], ("cores", 2), ("y", 3))
+            hidden = hold(hidden, [(2, "far"), (3, "near")], ("cores", 2), ("y", 3), ("x", 4))
         else:
             hidden = hold(hidden, [(3, "far")], ("cores", 3))
         kept.append((before, act_zero, pre_one.astype(bf16), act_one, pre_two, act_two, pre_three, act_three, tail, pooled))
@@ -1035,14 +1027,14 @@
     grad_pooled = dot_t(grad_low, head_low) * (GAMMA / CELLS)
     grad_final = (gelu_prime(pre_final.astype(bf16).astype(f32)) * grad_pooled[:, None, :]).astype(bf16).reshape(cells, -1)
     final_grad = dot_sum(grad_final, hidden_low).astype(bf16)
-    grad_hidden = dot_n(grad_final, final_low)
     if staged:
         packed = pack_gradients([final_grad], slot_part, devices, 16)
-        packed, grad_hidden = lax.optimization_barrier((packed, grad_hidden))
+        packed, grad_final = lax.optimization_barrier((packed, grad_final))
         final_part = lax.psum_scatter(
             packed.reshape(devices, -1, 128), "dp", scatter_dimension=0, tiled=False
         )
         final_sum = lax.psum(final_part, ("ha", "wa")).reshape(6, -1, 128)
+    grad_hidden = dot_n(grad_final, final_low)
 
     in_grads = [None] * LAYERS
     mid_grads = [None] * LAYERS

time: 850 us -> 840 us (0.988)
  matrix products: 132 us -> 149 us
  waiting for transfers between devices: 69.4 us -> 53.7 us
  other arithmetic: 43.3 us -> 32.3 us
    ppermute x5, waiting for transfers between devices: 35.2 us -> 14.3 us  [along_x(): self.near = lax.ppermute(after(mine, *others), 'dp', CHIP)]
    dot_general x11, matrix products: 57.7 us -> 68.9 us  [dot_t(): lax.dot_general(left, right, (((left.ndim - 1,), (1,)), ((), ())), prefer...]
    unnamed x202 -> x194, local copies, waits for them, and re-layouts: 22.8 us -> 25.3 us
  transfers between devices with their start and end apart: 27 -> 29, of which waited for: 10 -> 10; matrix products, arithmetic and copies ran while one was open for 20% -> 23% of each run, Pallas kernels for 55% -> 55%
where the time goes in v4:
time: 840 us; the launch traced here: 829 us
  Pallas kernels  492 us (59%)
  matrix products  149 us (18%)
  local copies, waits for them, and re-layouts  54.3 us (6%)
  waiting for transfers between devices  53.7 us (6%)
  other arithmetic  32.3 us (4%)
  starting transfers between devices  24.1 us (3%)
  between operations  23.3 us (3%)
    pallas_call x1, Pallas kernels, sum_at_owners(): pl.pallas_call(functools.partial(sum_kernel, orders, spans), out_shape=ja...  245 us
    dot_general x11, matrix products, dot_t(): lax.dot_general(left, right, (((left.ndim - 1,), (1,)), ((), ())), prefer...  68.9 us
    pallas_call x4, Pallas kernels, conv_backward(): pl.pallas_call(functools.partial(conv_back_kernel, taps, chunk), grid=(ch...  51.6 us
    pallas_call x2, Pallas kernels, update_packed(): pl.pallas_call(functools.partial(update_packed_kernel, tuple(shapes)), gr...  51.4 us
    dot_general x9, matrix products, dot_n(): lax.dot_general(left, right, (((left.ndim - 1,), (0,)), ((), ())), prefer...  47.1 us
    dot_general x6, matrix products, dot_sum(): lax.dot_general(up, low, (((0,), (0,)), ((), ())), preferred_element_type...  33 us
    pallas_call x3, Pallas kernels, update_factors(): pl.pallas_call(functools.partial(update_factors_kernel, owned, turned, bl...  32.7 us
    pallas_call x5, Pallas kernels, unpack_weights(): pl.pallas_call(functools.partial(unpack_kernel, count, shapes), out_shape...  28.9 us
  transfers between devices with their start and end apart: 29, of which 10 were waited for; matrix products, arithmetic and copies ran while one was open for 23% of the time, Pallas kernels for 55%

profile of v4, /device:TPU:0, one launch (start us, length us, event | category | flops | bytes accessed | tf_op | source)
XLA Modules:
  0.0 828.6 jit_solution(17051629841834723356)
XLA Ops:
  8.0 7.3 all-to-all-start
  46.2 6.4 pack_weights.7.refs_0_
  71.9 8.4 %collective-permute-done.5.refs_1_ = bf16[3,2592,128]{2,1,0:T(8,128)(2,1)} collective-permute-done((bf16[3,2592,128]{2,1,0:T(8,128)(2,1)}, bf16[3,2592,128]{2,1,0:T(8,128)(2,1)}, u32[]{:S(2)}, u32[]{:S(2)}) %collective-permute-start.5) | collective-permute-done | bytes 1990688 | tf_op jit(solution)/shard_map/ppermute | solution.py:230
  90.5 18.1 %all-to-all-done.tiles_ref = bf16[8,16,4,8,512]{4,3,2,1,0:T(8,128)(2,1)} async-done(((bf16[8,16,4,8,512]{4,3,2,1,0:T(8,128)(2,1)}), bf16[8,16,4,8,512]{4,3,2,1,0:T(8,128)(2,1)}, u32[]{:S(2)}, u32[]{:S(2)}) %all-to-all-start) | async-done | bytes 4194336 | tf_op jit(solution)/shard_map/all_to_all | solution.py:904
  109.6 11.4 %prepare.1 = (bf16[4,1024,512]{2,1,0:T(8,128)(2,1)S(1)}, bf16[1024,512]{1,0:T(8,128)(2,1)S(1)}) custom-call(bf16[8,16,4,8,512]{4,3,2,1,0:T(8,128)(2,1)} %all-to-all-done.tiles_ref, bf16[256,256]{1,0:T(8,128)(2,1)S(1)} %copy-done.26), custom_call_target="tpu_custom_call" | custom-call | flops 1073741824 | bytes 10485760 | tf_op jit(solution)/shard_map/prepare/pallas_call | solution.py:467
  121.0 9.4 %fusion.118 = (bf16[4,1024,768]{2,1,0:T(8,128)(2,1)}, bf16[4,1024,768]{2,1,0:T(8,128)(2,1)S(1)}) fusion(bf16[4,1024,512]{2,1,0:T(8,128)(2,1)S(1)} %get-tuple-element.107, bf16[2304,512]{1,0:T(8,128)(2,1)} %copy-done.15), kind=kOutput, calls=%fused_computation.248 | convolution fusion | flops 3252682752 | bytes 17563648 | tf_op jit(solution)/shard_map/dot_general | solution.py:816
  144.1 6.6 unpack_weights.6
  150.8 7.2 conv_forward.4
  158.0 6.4 conv_forward.5
  181.0 9.4 %collective-permute-done.11.refs_2_ = bf16[3,3168,128]{2,1,0:T(8,128)(2,1)} collective-permute-done((bf16[3,3168,128]{2,1,0:T(8,128)(2,1)}, bf16[3,3168,128]{2,1,0:T(8,128)(2,1)}, u32[]{:S(2)}, u32[]{:S(2)}) %collective-permute-start.11) | collective-permute-done | bytes 2433056 | tf_op jit(solution)/shard_map/ppermute | solution.py:233
  197.4 7.4 unpack_weights.7
  204.8 12.9 %convert_bitcast_fusion = (bf16[1,1024,768]{2,1,0:T(8,128)(2,1)}, bf16[1,1024,768]{2,1,0:T(8,128)(2,1)S(1)}) fusion(bf16[768,1536]{1,0:T(8,128)(2,1)S(1)} %get-tuple-element.127, f32[1024,1536]{1,0:T(8,128)} %fusion.36), kind=kOutput, calls=%fused_computation.118 | convolution fusion | flops 2437939200 | bytes 11796480 | tf_op jit(solution)/shard_map/dot_general | solution.py:816
  231.7 14.9 %bitcast_reduce_fusion = (f32[16,1536]{1,0:T(8,128)S(1)}, bf16[1024,1536]{1,0:T(8,128)(2,1)}) fusion(bf16[1024,768]{1,0:T(8,128)(2,1)S(1)} %get-tuple-element.134, bf16[1536,768]{1,0:T(8,128)(2,1)S(1)} %get-tuple-element.135), kind=kOutput, calls=%fused_computation.52 | convolution fusion | flops 2419040256 | bytes 7176192 | tf_op jit(solution)/shard_map/dot_general | solution.py:816
  258.1 7.0 unpack_weights.8
  265.2 16.8 %fusion.16 = (f32[16,3072]{1,0:T(8,128)S(1)}, bf16[1024,3072]{1,0:T(8,128)(2,1)}) fusion(bf16[1024,1536]{1,0:T(8,128)(2,1)S(1)} %fusion.35, bf16[3072,1536]{1,0:T(8,128)(2,1)} %unpack_weights.8), kind=kOutput, calls=%fused_computation.21 | convolution fusion | flops 9695084544 | bytes 19070976 | tf_op jit(solution)/shard_map/dot_general | solution.py:816
  297.7 6.8 fusion.9
  304.5 10.5 %convolution_convert_fusion.refs_0_ = bf16[3072,1536]{1,0:T(8,128)(2,1)S(1)} fusion(bf16[1024,3072]{1,0:T(8,128)(2,1)S(1)} %fusion.9, bf16[1024,1536]{1,0:T(8,128)(2,1)S(1)} %copy-done.66), kind=kOutput, calls=%fused_computation.22 | convolution fusion | flops 9668395008 | bytes 18874368 | tf_op jit(solution)/shard_map/dot_general | solution.py:830
  315.0 9.6 %pack_gradients.2 = bf16[24,2304,128]{2,1,0:T(8,128)(2,1)} custom-call(s32[24]{0:T(128)S(1)} %add.436.part_ref, s32[24]{0:T(128)S(1)} %add.439.slot_ref, bf16[3072,1536]{1,0:T(8,128)(2,1)S(1)} %convolution_convert_fusion.refs_0_), custom_call_target="tpu_custom_call" | custom-call | bytes 28311552 | tf_op jit(solution)/shard_map/pack_gradients/pallas_call | solution.py:270
  326.0 16.9 %multiply_reduce_fusion.1 = (f32[16,1536]{1,0:T(8,128)S(1)}, f32[1024,1536]{1,0:T(8,128)}) fusion(bf16[1024,1536]{1,0:T(8,128)(2,1)} %get-tuple-element.226, bf16[1024,3072]{1,0:T(8,128)(2,1)} %copy-done.60, bf16[3072,1536]{1,0:T(8,128)(2,1)} %unpack_weights.8), kind=kOutput, calls=%fused_computation.58 | convolution fusion | flops 9668370432 | bytes 25264128 | tf_op jit(solution)/shard_map/dot_general | solution.py:822
  355.8 11.6 %conv_backward.4 = (bf16[1,1024,768]{2,1,0:T(8,128)(2,1)S(1)}, bf16[768,1152]{1,0:T(8,128)(2,1)}) custom-call(bf16[1024,768]{1,0:T(8,128)(2,1)S(1)} %fusion.58.up_ref, bf16[1,1024,768]{2,1,0:T(8,128)(2,1)S(1)} %bitcast.178, bf16[1,1024,768]{2,1,0:T(8,128)(2,1)} %bitcast.176, bf16[768,1152]{1,0:T(8,128)(2,1)} %copy-done.37), custom_call_target="tpu_custom_call" | custom-call | flops 3623878656 | bytes 7864320 | tf_op jit(solution)/shard_map/conv_backward/pallas_call | solution.py:619
  367.4 11.6 %conv_backward.5 = (bf16[1,1024,768]{2,1,0:T(8,128)(2,1)S(1)}, bf16[768,1152]{1,0:T(8,128)(2,1)}) custom-call(bf16[1024,768]{1,0:T(8,128)(2,1)S(1)} %bitcast.179, bf16[1,1024,768]{2,1,0:T(8,128)(2,1)S(1)} %copy-done.50, bf16[1,1024,768]{2,1,0:T(8,128)(2,1)} %get-tuple-element.197.pre_ref, bf16[768,1152]{1,0:T(8,128)(2,1)} %copy-done.36), custom_call_target="tpu_custom_call" | custom-call | flops 3623878656 | bytes 7864320 | tf_op jit(solution)/shard_map/conv_backward/pallas_call | solution.py:619
  379.1 11.0 %multiply_reduce_fusion = (f32[16,1536]{1,0:T(8,128)S(1)}, f32[1024,1536]{1,0:T(8,128)}) fusion(bf16[1024,1536]{1,0:T(8,128)(2,1)S(1)} %copy-done.62, f32[1024,1536]{1,0:T(8,128)} %get-tuple-element.236, bf16[768,1536]{1,0:T(8,128)(2,1)S(1)} %copy-done.32, bf16[1,1024,768]{2,1,0:T(8,128)(2,1)S(1)} %get-tuple-element.147, f32[1024,1536]{1,0:T(8,128)} %fusion.36), kind=kOutput, calls=%fused_computation.57 | convolution fusion | flops 2448924672 | bytes 26050560 | tf_op jit(solution)/shard_map/dot_general | solution.py:822
  411.3 11.8 %conv_backward.6 = (bf16[1,1024,768]{2,1,0:T(8,128)(2,1)S(1)}, bf16[768,1152]{1,0:T(8,128)(2,1)}) custom-call(bf16[1024,768]{1,0:T(8,128)(2,1)S(1)} %fusion.49.up_ref, bf16[1,1024,768]{2,1,0:T(8,128)(2,1)S(1)} %bitcast.175, bf16[1,1024,768]{2,1,0:T(8,128)(2,1)} %bitcast.173, bf16[768,1152]{1,0:T(8,128)(2,1)} %copy-done.35), custom_call_target="tpu_custom_call" | custom-call | flops 3623878656 | bytes 7864320 | tf_op jit(solution)/shard_map/conv_backward/pallas_call | solution.py:619
  423.0 16.7 %conv_backward.7 = (bf16[4,1024,768]{2,1,0:T(8,128)(2,1)}, bf16[768,1152]{1,0:T(8,128)(2,1)S(1)}) custom-call(bf16[1024,768]{1,0:T(8,128)(2,1)S(1)} %bitcast.172, bf16[4,1024,768]{2,1,0:T(8,128)(2,1)} %copy-done.6, bf16[4,1024,768]{2,1,0:T(8,128)(2,1)} %get-tuple-element.195.pre_ref, bf16[768,1152]{1,0:T(8,128)(2,1)S(1)} %copy-done.14), custom_call_target="tpu_custom_call" | custom-call | flops 3623878656 | bytes 26738688 | tf_op jit(solution)/shard_map/conv_backward/pallas_call | solution.py:619
  439.7 6.4 fusion.69
  465.1 15.5 %pack_gradients.3 = bf16[24,4096,128]{2,1,0:T(8,128)(2,1)} custom-call(s32[24]{0:T(128)S(1)} %add.436.part_ref, s32[24]{0:T(128)S(1)} %add.439.slot_ref, bf16[2304,512]{1,0:T(8,128)(2,1)S(1)} %pad_maximum_fusion.refs_0_, bf16[768,1536]{1,0:T(8,128)(2,1)S(1)} %convolution_convert_fusion.3.refs_1_, bf16[1536,768]{1,0:T(8,128)(2,1)S(1)} %convolution_convert_fusion.2.refs_2_, ...), custom_call_target="tpu_custom_call" | custom-call | bytes 50331648 | tf_op jit(solution)/shard_map/pack_gradients/pallas_call | solution.py:270
  480.6 244.6 %sum_at_owners.1 = bf16[24,2,2,2,128,128]{5,4,3,2,1,0:T(8,128)(2,1)} custom-call(bf16[2,2,24,2,2,2,128,128]{7,6,5,4,3,2,1,0:T(8,128)(2,1)} %bitcast.180), custom_call_target="tpu_custom_call" | custom-call | flops 12582912 | bytes 50331648 | tf_op jit(solution)/shard_map/sum_at_owners/pallas_call | solution.py:423
  725.2 31.0 %update_packed.2 = (f32[864,512]{1,0:T(8,128)}, f32[864,512]{1,0:T(8,128)}, f32[864,512]{1,0:T(8,128)}, f32[1,288,1536]{2,1,0:T(8,128)}, f32[1,288,1536]{2,1,0:T...) custom-call(s32[1]{0:T(128)} %dynamic_slice.46.share_ref, ...), custom_call_target="tpu_custom_call" | custom-call | flops 92897280 | bytes 83607552 | tf_op jit(solution)/shard_map/update_packed/pallas_call | solution.py:695
  760.6 10.1 %update_factors.3 = (f32[2,288,1536]{2,1,0:T(8,128)}, f32[2,288,1536]{2,1,0:T(8,128)}, f32[2,288,1536]{2,1,0:T(8,128)}) custom-call(s32[1]{0:T(128)} %dynamic_slice.46.share_ref, bf16[2,512,288]{2,1,0:T(8,128)(2,1)} %pad_maximum_fusion.2.units_ref, bf16[512,13672]{1,0:T(8,128)(2,1)} %all-gather.2.cloned.1.call-done.inputs_ref, f32[2,288,1536]{2,1,0:T(8,128)} %w_ref.2, ...), custom_call_target="tpu_custom_call" | custom-call | flops 919240704 | bytes 21233664 | tf_op jit(solution)/shard_map/update_factors/pallas_call | solution.py:743
  773.9 10.1 %update_factors.4 = (f32[2,576,768]{2,1,0:T(8,128)}, f32[2,576,768]{2,1,0:T(8,128)}, f32[2,576,768]{2,1,0:T(8,128)}) custom-call(s32[1]{0:T(128)} %dynamic_slice.46.share_ref, bf16[2,512,576]{2,1,0:T(8,128)(2,1)} %pad_maximum_fusion.1.units_ref, bf16[512,13672]{1,0:T(8,128)(2,1)} %all-gather.2.cloned.1.call-done.inputs_ref, f32[2,576,768]{2,1,0:T(8,128)} %w_ref.3, ...), custom_call_target="tpu_custom_call" | custom-call | flops 919240704 | bytes 21233664 | tf_op jit(solution)/shard_map/update_factors/pallas_call | solution.py:743
  787.1 12.5 %update_factors.5 = (f32[1,1000,1152]{2,1,0:T(8,128)}, f32[1,1000,1152]{2,1,0:T(8,128)}, f32[1,1000,1152]{2,1,0:T(8,128)}) custom-call(s32[1]{0:T(128)} %dynamic_slice.46.share_ref, bf16[1,512,1152]{2,1,0:T(8,128)(2,1)} %dynamic-slice_bitcast_fusion.units_ref, bf16[512,13672]{1,0:T(8,128)(2,1)} %all-gather.2.cloned.1.call-done.inputs_ref, ...), custom_call_target="tpu_custom_call" | custom-call | flops 1196928000 | bytes 27648000 | tf_op jit(solution)/shard_map/update_factors/pallas_call | solution.py:743
  800.3 20.4 %update_packed.3 = (f32[1152,1536]{1,0:T(8,128)}, f32[1152,1536]{1,0:T(8,128)}, f32[1152,1536]{1,0:T(8,128)}) custom-call(s32[1]{0:T(128)} %dynamic_slice.46.share_ref, bf16[6,2304,128]{2,1,0:T(8,128)(2,1)} %all-reduce.3.cloned.1.call-done.packed_ref, f32[1152,1536]{1,0:T(8,128)} %refs_0_.9, f32[1152,1536]{1,0:T(8,128)} %refs_1_.7, f32[1152,1536]{1,0:T(8,128)} %refs_2_.7), custom_call_target="tpu_custom_call" | custom-call | flops 53084160 | bytes 47775744 | tf_op jit(solution)/shard_map/update_packed/pallas_call | solution.py:695
  (333 shorter events, 198.6 us)
Async XLA Ops:
  8.0 100.6 %all-to-all-start = ((bf16[8,16,4,8,512]{4,3,2,1,0:T(8,128)(2,1)}), bf16[8,16,4,8,512]{4,3,2,1,0:T(8,128)(2,1)}, u32[]{:S(2)}, u32[]{:S(2)}) async-start(bf16[8,16,4,8,512]{4,3,2,1,0:T(8,128)(2,1)} %bitcast.188), calls=%async_computation | async-start | bytes 8388608 | tf_op jit(solution)/shard_map/all_to_all | solution.py:904
  15.3 437.3 %reduce-scatter.2.cloned.1.call-start = ((), (), s32[]{:S(2)}) async-start(), calls=%async_computation.3 | async-start | bytes 17694720 | tf_op jit(solution)/shard_map/reduce_scatter | solution.py:1033
  20.9 14.7 %collective-permute-start = (bf16[3,576,128]{2,1,0:T(8,128)(2,1)S(1)}, bf16[3,576,128]{2,1,0:T(8,128)(2,1)}, u32[]{:S(2)}, u32[]{:S(2)}) collective-permute-start(bf16[3,576,128]{2,1,0:T(8,128)(2,1)S(1)} %constant_dynamic-slice_fusion.4), channel_id=1, source_target_pairs={{0,16},{8,24},{16,0},{24,8},{1,17},{9,25},{17,1},{25,9},{2,18},{10... | collective-permute-start | bytes 1327112 | tf_op jit(solution)/shard_map/ppermute | solution.py:230
  35.5 44.8 %collective-permute-start.5 = (bf16[3,2592,128]{2,1,0:T(8,128)(2,1)}, bf16[3,2592,128]{2,1,0:T(8,128)(2,1)}, u32[]{:S(2)}, u32[]{:S(2)}) collective-permute-start(bf16[3,2592,128]{2,1,0:T(8,128)(2,1)} %constant_dynamic-slice_fusion.3), channel_id=1, source_target_pairs={{0,16},{8,24},{16,0},{24,8},{1,17},{9,25},{17,1},{25,9},{2,18},{10... | collective-permute-start | bytes 5971976 | tf_op jit(solution)/shard_map/ppermute | solution.py:230
  36.1 47.3 %collective-permute-start.2 = (bf16[6,576,128]{2,1,0:T(8,128)(2,1)}, bf16[6,576,128]{2,1,0:T(8,128)(2,1)}, u32[]{:S(2)}, u32[]{:S(2)}) collective-permute-start(bf16[6,576,128]{2,1,0:T(8,128)(2,1)} %pack_weights.5.refs_0_), channel_id=1, source_target_pairs={{0,8},{8,0},{16,24},{24,16},{1,9},{9,1},{17,25},{25,17},{2,10},{10... | collective-permute-start | bytes 2654216 | tf_op jit(solution)/shard_map/ppermute | solution.py:237
  36.1 103.6 %collective-permute-start.8 = (bf16[6,2592,128]{2,1,0:T(8,128)(2,1)}, bf16[6,2592,128]{2,1,0:T(8,128)(2,1)}, u32[]{:S(2)}, u32[]{:S(2)}) collective-permute-start(bf16[6,2592,128]{2,1,0:T(8,128)(2,1)} %pack_weights.6.refs_0_), channel_id=1, source_target_pairs={{0,8},{8,0},{16,24},{24,16},{1,9},{9,1},{17,25},{25,17},{2,10},{10... | collective-permute-start | bytes 11943944 | tf_op jit(solution)/shard_map/ppermute | solution.py:237
  38.8 33.1 %collective-permute-start.1 = (bf16[3,576,128]{2,1,0:T(8,128)(2,1)}, bf16[3,576,128]{2,1,0:T(8,128)(2,1)}, u32[]{:S(2)}, u32[]{:S(2)}) collective-permute-start(bf16[3,576,128]{2,1,0:T(8,128)(2,1)} %collective-permute-done.refs_1_), channel_id=1, source_target_pairs={{0,1},{1,0},{2,3},{3,2},{4,5},{5,4},{6,7},{7,6},{8,9},{9,8},{10,11... | collective-permute-start | bytes 1327112 | tf_op jit(solution)/shard_map/ppermute | solution.py:233
  80.4 53.8 %collective-permute-start.7 = (bf16[3,3168,128]{2,1,0:T(8,128)(2,1)}, bf16[3,3168,128]{2,1,0:T(8,128)(2,1)}, u32[]{:S(2)}, u32[]{:S(2)}) collective-permute-start(bf16[3,3168,128]{2,1,0:T(8,128)(2,1)} %constant_dynamic-slice_fusion.2), channel_id=1, source_target_pairs={{0,16},{8,24},{16,0},{24,8},{1,17},{9,25},{17,1},{25,9},{2,18},{10... | collective-permute-start | bytes 7299080 | tf_op jit(solution)/shard_map/ppermute | solution.py:230
  81.6 52.6 %collective-permute-start.6 = (bf16[3,2592,128]{2,1,0:T(8,128)(2,1)}, bf16[3,2592,128]{2,1,0:T(8,128)(2,1)}, u32[]{:S(2)}, u32[]{:S(2)}) collective-permute-start(bf16[3,2592,128]{2,1,0:T(8,128)(2,1)} %collective-permute-done.5.refs_1_), channel_id=1, source_target_pairs={{0,1},{1,0},{2,3},{3,2},{4,5},{5,4},{6,7},{7,6},{8,9},{9,8},{10,11... | collective-permute-start | bytes 5971976 | tf_op jit(solution)/shard_map/ppermute | solution.py:233
  83.3 2.1 collective-permute-start.3
  83.4 2.6 collective-permute-start.4
  90.5 49.2 %collective-permute-start.9 = (bf16[3,2592,128]{2,1,0:T(8,128)(2,1)}, bf16[3,2592,128]{2,1,0:T(8,128)(2,1)}, u32[]{:S(2)}, u32[]{:S(2)}) collective-permute-start(bf16[3,2592,128]{2,1,0:T(8,128)(2,1)} %collective-permute-done.5.refs_1_), channel_id=1, source_target_pairs={{0,8},{8,0},{16,24},{24,16},{1,9},{9,1},{17,25},{25,17},{2,10},{10... | collective-permute-start | bytes 5971976 | tf_op jit(solution)/shard_map/ppermute | solution.py:237
  121.0 49.5 %copy-start.24 = (bf16[1024,512]{1,0:T(8,128)(2,1)}, bf16[1024,512]{1,0:T(8,128)(2,1)S(1)}, u32[]{:S(2)}) copy-start(bf16[1024,512]{1,0:T(8,128)(2,1)S(1)} %get-tuple-element.106) | copy-start | bytes 3145732
  134.2 7.1 collective-permute-start.10
  134.2 61.6 %collective-permute-start.13 = (bf16[6,3168,128]{2,1,0:T(8,128)(2,1)}, bf16[6,3168,128]{2,1,0:T(8,128)(2,1)}, u32[]{:S(2)}, u32[]{:S(2)}) collective-permute-start(bf16[6,3168,128]{2,1,0:T(8,128)(2,1)} %pack_weights.7.refs_0_), channel_id=1, source_target_pairs={{0,8},{8,0},{16,24},{24,16},{1,9},{9,1},{17,25},{25,17},{2,10},{10... | collective-permute-start | bytes 14598152 | tf_op jit(solution)/shard_map/ppermute | solution.py:237
  134.7 55.8 %collective-permute-start.11 = (bf16[3,3168,128]{2,1,0:T(8,128)(2,1)}, bf16[3,3168,128]{2,1,0:T(8,128)(2,1)}, u32[]{:S(2)}, u32[]{:S(2)}) collective-permute-start(bf16[3,3168,128]{2,1,0:T(8,128)(2,1)} %collective-permute-done.7.refs_1_), channel_id=1, source_target_pairs={{0,1},{1,0},{2,3},{3,2},{4,5},{5,4},{6,7},{7,6},{8,9},{9,8},{10,11... | collective-permute-start | bytes 7299080 | tf_op jit(solution)/shard_map/ppermute | solution.py:233
  139.7 56.1 %collective-permute-start.14 = (bf16[3,3168,128]{2,1,0:T(8,128)(2,1)}, bf16[3,3168,128]{2,1,0:T(8,128)(2,1)}, u32[]{:S(2)}, u32[]{:S(2)}) collective-permute-start(bf16[3,3168,128]{2,1,0:T(8,128)(2,1)} %collective-permute-done.7.refs_1_), channel_id=1, source_target_pairs={{0,8},{8,0},{16,24},{24,16},{1,9},{9,1},{17,25},{25,17},{2,10},{10... | collective-permute-start | bytes 7299080 | tf_op jit(solution)/shard_map/ppermute | solution.py:237
  139.7 41.3 %collective-permute-start.12 = (bf16[3,2304,128]{2,1,0:T(8,128)(2,1)}, bf16[3,2304,128]{2,1,0:T(8,128)(2,1)}, u32[]{:S(2)}, u32[]{:S(2)}) collective-permute-start(bf16[3,2304,128]{2,1,0:T(8,128)(2,1)} %constant_dynamic-slice_fusion.1), channel_id=1, source_target_pairs={{0,16},{8,24},{16,0},{24,8},{1,17},{9,25},{17,1},{25,9},{2,18},{10... | collective-permute-start | bytes 5308424 | tf_op jit(solution)/shard_map/ppermute | solution.py:230
  190.5 6.9 collective-permute-start.15
  191.1 63.3 %collective-permute-start.18 = (bf16[6,2304,128]{2,1,0:T(8,128)(2,1)S(1)}, bf16[6,2304,128]{2,1,0:T(8,128)(2,1)S(1)}, u32[]{:S(2)}, u32[]{:S(2)}) collective-permute-start(bf16[6,2304,128]{2,1,0:T(8,128)(2,1)S(1)} %pack_weights.8.refs_0_), channel_id=1, source_target_pairs={{0,8},{8,0},{16,24},{24,16},{1,9},{9,1},{17,25},{25,17},{2,10},{10... | collective-permute-start | bytes 10616840 | tf_op jit(solution)/shard_map/ppermute | solution.py:237
  194.0 59.5 %collective-permute-start.17 = (bf16[3,2304,128]{2,1,0:T(8,128)(2,1)}, bf16[3,2304,128]{2,1,0:T(8,128)(2,1)S(1)}, u32[]{:S(2)}, u32[]{:S(2)}) collective-permute-start(bf16[3,2304,128]{2,1,0:T(8,128)(2,1)} %collective-permute-done.12.refs_1_), channel_id=1, source_target_pairs={{0,1},{1,0},{2,3},{3,2},{4,5},{5,4},{6,7},{7,6},{8,9},{9,8},{10,11... | collective-permute-start | bytes 5308424 | tf_op jit(solution)/shard_map/ppermute | solution.py:233
  195.8 58.7 %collective-permute-start.19 = (bf16[3,2304,128]{2,1,0:T(8,128)(2,1)}, bf16[3,2304,128]{2,1,0:T(8,128)(2,1)S(1)}, u32[]{:S(2)}, u32[]{:S(2)}) collective-permute-start(bf16[3,2304,128]{2,1,0:T(8,128)(2,1)} %collective-permute-done.12.refs_1_), channel_id=1, source_target_pairs={{0,8},{8,0},{16,24},{24,16},{1,9},{9,1},{17,25},{25,17},{2,10},{10... | collective-permute-start | bytes 5308424 | tf_op jit(solution)/shard_map/ppermute | solution.py:237
  195.8 35.9 %collective-permute-start.16 = (bf16[3,1536,128]{2,1,0:T(8,128)(2,1)}, bf16[3,1536,128]{2,1,0:T(8,128)(2,1)}, u32[]{:S(2)}, u32[]{:S(2)}) collective-permute-start(bf16[3,1536,128]{2,1,0:T(8,128)(2,1)} %constant_dynamic-slice_fusion), channel_id=1, source_target_pairs={{0,16},{8,24},{16,0},{24,8},{1,17},{9,25},{17,1},{25,9},{2,18},{10... | collective-permute-start | bytes 3538952 | tf_op jit(solution)/shard_map/ppermute | solution.py:230
  204.8 41.9 %copy-start.8 = (bf16[768,1536]{1,0:T(8,128)(2,1)}, bf16[768,1536]{1,0:T(8,128)(2,1)S(1)}, u32[]{:S(2)}) copy-start(bf16[768,1536]{1,0:T(8,128)(2,1)S(1)} %get-tuple-element.136) | copy-start | bytes 7077892
  204.8 43.2 %copy-start.10 = (bf16[1536,768]{1,0:T(8,128)(2,1)}, bf16[1536,768]{1,0:T(8,128)(2,1)S(1)}, u32[]{:S(2)}) copy-start(bf16[1536,768]{1,0:T(8,128)(2,1)S(1)} %get-tuple-element.137) | copy-start | bytes 7077892
  253.6 4.6 collective-permute-start.20
  253.8 29.4 %collective-permute-start.22 = (bf16[6,1536,128]{2,1,0:T(8,128)(2,1)}, bf16[6,1536,128]{2,1,0:T(8,128)(2,1)}, u32[]{:S(2)}, u32[]{:S(2)}) collective-permute-start(bf16[6,1536,128]{2,1,0:T(8,128)(2,1)} %pack_weights.9.refs_0_), channel_id=1, source_target_pairs={{0,8},{8,0},{16,24},{24,16},{1,9},{9,1},{17,25},{25,17},{2,10},{10... | collective-permute-start | bytes 7077896 | tf_op jit(solution)/shard_map/ppermute | solution.py:237
  254.1 28.4 %collective-permute-start.21 = (bf16[3,1536,128]{2,1,0:T(8,128)(2,1)}, bf16[3,1536,128]{2,1,0:T(8,128)(2,1)}, u32[]{:S(2)}, u32[]{:S(2)}) collective-permute-start(bf16[3,1536,128]{2,1,0:T(8,128)(2,1)} %collective-permute-done.16.refs_1_), channel_id=1, source_target_pairs={{0,1},{1,0},{2,3},{3,2},{4,5},{5,4},{6,7},{7,6},{8,9},{9,8},{10,11... | collective-permute-start | bytes 3538952 | tf_op jit(solution)/shard_map/ppermute | solution.py:233
  254.4 28.8 %collective-permute-start.23 = (bf16[3,1536,128]{2,1,0:T(8,128)(2,1)}, bf16[3,1536,128]{2,1,0:T(8,128)(2,1)}, u32[]{:S(2)}, u32[]{:S(2)}) collective-permute-start(bf16[3,1536,128]{2,1,0:T(8,128)(2,1)} %collective-permute-done.16.refs_1_), channel_id=1, source_target_pairs={{0,8},{8,0},{16,24},{24,16},{1,9},{9,1},{17,25},{25,17},{2,10},{10... | collective-permute-start | bytes 3538952 | tf_op jit(solution)/shard_map/ppermute | solution.py:237
  282.5 3.1 collective-permute-start.24
  324.7 431.5 %all-gather.2.cloned.1.call-start = ((), (), s32[]{:S(2)}) async-start(), calls=%async_computation.2 | async-start | bytes 14462976 | tf_op jit(solution)/shard_map/all_gather | solution.py:1056
  402.0 398.4 %all-reduce.3.cloned.1.call-start = ((), (), s32[]{:S(2)}) async-start(), calls=%async_computation.4 | async-start | bytes 7077888 | tf_op jit(solution)/shard_map/psum | solution.py:1036
  (94 other events, 800.7 us)
Sparse Core Ops, SparseCore 0:
  324.8 114.1 reduce-scatter.1
  452.8 247.7 all-reduce.2
Sparse Core Ops, SparseCore 1:
  402.0 188.9 all-gather.1
